TPU v7x, 128 devices: a whole 4x4x4 slice. The times are simulated.
128 devices in a mesh: wide: 8 (over z, core), narrow: 16 (over x, y).
Axes of the slice: x: 4, y: 4, z: 4, core: 2. Of those that a mesh axis runs over, the one named last changes fastest.
Arguments:
- hidden_states: float32 [4096, 4096], P('wide', 'narrow'), may hold values from -300 to 300
- out_cotangent: float32 [4096, 4096], P('wide', 'narrow'), may hold values from -6 to 6
- enc_table: float32 [128, 128, 896], P('wide', 'narrow'), may hold values from -6 to 6
- nbr_ids: int32 [64, 2], replicated, may hold values from 0 to 127, as said below
- owner_map: int32 [128], replicated, may hold values from 0 to 127, as said below
- w_query: float32 [4096, 4096], P(None, 'narrow'), may hold values from -0.09375 to 0.09375
- w_key: float32 [896, 4096], P(None, 'narrow'), may hold values from -0.1875 to 0.1875
- w_value: float32 [896, 4096], P(None, 'narrow'), may hold values from -0.1875 to 0.1875
- w_out: float32 [4096, 4096], P(None, 'narrow'), may hold values from -0.09375 to 0.09375
Outputs:
- grad_hidden: float32 [4096, 4096], P('wide', 'narrow')
- grad_query: float32 [4096, 4096], P('wide', 'narrow')
- grad_key: float32 [896, 4096], P('wide', 'narrow')
- grad_value: float32 [896, 4096], P('wide', 'narrow')
- grad_out: float32 [4096, 4096], P('wide', 'narrow')
- grad_table: float32 [128, 128, 896], P('wide', 'narrow')
Inputs may be any that keep to these rules, and one draw needn't show every extreme that they name: A permutation: neighbour id n is stored in slot owner_map[n] of enc_table; slots o * 16 to (o + 1) * 16 - 1 belong to owner o. `nbr_ids`: of the 16 neighbour ids of the spans of one index of wide, at most 2 are stored with one owner, and exactly 2 with some owner. Ids may repeat.
All inputs are finite; a program needn't handle non-finite values.
Results may differ from a plain program's by a relative error of at most 0.0011.
Values sent between devices are 32-bit elements; how exact they have to be, the bound alone decides.
A program may use at most 192 MiB of HBM per device.

v0:
```python
import jax
import jax.numpy as jnp
from jax import lax
from jax.sharding import PartitionSpec as P

HEAD_DIM = 128
SPAN = 64
NEIGH = 2
CH_DEV = 8


HIGH = lax.Precision.HIGHEST


def body(
    hidden_states, out_cotangent, enc_table, nbr_ids, owner_map, w_query, w_key, w_value, w_out
):
    groups = lax.axis_size("wide")
    narrow_count = lax.axis_size("narrow")
    group = lax.axis_index("wide")
    gathered, cotangent = (
        lax.all_gather(hidden_states, "narrow", axis=1, tiled=True),
        lax.all_gather(out_cotangent, "narrow", axis=1, tiled=True),
    )
    stored = enc_table.shape[0]
    piece_rows = enc_table.shape[1]
    enc_width = enc_table.shape[2]
    table_size = owner_map.shape[0]
    inst = NEIGH * CH_DEV
    capacity = max(2, (inst + groups - 1) // groups)
    local_width = w_query.shape[1]
    heads_local = local_width // HEAD_DIM
    scale = HEAD_DIM ** (-0.5)
    match = nbr_ids[:, :, None] == jnp.arange(table_size, dtype=jnp.int32)[None, None, :]
    slots = jnp.sum(jnp.where(match, owner_map[None, None, :], 0), axis=-1)
    slots = slots.reshape(groups, inst)
    owners = slots // stored
    local_slot = slots - owners * stored
    earlier = jnp.arange(inst)[None, :] < jnp.arange(inst)[:, None]
    same = owners[:, :, None] == owners[:, None, :]
    rank = jnp.sum((same & earlier[None, :, :]).astype(jnp.int32), axis=-1)
    slot_range = jnp.arange(capacity, dtype=jnp.int32)
    pick = ((owners[:, None, :] == group) & (rank[:, None, :] == slot_range[None, :, None])).astype(
        jnp.float32
    )
    one_local = (
        local_slot[:, :, None] == jnp.arange(stored, dtype=jnp.int32)[None, None, :]
    ).astype(jnp.float32)
    place = jnp.einsum("bri,bis->brs", pick, one_local, precision=HIGH)
    mine_owner = lax.dynamic_index_in_dim(owners, group, 0, keepdims=False)
    mine_rank = lax.dynamic_index_in_dim(rank, group, 0, keepdims=False)
    take = (
        (mine_owner[:, None, None] == jnp.arange(groups, dtype=jnp.int32)[None, :, None])
        & (mine_rank[:, None, None] == slot_range[None, None, :])
    ).astype(jnp.float32)
    outgoing = jnp.einsum("brs,sxe->brxe", place, enc_table, precision=HIGH)
    spread = jnp.broadcast_to(outgoing[:, None], (groups, narrow_count) + outgoing.shape[1:])
    spread = spread.reshape((groups * narrow_count,) + outgoing.shape[1:])
    incoming = lax.all_to_all(spread, ("wide", "narrow"), split_axis=0, concat_axis=0, tiled=True)
    incoming = incoming.reshape(groups, narrow_count, capacity, piece_rows, enc_width)
    neighbours = jnp.einsum("iwr,wnrxe->inxe", take, incoming, precision=HIGH)
    neighbours = neighbours.reshape(inst, narrow_count * piece_rows, enc_width)
    full_rows = neighbours.shape[1]
    flat_neigh = neighbours.reshape(inst * full_rows, enc_width)
    spans_local = gathered.shape[0] // SPAN
    query = jnp.dot(gathered, w_query, precision=HIGH)
    keys = jnp.dot(flat_neigh, w_key, precision=HIGH)
    values = jnp.dot(flat_neigh, w_value, precision=HIGH)
    query_h = query.reshape(spans_local, SPAN, heads_local, HEAD_DIM)
    keys_h = keys.reshape(spans_local, NEIGH * full_rows, heads_local, HEAD_DIM)
    values_h = values.reshape(spans_local, NEIGH * full_rows, heads_local, HEAD_DIM)
    scores = jnp.einsum("cmhd,cnhd->chmn", query_h, keys_h, precision=HIGH) * scale
    probs = jax.nn.softmax(scores, axis=-1)
    attended = jnp.einsum("chmn,cnhd->cmhd", probs, values_h, precision=HIGH).reshape(
        gathered.shape[0], local_width
    )
    d_attended = jnp.dot(cotangent, w_out, precision=HIGH)
    d_att_h = d_attended.reshape(spans_local, SPAN, heads_local, HEAD_DIM)
    d_probs = jnp.einsum("cmhd,cnhd->chmn", d_att_h, values_h, precision=HIGH)
    d_scores = probs * (d_probs - jnp.sum(d_probs * probs, axis=-1, keepdims=True)) * scale
    d_query = jnp.einsum("chmn,cnhd->cmhd", d_scores, keys_h, precision=HIGH).reshape(
        gathered.shape[0], local_width
    )
    d_keys = jnp.einsum("chmn,cmhd->cnhd", d_scores, query_h, precision=HIGH).reshape(
        inst * full_rows, local_width
    )
    d_values = jnp.einsum("chmn,cmhd->cnhd", probs, d_att_h, precision=HIGH).reshape(
        inst * full_rows, local_width
    )
    input_term = lax.dot_general(d_query, w_query, (((1,), (1,)), ((), ())), precision=HIGH)
    grad_hidden = lax.psum_scatter(input_term, "narrow", scatter_dimension=1, tiled=True)
    first = lax.dot_general(gathered, d_query, (((0,), (0,)), ((), ())), precision=HIGH)
    second = lax.dot_general(cotangent, attended, (((0,), (0,)), ((), ())), precision=HIGH)
    projections = lax.psum_scatter(
        jnp.concatenate([first, second], axis=1), "wide", scatter_dimension=0, tiled=True
    )
    grad_query = projections[:, :local_width]
    grad_out = projections[:, local_width:]
    joined = jnp.concatenate([d_keys, d_values], axis=1)
    pair_grads = lax.psum_scatter(
        lax.dot_general(flat_neigh, joined, (((0,), (0,)), ((), ())), precision=HIGH),
        "wide",
        scatter_dimension=0,
        tiled=True,
    )
    grad_key = pair_grads[:, :local_width]
    grad_value = pair_grads[:, local_width:]
    d_neigh = lax.dot_general(d_keys, w_key, (((1,), (1,)), ((), ())), precision=HIGH)
    d_neigh = d_neigh + lax.dot_general(d_values, w_value, (((1,), (1,)), ((), ())), precision=HIGH)
    d_neigh = d_neigh.reshape(inst, full_rows, enc_width)
    split_rows = d_neigh.reshape(inst, narrow_count, piece_rows, enc_width)
    backward = jnp.einsum("iwr,inxe->wnrxe", take, split_rows, precision=HIGH)
    backward = backward.reshape(groups * narrow_count, capacity, piece_rows, enc_width)
    arrived = lax.all_to_all(backward, ("wide", "narrow"), split_axis=0, concat_axis=0, tiled=True)
    arrived = jnp.sum(
        arrived.reshape(groups, narrow_count, capacity, piece_rows, enc_width), axis=1
    )
    grad_table = jnp.einsum("brs,brxe->sxe", place, arrived, precision=HIGH)
    return (grad_hidden, grad_query, grad_key, grad_value, grad_out, grad_table)


def solution(mesh):
    placed = (
        P("wide", "narrow"),
        P("wide", "narrow"),
        P("wide", "narrow", None),
        P(),
        P(),
        P(None, "narrow"),
        P(None, "narrow"),
        P(None, "narrow"),
        P(None, "narrow"),
    )
    return jax.shard_map(
        body,
        mesh=mesh,
        in_specs=placed,
        out_specs=(
            P("wide", "narrow"),
            P("wide", "narrow"),
            P("wide", "narrow"),
            P("wide", "narrow"),
            P("wide", "narrow"),
            P("wide", "narrow", None),
        ),
        check_vma=False,
    )
```

profile of v0, /device:TPU:1, one launch (start us, length us, event | category | flops | bytes accessed | tf_op | source)
XLA Modules:
  0.0 537.1 jit_solution(853608806903815634)
XLA Ops:
  7.2 0.7 all-gather.5.cloned.1.call-update
  7.9 0.7 all-gather.3.cloned.1.call-update
  8.7 0.9 select_reduce_fusion
  10.2 1.6 fusion.28
  11.9 3.6 broadcast_in_dim.16
  15.5 11.9 %all-to-all-start = ((f32[128,2,8,896]{3,2,1,0:T(8,128)}), f32[128,2,8,896]{3,2,1,0:T(8,128)}, u32[]{:S(2)}, u32[]{:S(2)}) async-start(f32[128,2,8,896]{3,2,1,0:T(8,128)} %bitcast.110), calls=%async_computation | async-start | bytes 14680064 | tf_op jit(solution)/shard_map/all_to_all | solution.py:59
  28.1 92.5 %all-to-all-done = f32[128,2,8,896]{3,2,1,0:T(8,128)} async-done(((f32[128,2,8,896]{3,2,1,0:T(8,128)}), f32[128,2,8,896]{3,2,1,0:T(8,128)}, u32[]{:S(2)}, u32[]{:S(2)}) %all-to-all-start) | async-done | bytes 7340064 | tf_op jit(solution)/shard_map/all_to_all | solution.py:59
  120.7 11.0 %fusion.8 = f32[16,16,8,896]{3,0,2,1:T(8,128)S(1)} fusion(f32[8,16,2,8,896]{4,3,2,1,0:T(8,128)} %bitcast.7, pred[16,2]{0,1:T(4,128)(4,1)S(1)} %iota_compare_fusion.5, pred[16,8]{0,1:T(8,128)(4,1)S(1)} %iota_compare_fusion.4), kind=kOutput, calls=%fused_computation.13 | convolution fusion | flops 352321792 | bytes 14680224 | tf_op jit(solution)/shard_map/iwr,wnrxe->inxe/dot_general | solution.py:61
  131.7 2.4 copy.82
  134.0 8.4 %fusion.63 = f32[8,256,2,128]{3,1,2,0:T(8,128)} fusion(f32[8,256,896,1]{2,1,3,0:T(8,128)S(1)} %bitcast.102, f32[2,128,896,1]{2,1,0,3:T(8,128)S(1)} %bitcast.121), kind=kOutput, calls=%fused_computation.86 | convolution fusion | flops 5637144576 | bytes 10354688 | tf_op jit(solution)/shard_map/dot_general | solution.py:68
  142.4 7.3 %fusion.60 = f32[8,256,2,128]{3,1,2,0:T(8,128)S(1)} fusion(f32[8,256,896,1]{2,1,3,0:T(8,128)S(1)} %bitcast.103, f32[2,128,896,1]{2,1,0,3:T(8,128)S(1)} %bitcast.120), kind=kOutput, calls=%fused_computation.83 | convolution fusion | flops 5637144576 | bytes 10354688 | tf_op jit(solution)/shard_map/dot_general | solution.py:67
  149.8 8.6 %all-gather.5.cloned.1.call-done = f32[512,4096]{1,0:T(8,128)} async-done(((f32[512,256]{1,0:T(8,128)}), f32[512,4096]{1,0:T(8,128)}) %all-gather.5.cloned.1.call-update) | async-done | bytes 8388624 | tf_op jit(solution)/shard_map/all_gather | solution.py:23
  158.4 9.8 %fusion.62 = f32[512,256]{1,0:T(8,128)S(1)} fusion(f32[512,4096]{1,0:T(8,128)} %all-gather.5.cloned.1.call-done, f32[4096,256]{1,0:T(8,128)} %param.17), kind=kOutput, calls=%fused_computation.85 | convolution fusion | flops 6442450944 | bytes 13107200 | tf_op jit(solution)/shard_map/dot_general | solution.py:77
  168.1 1.1 reshape.211
  169.2 68.2 %all-gather.3.cloned.1.call-done = f32[512,4096]{1,0:T(8,128)} async-done(((f32[512,256]{1,0:T(8,128)}), f32[512,4096]{1,0:T(8,128)}) %all-gather.3.cloned.1.call-update) | async-done | bytes 8388624 | tf_op jit(solution)/shard_map/all_gather | solution.py:22
  237.4 10.2 %fusion.61 = f32[512,256]{1,0:T(8,128)S(1)} fusion(f32[512,4096]{1,0:T(8,128)} %all-gather.3.cloned.1.call-done, f32[4096,256]{1,0:T(8,128)} %param.14), kind=kOutput, calls=%fused_computation.84 | convolution fusion | flops 6442450944 | bytes 13107200 | tf_op jit(solution)/shard_map/dot_general | solution.py:66
  247.6 1.1 reshape.210
  248.7 3.6 fusion.59
  252.8 2.2 convolution_bitcast_fusion.2
  255.0 2.5 multiply_reduce_fusion
  257.6 2.5 convolution_bitcast_fusion.3
  260.1 1.2 copy.91
  261.3 0.9 copy.115
  262.2 1.4 copy.93
  263.6 0.9 copy.116
  264.5 1.4 copy-done.2
  265.9 25.1 %fusion.4 = f32[896,512]{1,0:T(8,128)} fusion(f32[2048,896]{1,0:T(8,128)S(1)} %bitcast.106, f32[2048,256]{0,1:T(8,128)S(1)} %bitcast.114, f32[2048,256]{0,1:T(8,128)S(1)} %bitcast.112), kind=kOutput, calls=%fused_computation.8 | convolution fusion | flops 11275337728 | bytes 13369344 | tf_op jit(solution)/shard_map/dot_general | solution.py:101
  291.2 3.9 convolution_bitcast_fusion.5
  295.5 3.2 convolution_bitcast_fusion.4
  299.1 10.1 %convolution_bitcast_fusion.1 = f32[4096,256]{0,1:T(8,128)S(1)} fusion(f32[512,4096]{1,0:T(8,128)} %all-gather.3.cloned.1.call-done, f32[64,8,2,128]{3,2,1,0:T(2,128)S(1)} %bitcast.118), kind=kOutput, calls=%fused_computation.7 | convolution fusion | flops 6442450944 | bytes 13107200 | tf_op jit(solution)/shard_map/dot_general | solution.py:92
  309.2 7.6 %convolution_bitcast_fusion = f32[4096,256]{0,1:T(8,128)S(1)} fusion(f32[512,4096]{1,0:T(8,128)S(1)} %bitcast.108, f32[64,8,2,128]{3,2,1,0:T(2,128)S(1)} %bitcast.124), kind=kOutput, calls=%fused_computation.6 | convolution fusion | flops 6442450944 | bytes 13107200 | tf_op jit(solution)/shard_map/dot_general | solution.py:93
  316.8 3.8 pad_maximum_fusion
  320.6 11.2 %fusion.19 = f32[512,4096]{1,0:T(8,128)} fusion(f32[4096,256]{1,0:T(8,128)} %param.14, f32[64,8,2,128]{3,2,1,0:T(2,128)S(1)} %bitcast.119), kind=kOutput, calls=%fused_computation.29 | convolution fusion | flops 6442450944 | bytes 13107200 | tf_op jit(solution)/shard_map/dot_general | solution.py:90
  331.8 1.2 copy-done.6
  333.0 14.0 %fusion.64 = f32[2048,896]{1,0:T(8,128)S(1)} fusion(f32[2048,256]{0,1:T(8,128)S(1)} %bitcast.113, f32[896,256]{1,0:T(8,128)S(1)} %copy-done.6), kind=kOutput, calls=%fused_computation.87 | convolution fusion | flops 5637144576 | bytes 10354688 | tf_op jit(solution)/shard_map/dot_general | solution.py:108
  347.0 13.7 %convolution_add_fusion = f32[2048,896]{1,0:T(8,128)S(1)} fusion(f32[2048,896]{1,0:T(8,128)S(1)} %fusion.64, f32[2048,256]{0,1:T(8,128)S(1)} %bitcast.115, f32[896,256]{1,0:T(8,128)S(1)} %copy-done.8), kind=kOutput, calls=%fused_computation.12 | convolution fusion | flops 5638979584 | bytes 17694720 | tf_op jit(solution)/shard_map/dot_general | solution.py:109
  360.7 7.7 %fusion.11 = f32[8,16,2,8,896]{4,0,2,3,1:T(8,128)S(1)} fusion(f32[16,16,8,896,1]{3,2,1,0,4:T(8,128)S(1)} %bitcast.111, pred[16,2]{0,1:T(4,128)(4,1)S(1)} %iota_compare_fusion.5, pred[16,8]{0,1:T(8,128)(4,1)S(1)} %iota_compare_fusion.4), kind=kOutput, calls=%fused_computation.14 | convolution fusion | flops 352321792 | bytes 14680224 | tf_op jit(solution)/shard_map/iwr,inxe->wnrxe/dot_general | solution.py:112
  368.4 5.5 %copy.95 = f32[8,16,2,8,896]{4,3,2,1,0:T(8,128)} copy(f32[8,16,2,8,896]{4,0,2,3,1:T(8,128)S(1)} %fusion.11) | data formatting | bytes 14680064 | tf_op jit(solution)/shard_map/iwr,inxe->wnrxe/transpose | solution.py:112
  373.9 8.9 %all-to-all-start.1 = ((f32[128,2,8,896]{3,2,1,0:T(8,128)}), f32[128,2,8,896]{3,2,1,0:T(8,128)}, u32[]{:S(2)}, u32[]{:S(2)}) async-start(f32[128,2,8,896]{3,2,1,0:T(8,128)} %bitcast.109), calls=%async_computation.4 | async-start | bytes 14680064 | tf_op jit(solution)/shard_map/all_to_all | solution.py:114
  382.8 1.7 fusion.58
  384.5 102.1 %all-to-all-done.1 = f32[128,2,8,896]{3,2,1,0:T(8,128)} async-done(((f32[128,2,8,896]{3,2,1,0:T(8,128)}), f32[128,2,8,896]{3,2,1,0:T(8,128)}, u32[]{:S(2)}, u32[]{:S(2)}) %all-to-all-start.1) | async-done | bytes 7340064 | tf_op jit(solution)/shard_map/all_to_all | solution.py:114
  486.6 3.7 bitcast_reduce_fusion
  490.2 0.6 convolution_bitcast_fusion.6
  490.9 0.9 copy.100
  491.8 1.3 fusion.57
  493.1 1.0 copy.99
  494.1 1.0 copy.98
  495.1 35.2 %reduce-scatter.4.cloned.1.call-done = f32[512,256]{1,0:T(8,128)} async-done(((f32[512,4096]{1,0:T(8,128)}), f32[512,256]{1,0:T(8,128)}) %reduce-scatter.4.cloned.1.call-update) | async-done | bytes 524304 | tf_op jit(solution)/shard_map/reduce_scatter | solution.py:91
  (62 shorter events, 3.0 us)
Async XLA Ops:
  7.2 151.2 %all-gather.5.cloned.1.call-start = ((), (), s32[]{:S(2)}) async-start(), calls=%async_computation.6 | async-start | bytes 8912896 | tf_op jit(solution)/shard_map/all_gather | solution.py:23
  7.9 229.5 %all-gather.3.cloned.1.call-start = ((), (), s32[]{:S(2)}) async-start(), calls=%async_computation.5 | async-start | bytes 8912896 | tf_op jit(solution)/shard_map/all_gather | solution.py:22
  15.5 12.0 %copy-start.7 = (f32[896,256]{1,0:T(8,128)S(1)}, f32[896,256]{1,0:T(8,128)}, u32[]{:S(2)}) copy-start(f32[896,256]{1,0:T(8,128)} %param.16) | copy-start | bytes 2752516
  15.5 12.3 %copy-start.5 = (f32[896,256]{1,0:T(8,128)S(1)}, f32[896,256]{1,0:T(8,128)}, u32[]{:S(2)}) copy-start(f32[896,256]{1,0:T(8,128)} %param.15) | copy-start | bytes 2752516
  15.5 105.2 %all-to-all-start = ((f32[128,2,8,896]{3,2,1,0:T(8,128)}), f32[128,2,8,896]{3,2,1,0:T(8,128)}, u32[]{:S(2)}, u32[]{:S(2)}) async-start(f32[128,2,8,896]{3,2,1,0:T(8,128)} %bitcast.110), calls=%async_computation | async-start | bytes 14680064 | tf_op jit(solution)/shard_map/all_to_all | solution.py:59
  27.4 355.4 %reduce-scatter.8.cloned.1.call-start = ((), (), s32[]{:S(2)}) async-start(), calls=%async_computation.9 | async-start | bytes 2064384 | tf_op jit(solution)/shard_map/reduce_scatter | solution.py:100
  134.0 8.4 %copy-start = (f32[16,16,8,896]{3,2,1,0:T(8,128)}, f32[16,16,8,896]{3,2,1,0:T(8,128)S(1)}, u32[]{:S(2)}) copy-start(f32[16,16,8,896]{3,2,1,0:T(8,128)S(1)} %copy.82) | copy-start | bytes 22020100
  149.7 98.9 %copy-start.1 = (f32[8,256,2,128]{3,1,2,0:T(8,128)}, f32[8,256,2,128]{3,1,2,0:T(8,128)S(1)}, u32[]{:S(2)}) copy-start(f32[8,256,2,128]{3,1,2,0:T(8,128)S(1)} %fusion.60) | copy-start | bytes 6291460
  248.7 4.1 copy-start.12
  248.7 6.3 %copy-start.9 = (f32[8,256,2,128]{3,1,2,0:T(8,128)S(1)}, f32[8,256,2,128]{3,1,2,0:T(8,128)}, u32[]{:S(2)}) copy-start(f32[8,256,2,128]{3,1,2,0:T(8,128)} %fusion.63) | copy-start | bytes 6291460
  252.3 38.8 %copy-start.4 = (f32[8,2,64,256]{3,2,1,0:T(8,128)}, f32[8,2,64,256]{3,2,1,0:T(8,128)S(1)}, u32[]{:S(2)}) copy-start(f32[8,2,64,256]{3,2,1,0:T(8,128)S(1)} %get-tuple-element.37) | copy-start | bytes 3145732
  252.7 4.8 copy-start.11
  257.6 3.8 copy-start.13
  260.1 5.8 %slice-start = ((s8[7340032]{0:T(1024)(128)(4,1)}), s8[4194304]{0:T(1024)(128)(4,1)S(1)}, s32[]{:S(2)}) async-start(s8[7340032]{0:T(1024)(128)(4,1)} %bitcast.104), calls=%async_computation.10 | async-start | bytes 8388608
  262.2 3.7 slice-start.1
  264.5 1.4 copy-start.2
  291.1 200.7 %reduce-scatter.6.cloned.1.call-start = ((), (), s32[]{:S(2)}) async-start(), calls=%async_computation.8 | async-start | bytes 9437184 | tf_op jit(solution)/shard_map/reduce_scatter | solution.py:94
  291.1 4.3 copy-start.10
  295.5 13.7 %slice-start.2 = ((s8[8388608]{0:T(1024)(128)(4,1)}), s8[4194304]{0:T(1024)(128)(4,1)S(1)}, s32[]{:S(2)}) async-start(s8[8388608]{0:T(1024)(128)(4,1)} %bitcast.107), calls=%async_computation.12 | async-start | bytes 8388608
  299.1 10.1 %slice-start.3 = ((s8[8388608]{0:T(1024)(128)(4,1)}), s8[4194304]{0:T(1024)(128)(4,1)S(1)}, s32[]{:S(2)}) async-start(s8[8388608]{0:T(1024)(128)(4,1)} %bitcast.107), calls=%async_computation.13 | async-start | bytes 8388608
  320.6 209.7 %reduce-scatter.4.cloned.1.call-start = ((), (), s32[]{:S(2)}) async-start(), calls=%async_computation.7 | async-start | bytes 8912896 | tf_op jit(solution)/shard_map/reduce_scatter | solution.py:91
  331.8 1.2 copy-start.6
  333.0 14.0 %copy-start.3 = (f32[32,8,8,256]{3,1,2,0:T(8,128)S(1)}, f32[32,8,8,256]{3,1,2,0:T(8,128)}, u32[]{:S(2)}) copy-start(f32[32,8,8,256]{3,1,2,0:T(8,128)} %copy-done.2) | copy-start | bytes 6291460
  333.0 14.0 %copy-start.8 = (f32[896,256]{1,0:T(8,128)S(1)}, f32[896,256]{1,0:T(8,128)}, u32[]{:S(2)}) copy-start(f32[896,256]{1,0:T(8,128)} %param.16) | copy-start | bytes 2752516
  373.9 112.6 %all-to-all-start.1 = ((f32[128,2,8,896]{3,2,1,0:T(8,128)}), f32[128,2,8,896]{3,2,1,0:T(8,128)}, u32[]{:S(2)}, u32[]{:S(2)}) async-start(f32[128,2,8,896]{3,2,1,0:T(8,128)} %bitcast.109), calls=%async_computation.4 | async-start | bytes 14680064 | tf_op jit(solution)/shard_map/all_to_all | solution.py:114
Sparse Core Ops, SparseCore 0:
  10.1 148.1 all-gather.4
  160.5 76.9 all-gather.2
  291.2 30.5 reduce-scatter.7
  324.1 53.7 reduce-scatter.5
  381.7 148.5 reduce-scatter.3
where the time goes:
time: 543 us; the launch traced here: 537 us
  waiting for transfers between devices  308 us (57%)
  matrix products  156 us (29%)
  local copies, waits for them, and re-layouts  28.2 us (5%)
  starting transfers between devices  21 us (4%)
  between operations  14.5 us (3%)
  other arithmetic  9.07 us (2%)
    all_to_all x1, waiting for transfers between devices, body(): lax.all_to_all(backward, ('wide', 'narrow'), split_axis=0, concat_axis=0,...  102 us
    all_to_all x1, waiting for transfers between devices, body(): lax.all_to_all(spread, ('wide', 'narrow'), split_axis=0, concat_axis=0, t...  92.5 us
    all_gather x1, waiting for transfers between devices, body(): lax.all_gather(hidden_states, 'narrow', axis=1, tiled=True)  68.2 us
    reduce_scatter x1, waiting for transfers between devices, body(): lax.psum_scatter(input_term, 'narrow', scatter_dimension=1, tiled=True)  35.2 us
    dot_general x1, matrix products, body(): lax.dot_general(flat_neigh, joined, (((0,), (0,)), ((), ())), precision=H...  25.1 us
    dot_general x1, matrix products, body(): lax.dot_general(d_keys, w_key, (((1,), (1,)), ((), ())), precision=HIGH)  14 us
    dot_general x1, matrix products, body(): lax.dot_general(d_values, w_value, (((1,), (1,)), ((), ())), precision=HIGH)  13.7 us
    all_to_all x1, starting transfers between devices, body(): lax.all_to_all(spread, ('wide', 'narrow'), split_axis=0, concat_axis=0, t...  11.9 us
  transfers between devices with their start and end apart: 7, of which 5 were waited for; matrix products, arithmetic and copies ran while one was open for 26% of the time, Pallas kernels for 0%

commit v1 on v0

v1 whole, which is shorter than its diff:
```python
import functools

import jax
import jax.numpy as jnp
from jax import lax
from jax.experimental import pallas as pl
from jax.experimental.pallas import tpu as pltpu
from jax.sharding import PartitionSpec as P

HEAD_DIM = 128
SPAN = 64
NEIGH = 2
SIDE = 4
VMEM_LIMIT = 60 * 1024 * 1024

HIGH = lax.Precision.HIGHEST
MID = lax.Precision.HIGH
MESH = pl.DeviceIdType.MESH


def wrap(value):
    return lax.rem(value + 2 * SIDE, SIDE)


class Place:
    def __init__(self):
        me = lax.axis_index("narrow")
        self.x = me // SIDE
        self.y = lax.rem(me, SIDE)

    def own(self, half):
        return (self.x, self.y) if half == 0 else (self.y, self.x)

    @staticmethod
    def block(half, first, second):
        return (first, second) if half == 0 else (second, first)

    def device(self, half, first, second):
        bx, by = self.block(half, first, second)
        return {"narrow": bx * SIDE + by}

    def line(self, half, turn, shift):
        first, second = self.own(half)
        if isinstance(turn, int) and turn == 0:
            return wrap(first + shift), second
        return first, wrap(second + shift)


def greet(place):
    groups = lax.axis_size("wide")
    group = lax.axis_index("wide")
    barrier = pltpu.get_barrier_semaphore()
    for half in (0, 1):
        for shift in (1, -1):
            pl.semaphore_signal(
                barrier,
                inc=1,
                device_id=place.device(half, *place.line(half, 0, shift)),
                device_id_type=MESH,
            )
    for step in range(1, groups):
        pl.semaphore_signal(
            barrier,
            inc=1,
            device_id={"wide": lax.rem(group + step, groups)},
            device_id_type=MESH,
        )
    pl.semaphore_wait(barrier, 4 + groups - 1)


def exchange(out_ref, in_ref, send, recv, local):
    groups = lax.axis_size("wide")
    group = lax.axis_index("wide")
    copies = []
    for step in range(1, groups):
        peer = lax.rem(group + step, groups)
        copy = pltpu.make_async_remote_copy(
            src_ref=out_ref.at[peer],
            dst_ref=in_ref.at[group],
            send_sem=send.at[step],
            recv_sem=recv.at[step],
            device_id={"wide": peer},
            device_id_type=MESH,
        )
        copy.start()
        copies.append(copy)
    mine = pltpu.make_async_copy(out_ref.at[group], in_ref.at[group], local)
    mine.start()
    copies.append(mine)
    return copies


class Gather:
    def __init__(self, place, buf, send, recv):
        self.place, self.buf, self.send, self.recv = place, buf, send, recv
        self.rows = buf.shape[2]

    def copy(self, half, turn, kind, block, dest):
        rows = self.rows // 2 if kind < 2 else self.rows // 4
        start = half * (self.rows // 2) + (self.rows // 4 if kind == 3 else 0)
        bx, by = self.place.block(half, *block)
        piece = self.buf.at[bx, by, pl.ds(start, rows)]
        slot = (half * 5 + turn) * 4 + kind
        return pltpu.make_async_remote_copy(
            src_ref=piece,
            dst_ref=piece,
            send_sem=self.send.at[slot],
            recv_sem=self.recv.at[slot],
            device_id=self.place.device(half, *dest),
            device_id_type=MESH,
        )

    def at(self, half, turn, shift):
        first, second = self.place.own(half)
        if isinstance(turn, int) and turn == 0:
            return wrap(first + shift), second
        return wrap(first + turn - 1), wrap(second + shift)

    def describe(self, half, turn, kind):
        shift = (0, 0, -1, 1)[kind]
        ahead = (1, -1, 1, -1)[kind]
        return self.copy(
            half, turn, kind, self.at(half, turn, shift), self.place.line(half, turn, ahead)
        )

    def arrival(self, half, turn, kind):
        shift = (-1, 1, 2, 2)[kind]
        ahead = (1, -1, 1, -1)[kind]
        return self.copy(
            half, turn, kind, self.at(half, turn, shift), self.place.line(half, turn, ahead)
        )

    def begin(self, half, turn):
        self.describe(half, turn, 0).start()
        self.describe(half, turn, 1).start()

    def forward(self, half, turn):
        for kind in (0, 1):
            self.arrival(half, turn, kind).wait_recv()
            self.describe(half, turn, kind + 2).start()

    def finish(self, half, turn):
        for kind in (2, 3):
            self.arrival(half, turn, kind).wait_recv()

    def drain(self):
        for half in (0, 1):
            for turn in range(5):
                for kind in range(4):
                    self.describe(half, turn, kind).wait_send()


def gather_kernel(
    hid_ref,
    cot_ref,
    going_ref,
    slot_ref,
    wq_ref,
    wo_ref,
    wk_ref,
    wv_ref,
    hid_out,
    cot_out,
    nei_out,
    q_ref,
    da_ref,
    keys_ref,
    values_ref,
    hid,
    cot,
    nei,
    wq,
    wo,
    wkv,
    came,
    hid_send,
    hid_recv,
    cot_send,
    cot_recv,
    nei_send,
    nei_recv,
    swap_send,
    swap_recv,
    load_sem,
    store_sem,
):
    place = Place()
    x, y = place.x, place.y
    width = q_ref.shape[1]
    tokens = q_ref.shape[0]
    piece_rows = going_ref.shape[2]
    inst = nei.shape[2] // piece_rows
    cap = going_ref.shape[1]
    own = [
        pltpu.make_async_copy(hid_ref, hid.at[x, y], load_sem.at[0]),
        pltpu.make_async_copy(cot_ref, cot.at[x, y], load_sem.at[1]),
    ]
    weights = [
        pltpu.make_async_copy(wq_ref, wq, load_sem.at[2]),
        pltpu.make_async_copy(wo_ref, wo, load_sem.at[3]),
        pltpu.make_async_copy(wk_ref, wkv.at[:, pl.ds(0, width)], load_sem.at[4]),
        pltpu.make_async_copy(wv_ref, wkv.at[:, pl.ds(width, width)], load_sem.at[5]),
    ]
    for copy in own:
        copy.start()
    greet(place)
    swaps = exchange(going_ref, came, swap_send, swap_recv, load_sem.at[6])
    for copy in own:
        copy.wait()
    gathers = [
        Gather(place, hid, hid_send, hid_recv),
        Gather(place, cot, cot_send, cot_recv),
        Gather(place, nei, nei_send, nei_recv),
    ]
    for turn in (0, 1):
        for gather in gathers[:2]:
            for half in (0, 1):
                gather.begin(half, turn)
    for copy in weights:
        copy.start()
    for copy in swaps:
        copy.wait()
    for i in range(inst):
        slot = slot_ref[i]
        nei[x, y, pl.ds(i * piece_rows, piece_rows), :] = came[slot // cap, lax.rem(slot, cap)]
    for turn in (0, 1):
        for half in (0, 1):
            gathers[2].begin(half, turn)
    for gather in gathers:
        for half in (0, 1):
            gather.forward(half, 0)
        for half in (0, 1):
            gather.begin(half, 2)
            gather.begin(half, 4)
    for gather in gathers:
        for half in (0, 1):
            gather.finish(half, 0)
            gather.begin(half, 3)
    for copy in weights:
        copy.wait()
    q_ref[...] = jnp.zeros_like(q_ref)
    da_ref[...] = jnp.zeros_like(da_ref)

    def turn_of(step):
        return step + (step // 2) * (1 - 2 * lax.rem(step, 2)) + 1

    def project(half, first):
        rows = pl.ds(half * (tokens // 2), tokens // 2)

        def column(second, carry):
            bx, by = place.block(half, first, second)
            part = pl.ds(pl.multiple_of((bx * SIDE + by) * width, width), width)
            q_ref[rows, :] += jnp.dot(
                hid[bx, by, rows, :], wq[part, :], precision=HIGH,
                preferred_element_type=jnp.float32,
            )
            da_ref[rows, :] += jnp.dot(
                cot[bx, by, rows, :], wo[part, :], precision=HIGH,
                preferred_element_type=jnp.float32,
            )
            return carry

        lax.fori_loop(0, SIDE, column, 0)
        few = nei.shape[2] // 2
        rows = pl.ds(half * few, few)
        if half == 0:
            blocks = nei[first, :, rows, :]
        else:
            blocks = nei[:, first, rows, :]
        both = jnp.dot(
            blocks.reshape(SIDE * few, nei.shape[3]), wkv[...], precision=HIGH,
            preferred_element_type=jnp.float32,
        ).reshape(SIDE, few, 2 * width)
        if half == 0:
            keys_ref[first, :, rows, :] = both[:, :, :width]
            values_ref[first, :, rows, :] = both[:, :, width:]
        else:
            keys_ref[:, first, rows, :] = both[:, :, :width]
            values_ref[:, first, rows, :] = both[:, :, width:]

    def keep(half, turn, first):
        copies = []
        for which, (buf, out) in enumerate(((hid, hid_out), (cot, cot_out), (nei, nei_out))):
            rows = pl.ds(half * (buf.shape[2] // 2), buf.shape[2] // 2)
            at = (first, slice(None), rows) if half == 0 else (slice(None), first, rows)
            copies.append(
                pltpu.make_async_copy(
                    buf.at[at], out.at[at], store_sem.at[(which * 2 + half) * 5 + turn]
                )
            )
        return copies

    def pass_on(turn):
        for gather in gathers:
            for half in (0, 1):
                gather.forward(half, turn)

    pass_on(turn_of(0))

    def main(step, carry):
        @pl.when(step < SIDE - 1)
        def _():
            pass_on(turn_of(step + 1))

        turn = turn_of(step)
        for half in (0, 1):
            for gather in gathers:
                gather.finish(half, turn)
            first = wrap(place.own(half)[0] + turn - 1)
            for copy in keep(half, turn, first):
                copy.start()
            project(half, first)
        return carry

    lax.fori_loop(0, SIDE, main, 0)
    for gather in gathers:
        gather.drain()

    def stored(turn, carry):
        for half in (0, 1):
            first = wrap(place.own(half)[0] + turn - 1)
            for copy in keep(half, turn, first):
                copy.wait()
        return carry

    lax.fori_loop(1, SIDE + 1, stored, 0)


class Reduce:
    def __init__(self, place, part, whole_in, quarter_in, send, recv):
        self.place, self.part = place, part
        self.whole_in, self.quarter_in = whole_in, quarter_in
        self.send, self.recv = send, recv
        self.rows = part.shape[2]

    def at(self, half, turn, shift):
        first, second = self.place.own(half)
        if isinstance(turn, int) and turn == 0:
            return wrap(first + shift), second
        return wrap(first + turn - 1), wrap(second + shift)

    def piece(self, half, block, kind):
        rows = self.rows // 2 if kind < 2 else self.rows // 4
        start = half * (self.rows // 2) + (self.rows // 4 if kind == 3 else 0)
        bx, by = self.place.block(half, *block)
        return bx, by, pl.ds(start, rows)

    def copy(self, half, turn, kind):
        ahead = (1, -1, 1, -1)[kind]
        shift = (1, -1, 2, 2)[kind]
        slot = (half * 5 + turn) * 2 + kind % 2
        landing = (self.whole_in if kind < 2 else self.quarter_in).at[slot]
        bx, by, rows = self.piece(half, self.at(half, turn, shift), kind)
        sem = (half * 5 + turn) * 4 + kind
        return pltpu.make_async_remote_copy(
            src_ref=self.part.at[bx, by, rows],
            dst_ref=landing,
            send_sem=self.send.at[sem],
            recv_sem=self.recv.at[sem],
            device_id=self.place.device(half, *self.place.line(half, turn, ahead)),
            device_id_type=MESH,
        )

    def begin(self, half, turn):
        for kind in (2, 3):
            self.copy(half, turn, kind).start()

    def middle(self, half, turn):
        for kind in (2, 3):
            self.copy(half, turn, kind).wait_recv()
            slot = (half * 5 + turn) * 2 + kind % 2
            shift = 1 if kind == 2 else -1
            bx, by, rows = self.piece(half, self.at(half, turn, shift), kind)
            self.part[bx, by, rows, :] += self.quarter_in[slot]
            self.copy(half, turn, kind - 2).start()

    def finish(self, half, turn):
        for kind in (0, 1):
            self.copy(half, turn, kind).wait_recv()
        slot = (half * 5 + turn) * 2
        bx, by, rows = self.piece(half, self.at(half, turn, 0), 0)
        self.part[bx, by, rows, :] += self.whole_in[slot] + self.whole_in[slot + 1]

    def drain(self):
        for half in (0, 1):
            for turn in range(5):
                for kind in range(4):
                    self.copy(half, turn, kind).wait_send()


TURNS = (3, 2, 4, 1)


def reduce_kernel(
    dq_ref,
    dk_ref,
    dv_ref,
    inst_ref,
    wq_ref,
    wk_ref,
    wv_ref,
    gh_ref,
    came_ref,
    gpart,
    dpart,
    ghalf,
    gquarter,
    dhalf,
    dquarter,
    wq,
    wk,
    wv,
    going,
    mine,
    g_send,
    g_recv,
    d_send,
    d_recv,
    swap_send,
    swap_recv,
    load_sem,
):
    place = Place()
    x, y = place.x, place.y
    tokens, width = dq_ref.shape
    groups, cap, piece_rows, _ = going.shape
    weights = [
        pltpu.make_async_copy(wq_ref, wq, load_sem.at[0]),
        pltpu.make_async_copy(wk_ref, wk, load_sem.at[1]),
        pltpu.make_async_copy(wv_ref, wv, load_sem.at[2]),
    ]
    for copy in weights:
        copy.start()
    greet(place)
    for copy in weights:
        copy.wait()
    wide_sum = Reduce(place, gpart, ghalf, gquarter, g_send, g_recv)
    near_sum = Reduce(place, dpart, dhalf, dquarter, d_send, d_recv)
    transposed = (((1,), (1,)), ((), ()))

    def hidden_part(half, block):
        bx, by = place.block(half, *block)
        rows = pl.ds(half * (tokens // 2), tokens // 2)
        part = pl.ds(pl.multiple_of((bx * SIDE + by) * width, width), width)
        gpart[bx, by, rows, :] = lax.dot_general(
            dq_ref[rows, :], wq[part, :], transposed, precision=HIGH,
            preferred_element_type=jnp.float32,
        )

    def order(step):
        return 3 - step + 3 * (step // 2) - 2 * (step // 3)

    def g_first(step, carry):
        turn = order(step)
        for half in (0, 1):
            hidden_part(half, wide_sum.at(half, turn, 2))
            wide_sum.begin(half, turn)
        return carry

    lax.fori_loop(0, SIDE, g_first, 0)

    def d_all(step, carry):
        bx, by = step // SIDE, lax.rem(step, SIDE)
        dpart[bx, by] = lax.dot_general(
            dk_ref[bx, by], wk[...], transposed, precision=HIGH,
            preferred_element_type=jnp.float32,
        ) + lax.dot_general(
            dv_ref[bx, by], wv[...], transposed, precision=HIGH,
            preferred_element_type=jnp.float32,
        )
        return carry

    lax.fori_loop(0, SIDE * SIDE, d_all, 0)
    for turn in TURNS:
        for half in (0, 1):
            near_sum.begin(half, turn)

    def g_second(step, carry):
        turn = order(step)
        for half in (0, 1):
            for shift in (1, -1):
                hidden_part(half, wide_sum.at(half, turn, shift))
            wide_sum.middle(half, turn)
        return carry

    lax.fori_loop(0, SIDE, g_second, 0)
    for turn in TURNS:
        for half in (0, 1):
            near_sum.middle(half, turn)
    def g_third(step, carry):
        turn = order(step)
        for half in (0, 1):
            hidden_part(half, wide_sum.at(half, turn, 0))
        return carry

    lax.fori_loop(0, SIDE, g_third, 0)
    for target in (wide_sum, near_sum):
        for half in (0, 1):
            target.finish(half, 3)
            target.begin(half, 0)
        for half in (0, 1):
            for turn in (2, 4):
                target.finish(half, turn)
            target.middle(half, 0)
        for half in (0, 1):
            target.finish(half, 1)
    for half in (0, 1):
        near_sum.finish(half, 0)
    for i in range(groups * cap):
        mine[i] = dpart[x, y, pl.ds(i * piece_rows, piece_rows), :]
    for slot in range(groups * cap):
        going[slot // cap, slot % cap] = mine[inst_ref[slot]]
    swaps = exchange(going, came_ref, swap_send, swap_recv, load_sem.at[3])
    for half in (0, 1):
        wide_sum.finish(half, 0)
    gh_ref[...] = gpart[x, y]
    for copy in swaps:
        copy.wait()
    wide_sum.drain()
    near_sum.drain()


def attention_kernel(q_ref, da_ref, keys_ref, values_ref, att_ref, dq_ref, dk_ref, dv_ref):
    scale = HEAD_DIM ** (-0.5)
    heads = q_ref.shape[1] // HEAD_DIM
    spans = q_ref.shape[0] // SPAN
    few = keys_ref.shape[2] // spans
    near = SIDE * SIDE * few

    def dot(a, b, ca, cb):
        return lax.dot_general(
            a, b, (((ca,), (cb,)), ((), ())), precision=HIGH, preferred_element_type=jnp.float32
        )

    def span(c, carry):
        rows = pl.ds(pl.multiple_of(c * SPAN, SPAN), SPAN)
        pieces = pl.ds(pl.multiple_of(c * few, few), few)
        for head in range(heads):
            cols = pl.ds(head * HEAD_DIM, HEAD_DIM)
            q = q_ref[rows, cols]
            da = da_ref[rows, cols]
            k = keys_ref[:, :, pieces, cols].reshape(near, HEAD_DIM)
            v = values_ref[:, :, pieces, cols].reshape(near, HEAD_DIM)
            scores = dot(q, k, 1, 1) * scale
            top = jnp.max(scores, axis=-1, keepdims=True)
            e = jnp.exp(scores - top)
            probs = e / jnp.sum(e, axis=-1, keepdims=True)
            att_ref[rows, cols] = dot(probs, v, 1, 0)
            dp = dot(da, v, 1, 1)
            ds = probs * (dp - jnp.sum(dp * probs, axis=-1, keepdims=True)) * scale
            dq_ref[rows, cols] = dot(ds, k, 1, 0)
            shape = (SIDE, SIDE, few, HEAD_DIM)
            dk_ref[:, :, pieces, cols] = dot(ds, q, 0, 0).reshape(shape)
            dv_ref[:, :, pieces, cols] = dot(probs, da, 0, 0).reshape(shape)
        return carry

    lax.fori_loop(0, spans, span, 0)


def vmem(n):
    return [pl.BlockSpec(memory_space=pltpu.VMEM)] * n


def hbm(n):
    return [pl.BlockSpec(memory_space=pl.ANY)] * n


def smem(n):
    return [pl.BlockSpec(memory_space=pltpu.SMEM)] * n


def f32(*shape):
    return jax.ShapeDtypeStruct(shape, jnp.float32)


def gather_call(hidden, cotangent, outgoing, slots, wq, wo, wk, wv):
    tokens, width = hidden.shape
    groups, cap, piece_rows, enc = outgoing.shape
    rows = slots.shape[0] * piece_rows
    dma = pltpu.SemaphoreType.DMA
    out_shape = [
        f32(SIDE, SIDE, tokens, width),
        f32(SIDE, SIDE, tokens, width),
        f32(SIDE, SIDE, rows, enc),
        f32(tokens, width),
        f32(tokens, width),
        f32(SIDE, SIDE, rows, width),
        f32(SIDE, SIDE, rows, width),
    ]
    scratch = [
        pltpu.VMEM((SIDE, SIDE, tokens, width), jnp.float32),
        pltpu.VMEM((SIDE, SIDE, tokens, width), jnp.float32),
        pltpu.VMEM((SIDE, SIDE, rows, enc), jnp.float32),
        pltpu.VMEM(wq.shape, jnp.float32),
        pltpu.VMEM(wo.shape, jnp.float32),
        pltpu.VMEM((enc, 2 * width), jnp.float32),
        pltpu.VMEM(outgoing.shape, jnp.float32),
    ]
    scratch += [dma((40,))] * 6 + [dma((groups,))] * 2 + [dma((8,)), dma((30,))]
    return pl.pallas_call(
        gather_kernel,
        out_shape=out_shape,
        in_specs=hbm(2) + vmem(1) + smem(1) + hbm(4),
        out_specs=hbm(3) + vmem(4),
        scratch_shapes=scratch,
        compiler_params=pltpu.CompilerParams(
            collective_id=0, has_side_effects=True, vmem_limit_bytes=VMEM_LIMIT
        ),
        cost_estimate=pl.CostEstimate(flops=24_000_000_000, bytes_accessed=60_000_000, transcendentals=0),
    )(hidden, cotangent, outgoing, slots, wq, wo, wk, wv)


def reduce_call(dq, dk, dv, inst_of, wq, wk, wv, groups):
    tokens, width = dq.shape
    rows = dk.shape[2]
    enc = wk.shape[0]
    slots = inst_of.shape[0]
    cap = slots // groups
    piece_rows = rows // slots
    dma = pltpu.SemaphoreType.DMA
    going = (groups, cap, piece_rows, enc)
    scratch = [
        pltpu.VMEM((SIDE, SIDE, tokens, width), jnp.float32),
        pltpu.VMEM((SIDE, SIDE, rows, enc), jnp.float32),
        pltpu.VMEM((20, tokens // 2, width), jnp.float32),
        pltpu.VMEM((20, tokens // 4, width), jnp.float32),
        pltpu.VMEM((20, rows // 2, enc), jnp.float32),
        pltpu.VMEM((20, rows // 4, enc), jnp.float32),
        pltpu.VMEM(wq.shape, jnp.float32),
        pltpu.VMEM(wk.shape, jnp.float32),
        pltpu.VMEM(wv.shape, jnp.float32),
        pltpu.VMEM(going, jnp.float32),
        pltpu.VMEM((slots, piece_rows, enc), jnp.float32),
    ]
    scratch += [dma((40,))] * 4 + [dma((groups,))] * 2 + [dma((4,))]
    return pl.pallas_call(
        reduce_kernel,
        out_shape=[f32(tokens, width), f32(*going)],
        in_specs=vmem(3) + smem(1) + hbm(3),
        out_specs=vmem(2),
        scratch_shapes=scratch,
        compiler_params=pltpu.CompilerParams(
            collective_id=1, has_side_effects=True, vmem_limit_bytes=VMEM_LIMIT
        ),
        cost_estimate=pl.CostEstimate(flops=50_000_000_000, bytes_accessed=60_000_000, transcendentals=0),
    )(dq, dk, dv, inst_of, wq, wk, wv)


def body(
    hidden_states, out_cotangent, enc_table, nbr_ids, owner_map, w_query, w_key, w_value, w_out
):
    groups = lax.axis_size("wide")
    group = lax.axis_index("wide")
    stored = enc_table.shape[0]
    table_size = owner_map.shape[0]
    tokens, width = hidden_states.shape
    inst = NEIGH * (tokens // SPAN)
    capacity = inst // groups
    match = nbr_ids[:, :, None] == jnp.arange(table_size, dtype=jnp.int32)[None, None, :]
    slots = jnp.sum(jnp.where(match, owner_map[None, None, :], 0), axis=-1)
    slots = slots.reshape(groups, inst)
    owners = slots // stored
    local_slot = slots - owners * stored
    earlier = jnp.arange(inst)[None, :] < jnp.arange(inst)[:, None]
    same = owners[:, :, None] == owners[:, None, :]
    rank = jnp.sum((same & earlier[None, :, :]).astype(jnp.int32), axis=-1)
    slot_range = jnp.arange(capacity, dtype=jnp.int32)
    pick = ((owners[:, None, :] == group) & (rank[:, None, :] == slot_range[None, :, None])).astype(
        jnp.float32
    )
    one_local = (
        local_slot[:, :, None] == jnp.arange(stored, dtype=jnp.int32)[None, None, :]
    ).astype(jnp.float32)
    place = jnp.einsum("bri,bis->brs", pick, one_local, precision=HIGH)
    outgoing = jnp.einsum("brs,sxe->brxe", place, enc_table, precision=HIGH)
    mine = lax.dynamic_index_in_dim(owners * capacity + rank, group, 0, keepdims=False)
    numbers = jnp.arange(inst, dtype=jnp.int32)
    inst_of = jnp.sum(jnp.where(mine[None, :] == numbers[:, None], numbers[None, :], 0), axis=1)

    hid, cot, nei, query, d_att, keys, values = gather_call(
        hidden_states, out_cotangent, outgoing, mine, w_query, w_out, w_key, w_value
    )
    rows, enc = nei.shape[2:]
    attended, d_query, d_keys, d_values = pl.pallas_call(
        attention_kernel,
        out_shape=[f32(*t.shape) for t in (query, query, keys, values)],
        in_specs=vmem(4),
        out_specs=vmem(4),
        compiler_params=pltpu.CompilerParams(vmem_limit_bytes=40 * 1024 * 1024),
    )(query, d_att, keys, values)

    def over_tokens(a, b):
        out = jnp.einsum("mtf,td->mfd", a.reshape(SIDE * SIDE, tokens, width), b, precision=MID)
        return lax.psum_scatter(
            out.reshape(-1, width), "wide", scatter_dimension=0, tiled=True
        )

    def over_rows(b):
        out = lax.dot_general(
            nei.reshape(-1, enc), b.reshape(-1, width), (((0,), (0,)), ((), ())), precision=MID
        )
        return lax.psum_scatter(out, "wide", scatter_dimension=0, tiled=True)

    grad_out = over_tokens(cot, attended)
    grad_query = over_tokens(hid, d_query)
    grad_key = over_rows(d_keys)
    grad_value = over_rows(d_values)
    grad_hidden, arrived = reduce_call(
        d_query, d_keys, d_values, inst_of, w_query, w_key, w_value, groups
    )
    grad_table = jnp.einsum("brs,brxe->sxe", place, arrived, precision=HIGH)
    return (grad_hidden, grad_query, grad_key, grad_value, grad_out, grad_table)


def solution(mesh):
    placed = (
        P("wide", "narrow"),
        P("wide", "narrow"),
        P("wide", "narrow", None),
        P(),
        P(),
        P(None, "narrow"),
        P(None, "narrow"),
        P(None, "narrow"),
        P(None, "narrow"),
    )
    return jax.shard_map(
        body,
        mesh=mesh,
        in_specs=placed,
        out_specs=(
            P("wide", "narrow"),
            P("wide", "narrow"),
            P("wide", "narrow"),
            P("wide", "narrow"),
            P("wide", "narrow"),
            P("wide", "narrow", None),
        ),
        check_vma=False,
    )
```

time: 543 us -> 378 us (0.70); the launches traced: 537 us -> 378 us
  waiting for transfers between devices: 308 us -> 0.07 us
  Pallas kernels: 0 us -> 292 us
  matrix products: 156 us -> 39.5 us
  starting transfers between devices: 21 us -> 0.57 us
  other arithmetic: 9.07 us -> 1.83 us
    pallas_call x0 -> x3, Pallas kernels: none -> 292 us  [the longest x1 148 us: gather_call(): pl.pallas_call(gather_kernel, out_shape=out_shape, in_specs=hbm(2) + vmem...]
    all_to_all x2 -> x0, waiting for transfers between devices: 195 us -> none  [the longest x1 102 us: body(): lax.all_to_all(backward, ('wide', 'narrow'), split_axis=0, concat_axis=0,...]
    dot_general x18 -> x4, matrix products: 154 us -> 36.1 us  [the longest x2 18.4 us: over_rows(): lax.dot_general(nei.reshape(-1, enc), b.reshape(-1, width), (((0,), (0,))...]
    all_gather x2 -> x0, waiting for transfers between devices: 76.8 us -> none  [the longest x1 68.2 us: body(): lax.all_gather(hidden_states, 'narrow', axis=1, tiled=True)]
    reduce_scatter x3 -> x4, waiting for transfers between devices: 35.2 us -> 0.01 us  [the longest x2 0.01 us: over_rows(): return lax.psum_scatter(out, 'wide', scatter_dimension=0, tiled=True)]
    all_to_all x2 -> x0, starting transfers between devices: 20.8 us -> none  [the longest x1 11.9 us: body(): lax.all_to_all(spread, ('wide', 'narrow'), split_axis=0, concat_axis=0, t...]
    reshape x2, local copies, waits for them, and re-layouts: 2.11 us -> 18.7 us  [over_tokens(): a.reshape(SIDE * SIDE, tokens, width)]
    transpose x5 -> x0, local copies, waits for them, and re-layouts: 8.96 us -> none  [the longest x1 5.53 us: body(): backward = jnp.einsum('iwr,inxe->wnrxe', take, split_rows, precision=HIGH)]
  transfers between devices with their start and end apart: 7 -> 4, of which waited for: 5 -> 0; matrix products, arithmetic and copies ran while one was open for 26% -> 13% of each run, Pallas kernels for 0% -> 32%
where the time goes in v1:
time: 378 us
  Pallas kernels  292 us (77%)
  matrix products  39.5 us (10%)
  local copies, waits for them, and re-layouts  29.6 us (8%)
  between operations  13.9 us (4%)
    pallas_call x1, Pallas kernels, gather_call(): pl.pallas_call(gather_kernel, out_shape=out_shape, in_specs=hbm(2) + vmem...  148 us
    pallas_call x1, Pallas kernels, reduce_call(): pl.pallas_call(reduce_kernel, out_shape=[f32(tokens, width), f32(*going)]...  122 us
    pallas_call x1, Pallas kernels, body(): pl.pallas_call(attention_kernel, out_shape=[f32(*t.shape) for t in (query...  21.7 us
    reshape x2, local copies, waits for them, and re-layouts, over_tokens(): a.reshape(SIDE * SIDE, tokens, width)  18.7 us
    dot_general x2, matrix products, over_rows(): lax.dot_general(nei.reshape(-1, enc), b.reshape(-1, width), (((0,), (0,))...  18.4 us
    dot_general x2, matrix products, over_tokens(): jnp.einsum('mtf,td->mfd', a.reshape(SIDE * SIDE, tokens, width), b, preci...  17.7 us
    unnamed x18, local copies, waits for them, and re-layouts  9.38 us
  transfers between devices with their start and end apart: 4, of which 0 were waited for; matrix products, arithmetic and copies ran while one was open for 13% of the time, Pallas kernels for 32%

profile of v1, /device:TPU:1, one launch (start us, length us, event | category | flops | bytes accessed | tf_op | source)
XLA Modules:
  0.0 377.5 jit_solution(4369131107897506620)
XLA Ops:
  7.2 0.0 reduce-scatter.9.cloned.1.call-start
  7.2 0.9 select_reduce_fusion
  8.1 0.1 copy.35
  8.2 0.1 reshape.125
  8.3 0.3 convert_reduce_fusion
  8.6 0.2 fusion.4
  8.8 1.6 fusion
  10.4 0.9 copy.38.going_ref
  11.2 0.5 dynamic-slice_bitcast_fusion.slot_ref
  11.8 147.9 %shard_map.136 = (f32[4,4,512,256]{3,2,1,0:T(8,128)}, f32[4,4,512,256]{3,2,1,0:T(8,128)}, f32[4,4,128,896]{3,2,1,0:T(8,128)}, f32[512,256]{1,0:T(8,128)}, f32[51...) custom-call(f32[512,256]{1,0:T(8,128)} %hid_ref.1, f32[512,256]{1,0:T(8,128)} %cot_ref.1, ...), custom_call_target="tpu_custom_call" | custom-call | flops 24000000000 | bytes 60000000 | tf_op jit(solution)/shard_map/pallas_call | solution.py:600
  159.7 0.0 copy-start.2
  159.7 1.6 copy-done.2
  161.3 0.0 copy-start.3
  161.3 1.6 copy-done.3
  162.9 0.0 copy-start.5
  162.9 1.0 copy-done.5
  163.9 0.0 copy-start.6
  163.9 1.0 copy-done.6
  165.0 21.7 %shard_map.137 = (f32[512,256]{1,0:T(8,128)S(1)}, f32[512,256]{1,0:T(8,128)S(1)}, f32[4,4,128,256]{3,2,1,0:T(8,128)S(1)}, f32[4,4,128,256]{3,2,1,0:T(8,128)S(1)}) custom-call(f32[512,256]{1,0:T(8,128)S(1)} %copy-done.5, f32[512,256]{1,0:T(8,128)S(1)} %copy-done.6, f32[4,4,128,256]{3,2,1,0:T(8,128)S(1)} %copy-done.2, f32[4,4,128,256]{3,2,1,0:T(8,128)S(1)} %copy-done.3), custom_call_target="tpu_custom_call" | custom-call | tf_op jit(solution)/shard_map/pallas_call | solution.py:684
  186.7 0.0 copy-start.1
  186.7 0.0 copy-start
  186.7 0.0 copy-start.4
  186.7 1.3 copy-done.1
  188.0 9.3 %convolution_bitcast_fusion = f32[896,256]{1,0:T(8,128)} fusion(f32[4,4,128,896]{3,2,1,0:T(8,128)} %get-tuple-element.28, f32[4,4,128,256]{3,2,1,0:T(8,128)S(1)} %get-tuple-element.25.dv_ref), kind=kOutput, calls=%fused_computation | convolution fusion | flops 2818572288 | bytes 10354688 | tf_op jit(solution)/shard_map/dot_general | solution.py:699
  197.3 0.0 reduce-scatter.9.cloned.1.call-update
  197.4 0.2 reduce-scatter.7.cloned.1.call-start
  197.6 9.1 %convolution_bitcast_fusion.1 = f32[896,256]{1,0:T(8,128)} fusion(f32[4,4,128,896]{3,2,1,0:T(8,128)} %get-tuple-element.28, f32[4,4,128,256]{3,2,1,0:T(8,128)S(1)} %get-tuple-element.24.dk_ref), kind=kOutput, calls=%fused_computation.1 | convolution fusion | flops 2818572288 | bytes 10354688 | tf_op jit(solution)/shard_map/dot_general | solution.py:699
  206.7 0.0 copy-done
  206.7 0.0 reduce-scatter.7.cloned.1.call-update
  206.7 0.0 reduce-scatter.5.cloned.1.call-start
  206.8 9.3 %copy.39 = f32[16,512,256]{1,2,0:T(8,128)} copy(f32[16,512,256]{2,1,0:T(8,128)} %bitcast.39) | data formatting | bytes 16777216 | tf_op jit(solution)/shard_map/reshape | solution.py:693
  216.1 0.0 copy-done.4
  216.1 8.8 %fusion.14 = f32[4096,256]{1,0:T(8,128)} fusion(f32[4096,512]{1,0:T(8,128)} %bitcast.37, f32[512,256]{1,0:T(8,128)S(1)} %get-tuple-element.23.dq_ref), kind=kOutput, calls=%fused_computation.34 | convolution fusion | flops 3221225472 | bytes 13107200 | tf_op jit(solution)/shard_map/mtf,td->mfd/dot_general | solution.py:693
  224.9 0.0 reduce-scatter.5.cloned.1.call-update
  225.0 0.3 reduce-scatter.11.cloned.1.call-start
  225.2 9.3 %copy.42 = f32[16,512,256]{1,2,0:T(8,128)} copy(f32[16,512,256]{2,1,0:T(8,128)} %bitcast.38) | data formatting | bytes 16777216 | tf_op jit(solution)/shard_map/reshape | solution.py:693
  234.6 8.8 %fusion.15 = f32[4096,256]{1,0:T(8,128)} fusion(f32[4096,512]{1,0:T(8,128)} %bitcast.36, f32[512,256]{1,0:T(8,128)S(1)} %get-tuple-element.30), kind=kOutput, calls=%fused_computation.35 | convolution fusion | flops 3221225472 | bytes 13107200 | tf_op jit(solution)/shard_map/mtf,td->mfd/dot_general | solution.py:693
  243.4 0.0 reduce-scatter.11.cloned.1.call-update
  243.5 0.0 copy-done.7
  243.5 0.6 select_reduce_fusion.1.inst_ref
  244.1 122.5 %shard_map.138 = (f32[512,256]{1,0:T(8,128)}, f32[8,2,8,896]{3,2,1,0:T(8,128)}) custom-call(f32[512,256]{1,0:T(8,128)} %copy-done.4, f32[4,4,128,256]{3,2,1,0:T(8,128)} %copy-done, f32[4,4,128,256]{3,2,1,0:T(8,128)} %copy-done.1, s32[16]{0:T(128)} %select_reduce_fusion.1.inst_ref, f32[4096,256]{1,0:T(8,128)} %wq_ref.3, f32[896,256]{1,0:T(8,128)} %wk_ref.3, ...), custom_call_target="tpu_custom_call" | custom-call | flops 49999998976 | bytes 60000000 | tf_op jit(solution)/shard_map/pallas_call | solution.py:636
  366.6 1.6 convolution_bitcast_fusion.2
  368.2 0.9 copy.45
  369.1 0.0 reduce-scatter.9.cloned.1.call-done
  369.1 0.0 reduce-scatter.7.cloned.1.call-done
  369.1 0.0 reduce-scatter.5.cloned.1.call-done
  369.1 0.0 reduce-scatter.11.cloned.1.call-done
  369.1 1.9 copy.67
  (5 shorter events, 0.0 us)
Async XLA Ops:
  7.2 362.0 %reduce-scatter.9.cloned.1.call-start = ((), (), s32[]{:S(2)}) async-start(), calls=%async_computation.6 | async-start | bytes 1032192 | tf_op jit(solution)/shard_map/reduce_scatter | solution.py:702
  159.7 1.6 copy-start.2
  161.3 1.6 copy-start.3
  162.9 1.0 copy-start.5
  163.9 1.0 copy-start.6
  186.7 1.4 copy-start.1
  186.7 20.0 %copy-start = (f32[4,4,128,256]{3,2,1,0:T(8,128)}, f32[4,4,128,256]{3,2,1,0:T(8,128)S(1)}, u32[]{:S(2)}) copy-start(f32[4,4,128,256]{3,2,1,0:T(8,128)S(1)} %get-tuple-element.24.dk_ref) | copy-start | bytes 6291460
  186.7 29.4 %copy-start.4 = (f32[512,256]{1,0:T(8,128)}, f32[512,256]{1,0:T(8,128)S(1)}, u32[]{:S(2)}) copy-start(f32[512,256]{1,0:T(8,128)S(1)} %get-tuple-element.23.dq_ref) | copy-start | bytes 1572868
  197.4 171.8 %reduce-scatter.7.cloned.1.call-start = ((), (), s32[]{:S(2)}) async-start(), calls=%async_computation.5 | async-start | bytes 1032192 | tf_op jit(solution)/shard_map/reduce_scatter | solution.py:702
  206.7 162.4 %reduce-scatter.5.cloned.1.call-start = ((), (), s32[]{:S(2)}) async-start(), calls=%async_computation.4 | async-start | bytes 4718592 | tf_op jit(solution)/shard_map/reduce_scatter | solution.py:694
  225.0 144.2 %reduce-scatter.11.cloned.1.call-start = ((), (), s32[]{:S(2)}) async-start(), calls=%async_computation.7 | async-start | bytes 4718592 | tf_op jit(solution)/shard_map/reduce_scatter | solution.py:694
  234.6 8.9 %copy-start.7 = (s32[16]{0:T(128)S(1)}, s32[16]{0:T(128)}, u32[]{:S(2)}) copy-start(s32[16]{0:T(128)} %dynamic-slice_bitcast_fusion.slot_ref) | copy-start | bytes 196
Sparse Core Ops, SparseCore 0:
  197.5 28.3 reduce-scatter.8
  229.0 30.6 reduce-scatter.6
  262.7 36.8 reduce-scatter.4
  302.5 37.2 reduce-scatter.10

commit v2 on v1

--- a/solution.py
+++ b/solution.py
@@ -12,6 +12,7 @@
 NEIGH = 2
 SIDE = 4
 VMEM_LIMIT = 60 * 1024 * 1024
+REDUCE_LIMIT = 63 * 1024 * 1024
 
 HIGH = lax.Precision.HIGHEST
 MID = lax.Precision.HIGH
@@ -150,6 +151,44 @@
                     self.describe(half, turn, kind).wait_send()
 
 
+def attend(q_ref, da_ref, keys_ref, values_ref, att_ref, dq_ref, dk_ref, dv_ref):
+    scale = HEAD_DIM ** (-0.5)
+    heads = q_ref.shape[1] // HEAD_DIM
+    spans = q_ref.shape[0] // SPAN
+    few = keys_ref.shape[2] // spans
+    near = SIDE * SIDE * few
+
+    def dot(a, b, ca, cb, precision=MID):
+        return lax.dot_general(
+            a, b, (((ca,), (cb,)), ((), ())), precision=precision,
+            preferred_element_type=jnp.float32,
+        )
+
+    def span(c, carry):
+        rows = pl.ds(pl.multiple_of(c * SPAN, SPAN), SPAN)
+        pieces = pl.ds(pl.multiple_of(c * few, few), few)
+        for head in range(heads):
+            cols = pl.ds(head * HEAD_DIM, HEAD_DIM)
+            q = q_ref[rows, cols]
+            da = da_ref[rows, cols]
+            k = keys_ref[:, :, pieces, cols].reshape(near, HEAD_DIM)
+            v = values_ref[:, :, pieces, cols].reshape(near, HEAD_DIM)
+            scores = dot(q, k, 1, 1, HIGH) * scale
+            dp = dot(da, v, 1, 1)
+            top = jnp.max(scores, axis=-1, keepdims=True)
+            e = jnp.exp(scores - top)
+            probs = e / jnp.sum(e, axis=-1, keepdims=True)
+            ds = probs * (dp - jnp.sum(dp * probs, axis=-1, keepdims=True)) * scale
+            att_ref[rows, cols] = dot(probs, v, 1, 0)
+            dq_ref[rows, cols] = dot(ds, k, 1, 0)
+            shape = (SIDE, SIDE, few, HEAD_DIM)
+            dk_ref[:, :, pieces, cols] = dot(ds, q, 0, 0).reshape(shape)
+            dv_ref[:, :, pieces, cols] = dot(probs, da, 0, 0).reshape(shape)
+        return carry
+
+    lax.fori_loop(0, spans, span, 0)
+
+
 def gather_kernel(
     hid_ref,
     cot_ref,
@@ -162,6 +201,10 @@
     hid_out,
     cot_out,
     nei_out,
+    att_ref,
+    dq_ref,
+    dk_ref,
+    dv_ref,
     q_ref,
     da_ref,
     keys_ref,
@@ -255,7 +298,7 @@
                 preferred_element_type=jnp.float32,
             )
             da_ref[rows, :] += jnp.dot(
-                cot[bx, by, rows, :], wo[part, :], precision=HIGH,
+                cot[bx, by, rows, :], wo[part, :], precision=MID,
                 preferred_element_type=jnp.float32,
             )
             return carry
@@ -313,6 +356,7 @@
         return carry
 
     lax.fori_loop(0, SIDE, main, 0)
+    attend(q_ref, da_ref, keys_ref, values_ref, att_ref, dq_ref, dk_ref, dv_ref)
     for gather in gathers:
         gather.drain()
 
@@ -388,173 +432,314 @@
                     self.copy(half, turn, kind).wait_send()
 
 
+class Ring:
+    def __init__(self, w, near_in, whole_in, half_in, send, recv):
+        group = lax.axis_index("wide")
+        self.z, self.core = group // 2, lax.rem(group, 2)
+        self.w, self.near_in, self.whole_in, self.half_in = w, near_in, whole_in, half_in
+        self.send, self.recv = send, recv
+        self.half_rows = w.shape[1] // 2
+
+    def index(self, shift):
+        return wrap(self.z + shift) * 2 + self.core
+
+    def swap(self, turn, shift):
+        to = wrap(self.z + shift)
+        return pltpu.make_async_remote_copy(
+            src_ref=self.w.at[to * 2 + 1 - self.core],
+            dst_ref=self.near_in.at[to],
+            send_sem=self.send.at[4 + turn],
+            recv_sem=self.recv.at[4 + turn],
+            device_id={"wide": self.z * 2 + 1 - self.core},
+            device_id_type=MESH,
+        )
+
+    def take(self, turn, shift):
+        self.swap(turn, shift).wait_recv()
+        self.w[self.index(shift)] += self.near_in[wrap(self.z + shift)]
+
+    def copy(self, kind):
+        ahead = (1, -1, 1, -1)[kind]
+        shift = (1, -1, 2, 2)[kind]
+        source = self.w.at[self.index(shift)]
+        landing = self.whole_in
+        if kind >= 2:
+            source = self.w.at[self.index(shift), pl.ds((kind - 2) * self.half_rows, self.half_rows)]
+            landing = self.half_in
+        return pltpu.make_async_remote_copy(
+            src_ref=source,
+            dst_ref=landing.at[kind % 2],
+            send_sem=self.send.at[kind],
+            recv_sem=self.recv.at[kind],
+            device_id={"wide": self.index(ahead)},
+            device_id_type=MESH,
+        )
+
+    def begin(self):
+        self.take(0, 2)
+        for kind in (2, 3):
+            self.copy(kind).start()
+
+    def middle(self):
+        for kind in (2, 3):
+            shift = 1 if kind == 2 else -1
+            self.take(kind - 1, shift)
+            self.copy(kind).wait_recv()
+            rows = pl.ds((kind - 2) * self.half_rows, self.half_rows)
+            self.w[self.index(shift), rows, :] += self.half_in[kind - 2]
+            self.copy(kind - 2).start()
+        self.take(3, 0)
+
+    def finish(self):
+        for kind in (0, 1):
+            self.copy(kind).wait_recv()
+        return self.w[self.index(0)] + self.whole_in[0] + self.whole_in[1]
+
+    def drain(self):
+        for kind in range(4):
+            self.copy(kind).wait_send()
+        for turn, shift in enumerate((2, 1, 3, 0)):
+            self.swap(turn, shift).wait_send()
+
+
 TURNS = (3, 2, 4, 1)
+
+
+def shift_of(step):
+    return 2 - step + 3 * (step // 2) - 2 * (step // 3)
+
+
+def stream(count, loads, work):
+    for copy in loads(0, 0):
+        copy.start()
+
+    def one(i, carry):
+        slot = lax.rem(i, 2)
+
+        @pl.when(i + 1 < count)
+        def _():
+            for copy in loads(i + 1, 1 - slot):
+                copy.start()
+
+        for copy in loads(i, slot):
+            copy.wait()
+        work(i, slot)
+        return carry
+
+    lax.fori_loop(0, count, one, 0)
 
 
 def reduce_kernel(
     dq_ref,
-    dk_ref,
-    dv_ref,
+    att_ref,
     inst_ref,
-    wq_ref,
-    wk_ref,
-    wv_ref,
+    dk_hbm,
+    dv_hbm,
+    hid_hbm,
+    cot_hbm,
+    nei_hbm,
+    wq_hbm,
+    wk_hbm,
+    wv_hbm,
     gh_ref,
     came_ref,
+    gq_ref,
+    go_ref,
+    gk_ref,
+    gv_ref,
     gpart,
     dpart,
     ghalf,
     gquarter,
     dhalf,
     dquarter,
-    wq,
+    tile,
+    near_tile,
+    dk_tile,
+    dv_tile,
     wk,
     wv,
     going,
     mine,
+    out_w,
+    out_near,
+    out_whole,
+    out_half,
+    in_w,
+    in_near,
+    in_whole,
+    in_half,
+    kv_w,
+    kv_near,
+    kv_whole,
+    kv_half,
     g_send,
     g_recv,
     d_send,
     d_recv,
+    out_send,
+    out_recv,
+    in_send,
+    in_recv,
+    kv_send,
+    kv_recv,
     swap_send,
     swap_recv,
     load_sem,
+    tile_sem,
+    near_sem,
 ):
     place = Place()
     x, y = place.x, place.y
-    tokens, width = dq_ref.shape
-    groups, cap, piece_rows, _ = going.shape
+    width = dq_ref.shape[1]
+    piece_rows = going.shape[2]
+    groups, cap = going.shape[:2]
+    rows, enc = dpart.shape[2:]
     weights = [
-        pltpu.make_async_copy(wq_ref, wq, load_sem.at[0]),
-        pltpu.make_async_copy(wk_ref, wk, load_sem.at[1]),
-        pltpu.make_async_copy(wv_ref, wv, load_sem.at[2]),
+        pltpu.make_async_copy(wk_hbm, wk, load_sem.at[1]),
+        pltpu.make_async_copy(wv_hbm, wv, load_sem.at[2]),
     ]
     for copy in weights:
         copy.start()
     greet(place)
+    wide_sum = Reduce(place, gpart, ghalf, gquarter, g_send, g_recv)
+    near_sum = Reduce(place, dpart, dhalf, dquarter, d_send, d_recv)
+    out_ring = Ring(out_w, out_near, out_whole, out_half, out_send, out_recv)
+    in_ring = Ring(in_w, in_near, in_whole, in_half, in_send, in_recv)
+    kv_ring = Ring(kv_w, kv_near, kv_whole, kv_half, kv_send, kv_recv)
+
+    def dot(a, b, ca, cb):
+        return lax.dot_general(
+            a, b, (((ca,), (cb,)), ((), ())), precision=MID, preferred_element_type=jnp.float32
+        )
+
+    def g_load(i, slot):
+        bx = wrap(x + shift_of(i // 2))
+        start = pl.multiple_of((bx * SIDE + 2 * lax.rem(i, 2)) * width, width)
+        return [pltpu.make_async_copy(wq_hbm.at[pl.ds(start, 2 * width)], tile.at[slot], tile_sem.at[slot])]
+
+    def g_work(i, slot):
+        bx, by = wrap(x + shift_of(i // 2)), 2 * lax.rem(i, 2)
+        both = dot(dq_ref[...], tile[slot], 1, 1)
+        gpart[bx, by] = both[:, :width]
+        gpart[bx, by + 1] = both[:, width:]
+
+        @pl.when(lax.rem(i, 2) == 1)
+        def _():
+            wide_sum.begin(0, shift_of(i // 2) + 1)
+
+        @pl.when(i == 1)
+        def _():
+            for turn in TURNS:
+                wide_sum.begin(1, turn)
+
+    stream(2 * SIDE, g_load, g_work)
+
+    def weight_grad(source, right_ref, ring):
+        def at(i):
+            j = i // 2
+            core = ring.core + (1 - j // SIDE) * (1 - 2 * ring.core)
+            return wrap(ring.z + shift_of(lax.rem(j, SIDE))) * 2 + core, lax.rem(i, 2)
+
+        def load(i, slot):
+            g, u = at(i)
+            m = 2 * g + u
+            return [
+                pltpu.make_async_copy(
+                    source.at[m // SIDE, lax.rem(m, SIDE)], tile.at[slot], tile_sem.at[slot]
+                )
+            ]
+
+        def work(i, slot):
+            g, u = at(i)
+            part = pl.ds(pl.multiple_of(u * width, width), width)
+            ring.w[g, part, :] = dot(tile[slot], right_ref[...], 0, 0)
+
+            @pl.when((u == 1) & (i < 2 * SIDE))
+            def _():
+                ring.swap(i // 2, shift_of(i // 2)).start()
+
+        stream(4 * SIDE, load, work)
+
+    weight_grad(cot_hbm, att_ref, out_ring)
+    for turn in TURNS:
+        for half in (0, 1):
+            wide_sum.middle(half, turn)
+    out_ring.begin()
     for copy in weights:
         copy.wait()
-    wide_sum = Reduce(place, gpart, ghalf, gquarter, g_send, g_recv)
-    near_sum = Reduce(place, dpart, dhalf, dquarter, d_send, d_recv)
-    transposed = (((1,), (1,)), ((), ()))
-
-    def hidden_part(half, block):
-        bx, by = place.block(half, *block)
-        rows = pl.ds(half * (tokens // 2), tokens // 2)
-        part = pl.ds(pl.multiple_of((bx * SIDE + by) * width, width), width)
-        gpart[bx, by, rows, :] = lax.dot_general(
-            dq_ref[rows, :], wq[part, :], transposed, precision=HIGH,
-            preferred_element_type=jnp.float32,
-        )
-
-    def order(step):
-        return 3 - step + 3 * (step // 2) - 2 * (step // 3)
-
-    def g_first(step, carry):
-        turn = order(step)
-        for half in (0, 1):
-            hidden_part(half, wide_sum.at(half, turn, 2))
-            wide_sum.begin(half, turn)
-        return carry
-
-    lax.fori_loop(0, SIDE, g_first, 0)
-
-    def d_all(step, carry):
-        bx, by = step // SIDE, lax.rem(step, SIDE)
-        dpart[bx, by] = lax.dot_general(
-            dk_ref[bx, by], wk[...], transposed, precision=HIGH,
-            preferred_element_type=jnp.float32,
-        ) + lax.dot_general(
-            dv_ref[bx, by], wv[...], transposed, precision=HIGH,
-            preferred_element_type=jnp.float32,
-        )
-        return carry
-
-    lax.fori_loop(0, SIDE * SIDE, d_all, 0)
+    kv_w[...] = jnp.zeros_like(kv_w)
+
+    def d_load(i, slot):
+        at = (i // 2, pl.ds(2 * lax.rem(i, 2), 2))
+        return [
+            pltpu.make_async_copy(source.at[at], buf.at[slot], near_sem.at[which * 2 + slot])
+            for which, (source, buf) in enumerate(
+                ((nei_hbm, near_tile), (dk_hbm, dk_tile), (dv_hbm, dv_tile))
+            )
+        ]
+
+    def d_work(i, slot):
+        bx, by = i // 2, 2 * lax.rem(i, 2)
+        dk = dk_tile[slot].reshape(2 * rows, width)
+        dv = dv_tile[slot].reshape(2 * rows, width)
+        near = near_tile[slot].reshape(2 * rows, enc)
+        dpart[bx, pl.ds(by, 2)] = (dot(dk, wk[...], 1, 1) + dot(dv, wv[...], 1, 1)).reshape(
+            2, rows, enc
+        )
+        pair = dot(near, jnp.concatenate([dk, dv], axis=1), 0, 0)
+        kv_w[...] += pair.reshape(kv_w.shape)
+
+    stream(2 * SIDE, d_load, d_work)
     for turn in TURNS:
         for half in (0, 1):
             near_sum.begin(half, turn)
-
-    def g_second(step, carry):
-        turn = order(step)
-        for half in (0, 1):
-            for shift in (1, -1):
-                hidden_part(half, wide_sum.at(half, turn, shift))
-            wide_sum.middle(half, turn)
-        return carry
-
-    lax.fori_loop(0, SIDE, g_second, 0)
+    for turn, shift in enumerate((2, 1, 3, 0)):
+        kv_ring.swap(turn, shift).start()
+    out_ring.middle()
+    for half in (0, 1):
+        wide_sum.finish(half, 3)
+        wide_sum.begin(half, 0)
+    for half in (0, 1):
+        for turn in (2, 4, 1):
+            wide_sum.finish(half, turn)
+    weight_grad(hid_hbm, dq_ref, in_ring)
+    for half in (0, 1):
+        wide_sum.middle(half, 0)
     for turn in TURNS:
         for half in (0, 1):
             near_sum.middle(half, turn)
-    def g_third(step, carry):
-        turn = order(step)
-        for half in (0, 1):
-            hidden_part(half, wide_sum.at(half, turn, 0))
-        return carry
-
-    lax.fori_loop(0, SIDE, g_third, 0)
-    for target in (wide_sum, near_sum):
-        for half in (0, 1):
-            target.finish(half, 3)
-            target.begin(half, 0)
-        for half in (0, 1):
-            for turn in (2, 4):
-                target.finish(half, turn)
-            target.middle(half, 0)
-        for half in (0, 1):
-            target.finish(half, 1)
+    kv_ring.begin()
+    in_ring.begin()
     for half in (0, 1):
+        near_sum.finish(half, 3)
+        near_sum.begin(half, 0)
+    for half in (0, 1):
+        for turn in (2, 4):
+            near_sum.finish(half, turn)
+        near_sum.middle(half, 0)
+    kv_ring.middle()
+    in_ring.middle()
+    go_ref[...] = out_ring.finish()
+    for half in (0, 1):
+        wide_sum.finish(half, 0)
+    gh_ref[...] = gpart[x, y]
+    for half in (0, 1):
+        near_sum.finish(half, 1)
         near_sum.finish(half, 0)
     for i in range(groups * cap):
         mine[i] = dpart[x, y, pl.ds(i * piece_rows, piece_rows), :]
     for slot in range(groups * cap):
         going[slot // cap, slot % cap] = mine[inst_ref[slot]]
     swaps = exchange(going, came_ref, swap_send, swap_recv, load_sem.at[3])
-    for half in (0, 1):
-        wide_sum.finish(half, 0)
-    gh_ref[...] = gpart[x, y]
+    pair = kv_ring.finish()
+    gk_ref[...] = pair[:, :width]
+    gv_ref[...] = pair[:, width:]
+    gq_ref[...] = in_ring.finish()
     for copy in swaps:
         copy.wait()
-    wide_sum.drain()
-    near_sum.drain()
-
-
-def attention_kernel(q_ref, da_ref, keys_ref, values_ref, att_ref, dq_ref, dk_ref, dv_ref):
-    scale = HEAD_DIM ** (-0.5)
-    heads = q_ref.shape[1] // HEAD_DIM
-    spans = q_ref.shape[0] // SPAN
-    few = keys_ref.shape[2] // spans
-    near = SIDE * SIDE * few
-
-    def dot(a, b, ca, cb):
-        return lax.dot_general(
-            a, b, (((ca,), (cb,)), ((), ())), precision=HIGH, preferred_element_type=jnp.float32
-        )
-
-    def span(c, carry):
-        rows = pl.ds(pl.multiple_of(c * SPAN, SPAN), SPAN)
-        pieces = pl.ds(pl.multiple_of(c * few, few), few)
-        for head in range(heads):
-            cols = pl.ds(head * HEAD_DIM, HEAD_DIM)
-            q = q_ref[rows, cols]
-            da = da_ref[rows, cols]
-            k = keys_ref[:, :, pieces, cols].reshape(near, HEAD_DIM)
-            v = values_ref[:, :, pieces, cols].reshape(near, HEAD_DIM)
-            scores = dot(q, k, 1, 1) * scale
-            top = jnp.max(scores, axis=-1, keepdims=True)
-            e = jnp.exp(scores - top)
-            probs = e / jnp.sum(e, axis=-1, keepdims=True)
-            att_ref[rows, cols] = dot(probs, v, 1, 0)
-            dp = dot(da, v, 1, 1)
-            ds = probs * (dp - jnp.sum(dp * probs, axis=-1, keepdims=True)) * scale
-            dq_ref[rows, cols] = dot(ds, k, 1, 0)
-            shape = (SIDE, SIDE, few, HEAD_DIM)
-            dk_ref[:, :, pieces, cols] = dot(ds, q, 0, 0).reshape(shape)
-            dv_ref[:, :, pieces, cols] = dot(probs, da, 0, 0).reshape(shape)
-        return carry
-
-    lax.fori_loop(0, spans, span, 0)
+    for target in (wide_sum, near_sum, out_ring, in_ring, kv_ring):
+        target.drain()
 
 
 def vmem(n):
@@ -588,6 +773,10 @@
         f32(SIDE, SIDE, rows, width),
     ]
     scratch = [
+        pltpu.VMEM((tokens, width), jnp.float32),
+        pltpu.VMEM((tokens, width), jnp.float32),
+        pltpu.VMEM((SIDE, SIDE, rows, width), jnp.float32),
+        pltpu.VMEM((SIDE, SIDE, rows, width), jnp.float32),
         pltpu.VMEM((SIDE, SIDE, tokens, width), jnp.float32),
         pltpu.VMEM((SIDE, SIDE, tokens, width), jnp.float32),
         pltpu.VMEM((SIDE, SIDE, rows, enc), jnp.float32),
@@ -610,7 +799,7 @@
     )(hidden, cotangent, outgoing, slots, wq, wo, wk, wv)
 
 
-def reduce_call(dq, dk, dv, inst_of, wq, wk, wv, groups):
+def reduce_call(dq, att, inst_of, dk, dv, hid, cot, nei, wq, wk, wv, groups):
     tokens, width = dq.shape
     rows = dk.shape[2]
     enc = wk.shape[0]
@@ -619,6 +808,14 @@
     piece_rows = rows // slots
     dma = pltpu.SemaphoreType.DMA
     going = (groups, cap, piece_rows, enc)
+    out_rows, enc_rows = wq.shape[0] // groups, enc // groups
+
+    def ring(rows, cols):
+        return [
+            pltpu.VMEM((n, r, cols), jnp.float32)
+            for n, r in ((groups, rows), (groups // 2, rows), (2, rows), (2, rows // 2))
+        ]
+
     scratch = [
         pltpu.VMEM((SIDE, SIDE, tokens, width), jnp.float32),
         pltpu.VMEM((SIDE, SIDE, rows, enc), jnp.float32),
@@ -626,24 +823,36 @@
         pltpu.VMEM((20, tokens // 4, width), jnp.float32),
         pltpu.VMEM((20, rows // 2, enc), jnp.float32),
         pltpu.VMEM((20, rows // 4, enc), jnp.float32),
-        pltpu.VMEM(wq.shape, jnp.float32),
+        pltpu.VMEM((2, 2 * width, width), jnp.float32),
+        pltpu.VMEM((2, 2, rows, enc), jnp.float32),
+        pltpu.VMEM((2, 2, rows, width), jnp.float32),
+        pltpu.VMEM((2, 2, rows, width), jnp.float32),
         pltpu.VMEM(wk.shape, jnp.float32),
         pltpu.VMEM(wv.shape, jnp.float32),
         pltpu.VMEM(going, jnp.float32),
         pltpu.VMEM((slots, piece_rows, enc), jnp.float32),
     ]
-    scratch += [dma((40,))] * 4 + [dma((groups,))] * 2 + [dma((4,))]
+    scratch += ring(out_rows, width) + ring(out_rows, width) + ring(enc_rows, 2 * width)
+    scratch += [dma((40,))] * 4 + [dma((8,))] * 6 + [dma((groups,))] * 2
+    scratch += [dma((4,)), dma((2,)), dma((6,))]
     return pl.pallas_call(
         reduce_kernel,
-        out_shape=[f32(tokens, width), f32(*going)],
-        in_specs=vmem(3) + smem(1) + hbm(3),
-        out_specs=vmem(2),
+        out_shape=[
+            f32(tokens, width),
+            f32(*going),
+            f32(out_rows, width),
+            f32(out_rows, width),
+            f32(enc_rows, width),
+            f32(enc_rows, width),
+        ],
+        in_specs=vmem(2) + smem(1) + hbm(8),
+        out_specs=vmem(6),
         scratch_shapes=scratch,
         compiler_params=pltpu.CompilerParams(
-            collective_id=1, has_side_effects=True, vmem_limit_bytes=VMEM_LIMIT
+            collective_id=1, has_side_effects=True, vmem_limit_bytes=REDUCE_LIMIT
         ),
         cost_estimate=pl.CostEstimate(flops=50_000_000_000, bytes_accessed=60_000_000, transcendentals=0),
-    )(dq, dk, dv, inst_of, wq, wk, wv)
+    )(dq, att, inst_of, dk, dv, hid, cot, nei, wq, wk, wv)
 
 
 def body(
@@ -677,36 +886,11 @@
     numbers = jnp.arange(inst, dtype=jnp.int32)
     inst_of = jnp.sum(jnp.where(mine[None, :] == numbers[:, None], numbers[None, :], 0), axis=1)
 
-    hid, cot, nei, query, d_att, keys, values = gather_call(
+    hid, cot, nei, attended, d_query, d_keys, d_values = gather_call(
         hidden_states, out_cotangent, outgoing, mine, w_query, w_out, w_key, w_value
     )
-    rows, enc = nei.shape[2:]
-    attended, d_query, d_keys, d_values = pl.pallas_call(
-        attention_kernel,
-        out_shape=[f32(*t.shape) for t in (query, query, keys, values)],
-        in_specs=vmem(4),
-        out_specs=vmem(4),
-        compiler_params=pltpu.CompilerParams(vmem_limit_bytes=40 * 1024 * 1024),
-    )(query, d_att, keys, values)
-
-    def over_tokens(a, b):
-        out = jnp.einsum("mtf,td->mfd", a.reshape(SIDE * SIDE, tokens, width), b, precision=MID)
-        return lax.psum_scatter(
-            out.reshape(-1, width), "wide", scatter_dimension=0, tiled=True
-        )
-
-    def over_rows(b):
-        out = lax.dot_general(
-            nei.reshape(-1, enc), b.reshape(-1, width), (((0,), (0,)), ((), ())), precision=MID
-        )
-        return lax.psum_scatter(out, "wide", scatter_dimension=0, tiled=True)
-
-    grad_out = over_tokens(cot, attended)
-    grad_query = over_tokens(hid, d_query)
-    grad_key = over_rows(d_keys)
-    grad_value = over_rows(d_values)
-    grad_hidden, arrived = reduce_call(
-        d_query, d_keys, d_values, inst_of, w_query, w_key, w_value, groups
+    grad_hidden, arrived, grad_query, grad_out, grad_key, grad_value = reduce_call(
+        d_query, attended, inst_of, d_keys, d_values, hid, cot, nei, w_query, w_key, w_value, groups
     )
     grad_table = jnp.einsum("brs,brxe->sxe", place, arrived, precision=HIGH)
     return (grad_hidden, grad_query, grad_key, grad_value, grad_out, grad_table)

time: 378 us -> 295 us (0.78)
  matrix products: 39.5 us -> 3.45 us
  local copies, waits for them, and re-layouts: 29.6 us -> 8.69 us
  between operations: 13.9 us -> 0.73 us
  Pallas kernels: 292 us -> 280 us
    dot_general x4 -> x0, matrix products: 36.1 us -> none  [the longest x2 18.4 us: over_rows(): lax.dot_general(nei.reshape(-1, enc), b.reshape(-1, width), (((0,), (0,))...]
    pallas_call x2 -> x1, Pallas kernels: 144 us -> 122 us  [reduce_call(): pl.pallas_call(reduce_kernel, out_shape=[f32(tokens, width), f32(*going),...]
    reshape x2 -> x0, local copies, waits for them, and re-layouts: 18.7 us -> none  [over_tokens(): a.reshape(SIDE * SIDE, tokens, width)]
    pallas_call x1, Pallas kernels: 148 us -> 157 us  [gather_call(): pl.pallas_call(gather_kernel, out_shape=out_shape, in_specs=hbm(2) + vmem...]
    unnamed x18 -> x12, local copies, waits for them, and re-layouts: 9.38 us -> 7.65 us
  transfers between devices with their start and end apart: 4 -> 0, of which waited for: 0 -> 0; matrix products, arithmetic and copies ran while one was open for 13% -> 0% of each run, Pallas kernels for 32% -> 0%
where the time goes in v2:
time: 295 us; the launch traced here: 294 us
  Pallas kernels  280 us (95%)
  local copies, waits for them, and re-layouts  8.69 us (3%)
  matrix products  3.45 us (1%)
    pallas_call x1, Pallas kernels, gather_call(): pl.pallas_call(gather_kernel, out_shape=out_shape, in_specs=hbm(2) + vmem...  157 us
    pallas_call x1, Pallas kernels, reduce_call(): pl.pallas_call(reduce_kernel, out_shape=[f32(tokens, width), f32(*going),...  122 us
    unnamed x12, local copies, waits for them, and re-layouts  7.65 us

profile of v2, /device:TPU:1, one launch (start us, length us, event | category | flops | bytes accessed | tf_op | source)
XLA Modules:
  0.0 294.3 jit_solution(3924231617669176437)
XLA Ops:
  0.6 0.9 select_reduce_fusion
  1.5 0.1 copy.29
  1.6 0.1 reshape.111
  1.7 0.3 convert_reduce_fusion
  2.1 0.0 copy-start.2
  2.1 0.6 select_reduce_fusion.1.inst_ref
  2.7 0.2 fusion.4
  2.9 1.6 fusion
  4.4 0.9 copy.32.going_ref
  5.3 0.0 copy-done.2
  5.3 157.4 %shard_map.136 = (f32[4,4,512,256]{3,2,1,0:T(8,128)}, f32[4,4,512,256]{3,2,1,0:T(8,128)}, f32[4,4,128,896]{3,2,1,0:T(8,128)}, f32[512,256]{1,0:T(8,128)}, f32[51...) custom-call(f32[512,256]{1,0:T(8,128)} %hid_ref.1, f32[512,256]{1,0:T(8,128)} %cot_ref.1, ...), custom_call_target="tpu_custom_call" | custom-call | flops 24000000000 | bytes 60000000 | tf_op jit(solution)/shard_map/pallas_call | solution.py:789
  162.7 122.3 %shard_map.137 = (f32[512,256]{1,0:T(8,128)}, f32[8,2,8,896]{3,2,1,0:T(8,128)}, f32[512,256]{1,0:T(8,128)}, f32[512,256]{1,0:T(8,128)}, f32[112,256]{1,0:T(8,128)}, /*index=5*/f32[112,256]{1,0:T(8,128)}) custom-call(f32[512,256]{1,0:T(8,128)} %get-tuple-element.19.dq_ref, f32[512,256]{1,0:T(8,128)} %get-tuple-element.20.att_ref, ...), custom_call_target="tpu_custom_call" | custom-call | flops 49999998976 | bytes 60000000 | tf_op jit(solution)/shard_map/pallas_call | solution.py:838
  285.0 0.0 copy-start.1
  285.0 0.0 copy-start
  285.0 1.7 convolution_bitcast_fusion
  286.7 0.9 copy.35
  287.6 1.9 copy.57
  289.5 1.9 copy.58
  291.3 1.6 copy.59
  292.9 0.0 copy-done.1
  292.9 0.6 copy.60
  293.5 0.0 copy-done
  293.6 0.8 copy.61
  (5 shorter events, 0.1 us)
Async XLA Ops:
  2.1 3.2 %copy-start.2 = (s32[16]{0:T(128)}, s32[16]{0:T(128)S(1)}, u32[]{:S(2)}) copy-start(s32[16]{0:T(128)S(1)} %dynamic-slice_bitcast_fusion.slot_ref) | copy-start | bytes 196
  285.0 7.9 %copy-start.1 = (f32[112,256]{1,0:T(8,128)S(1)}, f32[112,256]{1,0:T(8,128)}, u32[]{:S(2)}) copy-start(f32[112,256]{1,0:T(8,128)} %get-tuple-element.61) | copy-start | bytes 344068
  285.0 8.6 %copy-start = (f32[512,256]{1,0:T(8,128)S(1)}, f32[512,256]{1,0:T(8,128)}, u32[]{:S(2)}) copy-start(f32[512,256]{1,0:T(8,128)} %get-tuple-element.62) | copy-start | bytes 1572868

commit v3 on v2

--- a/solution.py
+++ b/solution.py
@@ -192,7 +192,8 @@
 def gather_kernel(
     hid_ref,
     cot_ref,
-    going_ref,
+    table_ref,
+    pick_ref,
     slot_ref,
     wq_ref,
     wo_ref,
@@ -215,6 +216,7 @@
     wq,
     wo,
     wkv,
+    going,
     came,
     hid_send,
     hid_recv,
@@ -231,9 +233,8 @@
     x, y = place.x, place.y
     width = q_ref.shape[1]
     tokens = q_ref.shape[0]
-    piece_rows = going_ref.shape[2]
+    groups, cap, piece_rows, _ = came.shape
     inst = nei.shape[2] // piece_rows
-    cap = going_ref.shape[1]
     own = [
         pltpu.make_async_copy(hid_ref, hid.at[x, y], load_sem.at[0]),
         pltpu.make_async_copy(cot_ref, cot.at[x, y], load_sem.at[1]),
@@ -247,7 +248,6 @@
     for copy in own:
         copy.start()
     greet(place)
-    swaps = exchange(going_ref, came, swap_send, swap_recv, load_sem.at[6])
     for copy in own:
         copy.wait()
     gathers = [
@@ -259,6 +259,9 @@
         for gather in gathers[:2]:
             for half in (0, 1):
                 gather.begin(half, turn)
+    for i in range(groups * cap):
+        going[i // cap, i % cap] = table_ref[pick_ref[i]]
+    swaps = exchange(going, came, swap_send, swap_recv, load_sem.at[6])
     for copy in weights:
         copy.start()
     for copy in swaps:
@@ -635,11 +638,11 @@
 
     stream(2 * SIDE, g_load, g_work)
 
-    def weight_grad(source, right_ref, ring):
+    def weight_grad(source, right_ref, ring, other):
+        core = 1 - ring.core if other else ring.core
+
         def at(i):
-            j = i // 2
-            core = ring.core + (1 - j // SIDE) * (1 - 2 * ring.core)
-            return wrap(ring.z + shift_of(lax.rem(j, SIDE))) * 2 + core, lax.rem(i, 2)
+            return wrap(ring.z + shift_of(i // 2)) * 2 + core, lax.rem(i, 2)
 
         def load(i, slot):
             g, u = at(i)
@@ -654,94 +657,126 @@
             g, u = at(i)
             part = pl.ds(pl.multiple_of(u * width, width), width)
             ring.w[g, part, :] = dot(tile[slot], right_ref[...], 0, 0)
-
-            @pl.when((u == 1) & (i < 2 * SIDE))
-            def _():
-                ring.swap(i // 2, shift_of(i // 2)).start()
-
-        stream(4 * SIDE, load, work)
-
-    weight_grad(cot_hbm, att_ref, out_ring)
-    for turn in TURNS:
-        for half in (0, 1):
-            wide_sum.middle(half, turn)
-    out_ring.begin()
-    for copy in weights:
-        copy.wait()
-    kv_w[...] = jnp.zeros_like(kv_w)
-
-    def d_load(i, slot):
-        at = (i // 2, pl.ds(2 * lax.rem(i, 2), 2))
-        return [
-            pltpu.make_async_copy(source.at[at], buf.at[slot], near_sem.at[which * 2 + slot])
-            for which, (source, buf) in enumerate(
-                ((nei_hbm, near_tile), (dk_hbm, dk_tile), (dv_hbm, dv_tile))
-            )
-        ]
+            if other:
+
+                @pl.when(u == 1)
+                def _():
+                    ring.swap(i // 2, shift_of(i // 2)).start()
+
+        stream(2 * SIDE, load, work)
+
+    def near_load(sources):
+        def load(i, slot):
+            at = (i // 2, pl.ds(2 * lax.rem(i, 2), 2))
+            return [
+                pltpu.make_async_copy(source.at[at], buf.at[slot], near_sem.at[2 * which + slot])
+                for which, (source, buf) in enumerate(sources)
+            ]
+
+        return load
 
     def d_work(i, slot):
         bx, by = i // 2, 2 * lax.rem(i, 2)
         dk = dk_tile[slot].reshape(2 * rows, width)
         dv = dv_tile[slot].reshape(2 * rows, width)
-        near = near_tile[slot].reshape(2 * rows, enc)
         dpart[bx, pl.ds(by, 2)] = (dot(dk, wk[...], 1, 1) + dot(dv, wv[...], 1, 1)).reshape(
             2, rows, enc
         )
+
+    def neighbour_grad():
+        for copy in weights:
+            copy.wait()
+        stream(2 * SIDE, near_load(((dk_hbm, dk_tile), (dv_hbm, dv_tile))), d_work)
+        for turn in TURNS:
+            for half in (0, 1):
+                near_sum.begin(half, turn)
+
+    def kv_work(i, slot):
+        dk = dk_tile[slot].reshape(2 * rows, width)
+        dv = dv_tile[slot].reshape(2 * rows, width)
+        near = near_tile[slot].reshape(2 * rows, enc)
         pair = dot(near, jnp.concatenate([dk, dv], axis=1), 0, 0)
         kv_w[...] += pair.reshape(kv_w.shape)
 
-    stream(2 * SIDE, d_load, d_work)
-    for turn in TURNS:
+    def kv_grad():
+        kv_w[...] = jnp.zeros_like(kv_w)
+        stream(
+            2 * SIDE, near_load(((dk_hbm, dk_tile), (dv_hbm, dv_tile), (nei_hbm, near_tile))), kv_work
+        )
+        for turn, shift in enumerate((2, 1, 3, 0)):
+            kv_ring.swap(turn, shift).start()
+
+    def middle(target, turn):
         for half in (0, 1):
-            near_sum.begin(half, turn)
-    for turn, shift in enumerate((2, 1, 3, 0)):
-        kv_ring.swap(turn, shift).start()
+            target.middle(half, turn)
+
+    def finish(target, turn):
+        for half in (0, 1):
+            target.finish(half, turn)
+        if turn == 3:
+            for half in (0, 1):
+                target.begin(half, 0)
+
+    middle(wide_sum, 3)
+    weight_grad(hid_hbm, dq_ref, in_ring, True)
+    middle(wide_sum, 2)
+    neighbour_grad()
+    weight_grad(hid_hbm, dq_ref, in_ring, False)
+    middle(wide_sum, 4)
+    in_ring.begin()
+    weight_grad(cot_hbm, att_ref, out_ring, True)
+    middle(near_sum, 2)
+    weight_grad(cot_hbm, att_ref, out_ring, False)
+    middle(near_sum, 1)
+    middle(wide_sum, 1)
+    in_ring.middle()
+    out_ring.begin()
+    middle(near_sum, 3)
+    kv_grad()
+    middle(near_sum, 4)
+    finish(wide_sum, 4)
+    kv_ring.begin()
+    finish(near_sum, 2)
     out_ring.middle()
-    for half in (0, 1):
-        wide_sum.finish(half, 3)
-        wide_sum.begin(half, 0)
-    for half in (0, 1):
-        for turn in (2, 4, 1):
-            wide_sum.finish(half, turn)
-    weight_grad(hid_hbm, dq_ref, in_ring)
-    for half in (0, 1):
-        wide_sum.middle(half, 0)
-    for turn in TURNS:
-        for half in (0, 1):
-            near_sum.middle(half, turn)
-    kv_ring.begin()
-    in_ring.begin()
-    for half in (0, 1):
-        near_sum.finish(half, 3)
-        near_sum.begin(half, 0)
-    for half in (0, 1):
-        for turn in (2, 4):
-            near_sum.finish(half, turn)
-        near_sum.middle(half, 0)
+    finish(near_sum, 3)
+    gq_ref[...] = in_ring.finish()
+    finish(wide_sum, 3)
+    finish(near_sum, 4)
+    finish(wide_sum, 2)
+    middle(near_sum, 0)
     kv_ring.middle()
-    in_ring.middle()
+    finish(wide_sum, 1)
+    middle(wide_sum, 0)
+    finish(near_sum, 1)
     go_ref[...] = out_ring.finish()
-    for half in (0, 1):
-        wide_sum.finish(half, 0)
-    gh_ref[...] = gpart[x, y]
-    for half in (0, 1):
-        near_sum.finish(half, 1)
-        near_sum.finish(half, 0)
+    finish(near_sum, 0)
     for i in range(groups * cap):
         mine[i] = dpart[x, y, pl.ds(i * piece_rows, piece_rows), :]
     for slot in range(groups * cap):
         going[slot // cap, slot % cap] = mine[inst_ref[slot]]
     swaps = exchange(going, came_ref, swap_send, swap_recv, load_sem.at[3])
+    finish(wide_sum, 0)
+    gh_ref[...] = gpart[x, y]
     pair = kv_ring.finish()
     gk_ref[...] = pair[:, :width]
     gv_ref[...] = pair[:, width:]
-    gq_ref[...] = in_ring.finish()
     for copy in swaps:
         copy.wait()
     for target in (wide_sum, near_sum, out_ring, in_ring, kv_ring):
         target.drain()
 
 
+def result_kernel(slot_ref, came_ref, *refs):
+    sources, table_ref, results = refs[:5], refs[5], refs[6:]
+    for source, result in zip(sources, results):
+        result[...] = source[...]
+    table_ref[...] = jnp.zeros_like(table_ref)
+    cap = came_ref.shape[1]
+    for i in range(came_ref.shape[0] * cap):
+        slot = slot_ref[i]
+        table_ref[slot] += came_ref[i // cap, i % cap]
+
+
 def vmem(n):
     return [pl.BlockSpec(memory_space=pltpu.VMEM)] * n
 
@@ -758,9 +793,10 @@
     return jax.ShapeDtypeStruct(shape, jnp.float32)
 
 
-def gather_call(hidden, cotangent, outgoing, slots, wq, wo, wk, wv):
+def gather_call(hidden, cotangent, table, picks, slots, wq, wo, wk, wv, groups):
     tokens, width = hidden.shape
-    groups, cap, piece_rows, enc = outgoing.shape
+    _, piece_rows, enc = table.shape
+    going = (groups, slots.shape[0] // groups, piece_rows, enc)
     rows = slots.shape[0] * piece_rows
     dma = pltpu.SemaphoreType.DMA
     out_shape = [
@@ -783,20 +819,21 @@
         pltpu.VMEM(wq.shape, jnp.float32),
         pltpu.VMEM(wo.shape, jnp.float32),
         pltpu.VMEM((enc, 2 * width), jnp.float32),
-        pltpu.VMEM(outgoing.shape, jnp.float32),
+        pltpu.VMEM(going, jnp.float32),
+        pltpu.VMEM(going, jnp.float32),
     ]
     scratch += [dma((40,))] * 6 + [dma((groups,))] * 2 + [dma((8,)), dma((30,))]
     return pl.pallas_call(
         gather_kernel,
         out_shape=out_shape,
-        in_specs=hbm(2) + vmem(1) + smem(1) + hbm(4),
+        in_specs=hbm(2) + vmem(1) + smem(2) + hbm(4),
         out_specs=hbm(3) + vmem(4),
         scratch_shapes=scratch,
         compiler_params=pltpu.CompilerParams(
             collective_id=0, has_side_effects=True, vmem_limit_bytes=VMEM_LIMIT
         ),
         cost_estimate=pl.CostEstimate(flops=24_000_000_000, bytes_accessed=60_000_000, transcendentals=0),
-    )(hidden, cotangent, outgoing, slots, wq, wo, wk, wv)
+    )(hidden, cotangent, table, picks, slots, wq, wo, wk, wv)
 
 
 def reduce_call(dq, att, inst_of, dk, dv, hid, cot, nei, wq, wk, wv, groups):
@@ -874,26 +911,26 @@
     same = owners[:, :, None] == owners[:, None, :]
     rank = jnp.sum((same & earlier[None, :, :]).astype(jnp.int32), axis=-1)
     slot_range = jnp.arange(capacity, dtype=jnp.int32)
-    pick = ((owners[:, None, :] == group) & (rank[:, None, :] == slot_range[None, :, None])).astype(
-        jnp.float32
-    )
-    one_local = (
-        local_slot[:, :, None] == jnp.arange(stored, dtype=jnp.int32)[None, None, :]
-    ).astype(jnp.float32)
-    place = jnp.einsum("bri,bis->brs", pick, one_local, precision=HIGH)
-    outgoing = jnp.einsum("brs,sxe->brxe", place, enc_table, precision=HIGH)
+    pick = (owners[:, None, :] == group) & (rank[:, None, :] == slot_range[None, :, None])
+    picks = jnp.sum(jnp.where(pick, local_slot[:, None, :], 0), axis=-1).reshape(-1)
     mine = lax.dynamic_index_in_dim(owners * capacity + rank, group, 0, keepdims=False)
     numbers = jnp.arange(inst, dtype=jnp.int32)
     inst_of = jnp.sum(jnp.where(mine[None, :] == numbers[:, None], numbers[None, :], 0), axis=1)
 
     hid, cot, nei, attended, d_query, d_keys, d_values = gather_call(
-        hidden_states, out_cotangent, outgoing, mine, w_query, w_out, w_key, w_value
+        hidden_states, out_cotangent, enc_table, picks, mine, w_query, w_out, w_key, w_value, groups
     )
     grad_hidden, arrived, grad_query, grad_out, grad_key, grad_value = reduce_call(
         d_query, attended, inst_of, d_keys, d_values, hid, cot, nei, w_query, w_key, w_value, groups
     )
-    grad_table = jnp.einsum("brs,brxe->sxe", place, arrived, precision=HIGH)
-    return (grad_hidden, grad_query, grad_key, grad_value, grad_out, grad_table)
+    sums = (grad_hidden, grad_query, grad_key, grad_value, grad_out)
+    grad_table, *sums = pl.pallas_call(
+        result_kernel,
+        out_shape=[f32(*enc_table.shape)] + [f32(*t.shape) for t in sums],
+        in_specs=smem(1) + vmem(6),
+        out_specs=vmem(6),
+    )(picks, arrived, *sums)
+    return (*sums, grad_table)
 
 
 def solution(mesh):

time: 295 us -> 262 us (0.89)
  Pallas kernels: 280 us -> 257 us
  local copies, waits for them, and re-layouts: 8.69 us -> 0.93 us
  matrix products: 3.45 us -> 0 us
    pallas_call x1, Pallas kernels: 122 us -> 97.2 us  [reduce_call(): pl.pallas_call(reduce_kernel, out_shape=[f32(tokens, width), f32(*going),...]
    unnamed x12 -> x2, local copies, waits for them, and re-layouts: 7.65 us -> 0.01 us
    dot_general x3 -> x0, matrix products: 3.45 us -> none  [the longest x1 1.7 us: body(): grad_table = jnp.einsum('brs,brxe->sxe', place, arrived, precision=HIGH)]
    pallas_call x0 -> x1, Pallas kernels: none -> 3.01 us  [body(): pl.pallas_call(result_kernel, out_shape=[f32(*enc_table.shape)] + [f32(*t...]
where the time goes in v3:
time: 262 us; the launch traced here: 261 us
  Pallas kernels  257 us (98%)
    pallas_call x1, Pallas kernels, gather_call(): pl.pallas_call(gather_kernel, out_shape=out_shape, in_specs=hbm(2) + vmem...  157 us
    pallas_call x1, Pallas kernels, reduce_call(): pl.pallas_call(reduce_kernel, out_shape=[f32(tokens, width), f32(*going),...  97.2 us

profile of v3, /device:TPU:1, one launch (start us, length us, event | category | flops | bytes accessed | tf_op | source)
XLA Modules:
  0.0 261.1 jit_solution(1349134056753365977)
XLA Ops:
  0.6 0.9 select_reduce_fusion
  1.5 0.1 copy.17
  1.6 0.1 reshape.114
  1.7 0.3 convert_reduce_fusion
  2.0 0.1 select_reduce_fusion.2
  2.2 0.0 copy-start
  2.2 0.6 select_reduce_fusion.1.inst_ref
  2.8 0.1 copy.18
  2.9 0.7 reshape.115.pick_ref.slot_ref
  3.6 0.0 copy-done
  3.6 157.3 %shard_map.136 = (f32[4,4,512,256]{3,2,1,0:T(8,128)}, f32[4,4,512,256]{3,2,1,0:T(8,128)}, f32[4,4,128,896]{3,2,1,0:T(8,128)}, f32[512,256]{1,0:T(8,128)}, f32[51...) custom-call(f32[512,256]{1,0:T(8,128)} %hid_ref.1, f32[512,256]{1,0:T(8,128)} %cot_ref.1, ...), custom_call_target="tpu_custom_call" | custom-call | flops 24000000000 | bytes 60000000 | tf_op jit(solution)/shard_map/pallas_call | solution.py:826
  160.9 97.2 %shard_map.137 = (f32[512,256]{1,0:T(8,128)}, f32[8,2,8,896]{3,2,1,0:T(8,128)}, f32[512,256]{1,0:T(8,128)}, f32[512,256]{1,0:T(8,128)}, f32[112,256]{1,0:T(8,128)}, /*index=5*/f32[112,256]{1,0:T(8,128)}) custom-call(f32[512,256]{1,0:T(8,128)} %get-tuple-element.25.dq_ref, f32[512,256]{1,0:T(8,128)} %get-tuple-element.26.att_ref, ...), custom_call_target="tpu_custom_call" | custom-call | flops 49999998976 | bytes 60000000 | tf_op jit(solution)/shard_map/pallas_call | solution.py:875
  258.1 3.0 %shard_map.138 = (f32[16,8,896]{2,1,0:T(8,128)}, f32[512,256]{1,0:T(8,128)}, f32[512,256]{1,0:T(8,128)}, f32[112,256]{1,0:T(8,128)}, f32[112,256]{1,0:T(8,128)}, /*index=5*/f32[512,256]{1,0:T(8,128)}) custom-call(s32[16]{0:T(128)} %reshape.115.pick_ref.slot_ref, f32[8,2,8,896]{3,2,1,0:T(8,128)} %get-tuple-element.32.came_ref, ...), custom_call_target="tpu_custom_call" | custom-call | tf_op jit(solution)/shard_map/pallas_call | solution.py:927
  (5 shorter events, 0.1 us)
Async XLA Ops:
  2.2 1.4 copy-start

commit v4 on v3

--- a/solution.py
+++ b/solution.py
@@ -28,6 +28,17 @@
         me = lax.axis_index("narrow")
         self.x = me // SIDE
         self.y = lax.rem(me, SIDE)
+        self.set = self.y // 2
+        self.member = lax.rem(self.y, 2)
+
+    def at(self, dx, dy):
+        return {"narrow": wrap(self.x + dx) * SIDE + wrap(self.y + dy)}
+
+    def mate(self):
+        return {"narrow": self.x * SIDE + self.y + 1 - 2 * self.member}
+
+    def partner(self):
+        return {"narrow": self.x * SIDE + SIDE - 1 - self.y}
 
     def own(self, half):
         return (self.x, self.y) if half == 0 else (self.y, self.x)
@@ -47,7 +58,153 @@
         return first, wrap(second + shift)
 
 
-def greet(place):
+class SetGather:
+    def __init__(self, place, buf, send, recv):
+        self.place, self.buf, self.send, self.recv = place, buf, send, recv
+        self.rows = buf.shape[2] // 2
+
+    def copy(self, slot, bx, member, start, rows, device):
+        piece = self.buf.at[bx, member, pl.ds(start, rows)]
+        return pltpu.make_async_remote_copy(
+            src_ref=piece,
+            dst_ref=piece,
+            send_sem=self.send.at[slot],
+            recv_sem=self.recv.at[slot],
+            device_id=device,
+            device_id_type=MESH,
+        )
+
+    def ring(self, which, kind, arriving=False):
+        place = self.place
+        member = place.member if which < 2 else 1 - place.member
+        ahead = (1, -1, 1, -1)[kind]
+        shift = (0, 0, -1, 1)[kind] - (ahead if arriving else 0)
+        start = self.rows * (which > 0) + (self.rows // 2 if kind == 3 else 0)
+        rows = self.rows if kind < 2 else self.rows // 2
+        return self.copy(
+            which * 4 + kind, wrap(place.x + shift), member, start, rows, place.at(ahead, 0)
+        )
+
+    def across(self, turn, arriving=False):
+        place = self.place
+        member = 1 - place.member if arriving else place.member
+        bx = wrap(place.x + turn)
+        start = self.rows if turn == 4 else 0
+        return self.copy(12 + turn, bx, member, start, self.rows, place.mate())
+
+    def begin(self, which):
+        for kind in (0, 1):
+            self.ring(which, kind).start()
+
+    def forward(self, which):
+        for kind in (0, 1):
+            self.ring(which, kind, True).wait_recv()
+            self.ring(which, kind + 2).start()
+
+    def finish(self, which):
+        for kind in (2, 3):
+            self.ring(which, kind, True).wait_recv()
+
+    def drain(self):
+        for which in range(3):
+            for kind in range(4):
+                self.ring(which, kind).wait_send()
+        for turn in range(5):
+            self.across(turn).wait_send()
+
+
+class SetReduce:
+    def __init__(self, place, part, whole_in, quarter_in, across_in, send, recv):
+        self.place, self.part = place, part
+        self.whole_in, self.quarter_in, self.across_in = whole_in, quarter_in, across_in
+        self.send, self.recv = send, recv
+        self.rows = part.shape[2] // 2
+
+    def ring(self, which, kind):
+        place = self.place
+        member = place.member if which < 2 else 1 - place.member
+        ahead = (1, -1, 1, -1)[kind]
+        shift = (1, -1, 2, 2)[kind]
+        start = self.rows * (which > 0) + (self.rows // 2 if kind == 3 else 0)
+        rows = self.rows if kind < 2 else self.rows // 2
+        landing = self.whole_in if kind < 2 else self.quarter_in
+        slot = which * 4 + kind
+        return pltpu.make_async_remote_copy(
+            src_ref=self.part.at[wrap(place.x + shift), member, pl.ds(start, rows)],
+            dst_ref=landing.at[which * 2 + kind % 2],
+            send_sem=self.send.at[slot],
+            recv_sem=self.recv.at[slot],
+            device_id=place.at(ahead, 0),
+            device_id_type=MESH,
+        )
+
+    def across(self, turn):
+        place = self.place
+        start = self.rows if isinstance(turn, int) and turn == 4 else 0
+        return pltpu.make_async_remote_copy(
+            src_ref=self.part.at[
+                wrap(place.x + turn), 1 - place.member, pl.ds(start, self.rows)
+            ],
+            dst_ref=self.across_in.at[turn],
+            send_sem=self.send.at[12 + turn],
+            recv_sem=self.recv.at[12 + turn],
+            device_id=place.mate(),
+            device_id_type=MESH,
+        )
+
+    def take(self, turn):
+        self.across(turn).wait_recv()
+        rows = pl.ds(self.rows if turn == 4 else 0, self.rows)
+        self.part[wrap(self.place.x + turn), self.place.member, rows, :] += self.across_in[turn]
+
+    def begin(self, which):
+        for kind in (2, 3):
+            self.ring(which, kind).start()
+
+    def middle(self, which):
+        member = self.place.member if which < 2 else 1 - self.place.member
+        for kind in (2, 3):
+            self.ring(which, kind).wait_recv()
+            start = self.rows * (which > 0) + (self.rows // 2 if kind == 3 else 0)
+            bx = wrap(self.place.x + (1 if kind == 2 else -1))
+            self.part[bx, member, pl.ds(start, self.rows // 2), :] += self.quarter_in[
+                which * 2 + kind % 2
+            ]
+            self.ring(which, kind - 2).start()
+
+    def finish(self, which):
+        member = self.place.member if which < 2 else 1 - self.place.member
+        for kind in (0, 1):
+            self.ring(which, kind).wait_recv()
+        rows = pl.ds(self.rows * (which > 0), self.rows)
+        self.part[self.place.x, member, rows, :] += (
+            self.whole_in[which * 2] + self.whole_in[which * 2 + 1]
+        )
+
+    def drain(self):
+        for which in range(3):
+            for kind in range(4):
+                self.ring(which, kind).wait_send()
+        for turn in range(5):
+            self.across(turn).wait_send()
+
+
+def partner_copy(place, src, dst, send, recv, other_core=False):
+    device = place.partner()
+    if other_core:
+        group = lax.axis_index("wide")
+        device = {"wide": group + 1 - 2 * lax.rem(group, 2), **device}
+    return pltpu.make_async_remote_copy(
+        src_ref=src,
+        dst_ref=dst,
+        send_sem=send,
+        recv_sem=recv,
+        device_id=device,
+        device_id_type=MESH,
+    )
+
+
+def greet(place, diagonal=False):
     groups = lax.axis_size("wide")
     group = lax.axis_index("wide")
     barrier = pltpu.get_barrier_semaphore()
@@ -66,7 +223,14 @@
             device_id={"wide": lax.rem(group + step, groups)},
             device_id_type=MESH,
         )
-    pl.semaphore_wait(barrier, 4 + groups - 1)
+    if diagonal:
+        pl.semaphore_signal(
+            barrier,
+            inc=1,
+            device_id={"wide": group + 1 - 2 * lax.rem(group, 2), **place.partner()},
+            device_id_type=MESH,
+        )
+    pl.semaphore_wait(barrier, 4 + groups - 1 + int(diagonal))
 
 
 def exchange(out_ref, in_ref, send, recv, local):
@@ -189,6 +353,66 @@
     lax.fori_loop(0, spans, span, 0)
 
 
+class Spread:
+    def __init__(self, place, source, wide_w, send, recv):
+        self.place, self.source, self.w = place, source, wide_w
+        self.send, self.recv = send, recv
+        self.group = lax.axis_index("wide")
+        self.z, self.core = self.group // 2, lax.rem(self.group, 2)
+        self.width = source.shape[3]
+
+    def slot(self, group):
+        return self.w.at[group // 2, lax.rem(group, 2), :, pl.ds(self.width, self.width)]
+
+    def first(self):
+        block = self.source.at[self.z, 2 * (1 - self.place.set) + self.core]
+        return partner_copy(
+            self.place, block, self.slot(self.group), self.send.at[0], self.recv.at[0]
+        )
+
+    def to(self, index, group, target):
+        return pltpu.make_async_remote_copy(
+            src_ref=self.slot(group),
+            dst_ref=self.slot(group),
+            send_sem=self.send.at[index],
+            recv_sem=self.recv.at[index],
+            device_id={"wide": target},
+            device_id_type=MESH,
+        )
+
+    def along(self, step, arriving=False):
+        there = wrap(self.z + step) * 2 + self.core
+        back = wrap(self.z - step) * 2 + self.core
+        return self.to(step, back if arriving else self.group, there)
+
+    def beside(self, step, arriving=False):
+        core = 1 - self.core if arriving else self.core
+        other = self.z * 2 + 1 - self.core
+        return self.to(4 + step, wrap(self.z - step) * 2 + core, other)
+
+    def spread(self):
+        self.first().wait_recv()
+        for step in (1, 3, 2):
+            self.along(step).start()
+        self.beside(0).start()
+
+    def pass_on(self):
+        for step in (1, 3, 2):
+            self.along(step, True).wait_recv()
+            self.beside(step).start()
+
+    def finish(self):
+        for step in range(SIDE):
+            self.beside(step, True).wait_recv()
+
+    def drain(self):
+        self.first().wait_send()
+        for step in (1, 2, 3):
+            self.along(step).wait_send()
+        for step in range(SIDE):
+            self.beside(step).wait_send()
+
+
 def gather_kernel(
     hid_ref,
     cot_ref,
@@ -202,12 +426,15 @@
     hid_out,
     cot_out,
     nei_out,
+    wq_out,
     att_ref,
     dq_ref,
     dk_ref,
     dv_ref,
-    q_ref,
-    da_ref,
+    q_two,
+    da_two,
+    q_came,
+    da_came,
     keys_ref,
     values_ref,
     hid,
@@ -224,6 +451,12 @@
     cot_recv,
     nei_send,
     nei_recv,
+    wq_send,
+    wq_recv,
+    wo_send,
+    wo_recv,
+    pair_send,
+    pair_recv,
     swap_send,
     swap_recv,
     load_sem,
@@ -231,17 +464,18 @@
 ):
     place = Place()
     x, y = place.x, place.y
-    width = q_ref.shape[1]
-    tokens = q_ref.shape[0]
+    tokens, width = dq_ref.shape
     groups, cap, piece_rows, _ = came.shape
     inst = nei.shape[2] // piece_rows
     own = [
-        pltpu.make_async_copy(hid_ref, hid.at[x, y], load_sem.at[0]),
-        pltpu.make_async_copy(cot_ref, cot.at[x, y], load_sem.at[1]),
+        pltpu.make_async_copy(hid_ref, hid.at[x, place.member], load_sem.at[0]),
+        pltpu.make_async_copy(cot_ref, cot.at[x, place.member], load_sem.at[1]),
     ]
+    mine = pl.ds(2 * place.set, 2)
+    left = pl.ds(0, width)
     weights = [
-        pltpu.make_async_copy(wq_ref, wq, load_sem.at[2]),
-        pltpu.make_async_copy(wo_ref, wo, load_sem.at[3]),
+        pltpu.make_async_copy(wq_ref.at[:, mine], wq.at[:, :, :, left], load_sem.at[2]),
+        pltpu.make_async_copy(wo_ref.at[:, mine], wo.at[:, :, :, left], load_sem.at[3]),
         pltpu.make_async_copy(wk_ref, wkv.at[:, pl.ds(0, width)], load_sem.at[4]),
         pltpu.make_async_copy(wv_ref, wkv.at[:, pl.ds(width, width)], load_sem.at[5]),
     ]
@@ -250,63 +484,117 @@
     greet(place)
     for copy in own:
         copy.wait()
-    gathers = [
-        Gather(place, hid, hid_send, hid_recv),
-        Gather(place, cot, cot_send, cot_recv),
-        Gather(place, nei, nei_send, nei_recv),
+    pair = [
+        SetGather(place, hid, hid_send, hid_recv),
+        SetGather(place, cot, cot_send, cot_recv),
     ]
-    for turn in (0, 1):
-        for gather in gathers[:2]:
-            for half in (0, 1):
-                gather.begin(half, turn)
+    near = Gather(place, nei, nei_send, nei_recv)
+    spreads = [
+        Spread(place, wq_ref, wq, wq_send, wq_recv),
+        Spread(place, wo_ref, wo, wo_send, wo_recv),
+    ]
+    for gather in pair:
+        gather.begin(0)
+        gather.across(4).start()
+    for spread in spreads:
+        spread.first().start()
+    for gather in pair:
+        gather.across(0).start()
+        gather.begin(1)
     for i in range(groups * cap):
         going[i // cap, i % cap] = table_ref[pick_ref[i]]
     swaps = exchange(going, came, swap_send, swap_recv, load_sem.at[6])
     for copy in weights:
         copy.start()
+    for gather in pair:
+        gather.forward(0)
+        gather.across(1).start()
+        gather.across(3).start()
+        gather.across(4, True).wait_recv()
+        gather.begin(2)
+    for spread in spreads:
+        spread.spread()
     for copy in swaps:
         copy.wait()
     for i in range(inst):
         slot = slot_ref[i]
         nei[x, y, pl.ds(i * piece_rows, piece_rows), :] = came[slot // cap, lax.rem(slot, cap)]
-    for turn in (0, 1):
-        for half in (0, 1):
-            gathers[2].begin(half, turn)
-    for gather in gathers:
-        for half in (0, 1):
-            gather.forward(half, 0)
-        for half in (0, 1):
-            gather.begin(half, 2)
-            gather.begin(half, 4)
-    for gather in gathers:
-        for half in (0, 1):
-            gather.finish(half, 0)
-            gather.begin(half, 3)
+    for half in (0, 1):
+        near.begin(half, 0)
+    for gather in pair:
+        gather.finish(0)
+        gather.across(2).start()
+    for gather in pair:
+        gather.forward(1)
+    for half in (0, 1):
+        near.begin(half, 1)
+    for gather in pair:
+        gather.forward(2)
+    for spread in spreads:
+        spread.pass_on()
+    for half in (0, 1):
+        near.forward(half, 0)
+        near.begin(half, 2)
+        near.begin(half, 4)
     for copy in weights:
         copy.wait()
-    q_ref[...] = jnp.zeros_like(q_ref)
-    da_ref[...] = jnp.zeros_like(da_ref)
-
-    def turn_of(step):
-        return step + (step // 2) * (1 - 2 * lax.rem(step, 2)) + 1
-
-    def project(half, first):
+    for spread in spreads:
+        spread.finish()
+    keep_weights = pltpu.make_async_copy(wq, wq_out, load_sem.at[7])
+    keep_weights.start()
+    q_two[...] = jnp.zeros_like(q_two)
+    da_two[...] = jnp.zeros_like(da_two)
+
+    def project(half, bx):
         rows = pl.ds(half * (tokens // 2), tokens // 2)
 
-        def column(second, carry):
-            bx, by = place.block(half, first, second)
-            part = pl.ds(pl.multiple_of((bx * SIDE + by) * width, width), width)
-            q_ref[rows, :] += jnp.dot(
-                hid[bx, by, rows, :], wq[part, :], precision=HIGH,
+        def column(member, carry):
+            q_two[rows, :] += jnp.dot(
+                hid[bx, member, rows, :], wq[bx, member], precision=HIGH,
                 preferred_element_type=jnp.float32,
             )
-            da_ref[rows, :] += jnp.dot(
-                cot[bx, by, rows, :], wo[part, :], precision=MID,
+            da_two[rows, :] += jnp.dot(
+                cot[bx, member, rows, :], wo[bx, member], precision=MID,
                 preferred_element_type=jnp.float32,
             )
             return carry
 
-        lax.fori_loop(0, SIDE, column, 0)
+        lax.fori_loop(0, 2, column, 0)
+
+    for turn in (0, 1, 3, 2):
+        for gather in pair:
+            gather.across(turn, True).wait_recv()
+        project(0, wrap(x + turn))
+    for half in (0, 1):
+        near.finish(half, 0)
+        near.begin(half, 3)
+    for gather in pair:
+        gather.finish(1)
+        gather.finish(2)
+
+    def second_half(bx, carry):
+        project(1, bx)
+        return carry
+
+    lax.fori_loop(0, SIDE, second_half, 0)
+    right = pl.ds(width, width)
+    halves = [
+        partner_copy(place, q_two.at[:, right], q_came, pair_send.at[0], pair_recv.at[0]),
+        partner_copy(place, da_two.at[:, right], da_came, pair_send.at[1], pair_recv.at[1]),
+    ]
+    for copy in halves:
+        copy.start()
+    keeps = [
+        pltpu.make_async_copy(hid, hid_out, store_sem.at[0]),
+        pltpu.make_async_copy(cot, cot_out, store_sem.at[1]),
+    ]
+    for copy in keeps:
+        copy.start()
+
+    def turn_of(step):
+        return step + (step // 2) * (1 - 2 * lax.rem(step, 2)) + 1
+
+    def near_project(half, first):
         few = nei.shape[2] // 2
         rows = pl.ds(half * few, few)
         if half == 0:
@@ -325,21 +613,13 @@
             values_ref[:, first, rows, :] = both[:, :, width:]
 
     def keep(half, turn, first):
-        copies = []
-        for which, (buf, out) in enumerate(((hid, hid_out), (cot, cot_out), (nei, nei_out))):
-            rows = pl.ds(half * (buf.shape[2] // 2), buf.shape[2] // 2)
-            at = (first, slice(None), rows) if half == 0 else (slice(None), first, rows)
-            copies.append(
-                pltpu.make_async_copy(
-                    buf.at[at], out.at[at], store_sem.at[(which * 2 + half) * 5 + turn]
-                )
-            )
-        return copies
+        rows = pl.ds(half * (nei.shape[2] // 2), nei.shape[2] // 2)
+        at = (first, slice(None), rows) if half == 0 else (slice(None), first, rows)
+        return pltpu.make_async_copy(nei.at[at], nei_out.at[at], store_sem.at[2 + half * 5 + turn])
 
     def pass_on(turn):
-        for gather in gathers:
-            for half in (0, 1):
-                gather.forward(half, turn)
+        for half in (0, 1):
+            near.forward(half, turn)
 
     pass_on(turn_of(0))
 
@@ -350,24 +630,27 @@
 
         turn = turn_of(step)
         for half in (0, 1):
-            for gather in gathers:
-                gather.finish(half, turn)
+            near.finish(half, turn)
             first = wrap(place.own(half)[0] + turn - 1)
-            for copy in keep(half, turn, first):
-                copy.start()
-            project(half, first)
+            keep(half, turn, first).start()
+            near_project(half, first)
         return carry
 
     lax.fori_loop(0, SIDE, main, 0)
-    attend(q_ref, da_ref, keys_ref, values_ref, att_ref, dq_ref, dk_ref, dv_ref)
-    for gather in gathers:
-        gather.drain()
+    for copy in halves:
+        copy.wait()
+    q_came[...] += q_two[:, :width]
+    da_came[...] += da_two[:, :width]
+    attend(q_came, da_came, keys_ref, values_ref, att_ref, dq_ref, dk_ref, dv_ref)
+    for target in (*pair, near, *spreads):
+        target.drain()
+    keep_weights.wait()
+    for copy in keeps:
+        copy.wait()
 
     def stored(turn, carry):
         for half in (0, 1):
-            first = wrap(place.own(half)[0] + turn - 1)
-            for copy in keep(half, turn, first):
-                copy.wait()
+            keep(half, turn, wrap(place.own(half)[0] + turn - 1)).wait()
         return carry
 
     lax.fori_loop(1, SIDE + 1, stored, 0)
@@ -436,20 +719,17 @@
 
 
 class Ring:
-    def __init__(self, w, near_in, whole_in, half_in, send, recv):
+    def __init__(self, w, near_in, whole_in, half_in, send, recv, keep):
         group = lax.axis_index("wide")
-        self.z, self.core = group // 2, lax.rem(group, 2)
+        self.z, self.core, self.keep = group // 2, lax.rem(group, 2), keep
         self.w, self.near_in, self.whole_in, self.half_in = w, near_in, whole_in, half_in
         self.send, self.recv = send, recv
-        self.half_rows = w.shape[1] // 2
-
-    def index(self, shift):
-        return wrap(self.z + shift) * 2 + self.core
+        self.half_rows = w.shape[2] // 2
 
     def swap(self, turn, shift):
         to = wrap(self.z + shift)
         return pltpu.make_async_remote_copy(
-            src_ref=self.w.at[to * 2 + 1 - self.core],
+            src_ref=self.w.at[1 - self.keep, to],
             dst_ref=self.near_in.at[to],
             send_sem=self.send.at[4 + turn],
             recv_sem=self.recv.at[4 + turn],
@@ -459,22 +739,23 @@
 
     def take(self, turn, shift):
         self.swap(turn, shift).wait_recv()
-        self.w[self.index(shift)] += self.near_in[wrap(self.z + shift)]
+        to = wrap(self.z + shift)
+        self.w[self.keep, to] += self.near_in[to]
 
     def copy(self, kind):
         ahead = (1, -1, 1, -1)[kind]
         shift = (1, -1, 2, 2)[kind]
-        source = self.w.at[self.index(shift)]
+        source = self.w.at[self.keep, wrap(self.z + shift)]
         landing = self.whole_in
         if kind >= 2:
-            source = self.w.at[self.index(shift), pl.ds((kind - 2) * self.half_rows, self.half_rows)]
+            source = source.at[pl.ds((kind - 2) * self.half_rows, self.half_rows)]
             landing = self.half_in
         return pltpu.make_async_remote_copy(
             src_ref=source,
             dst_ref=landing.at[kind % 2],
             send_sem=self.send.at[kind],
             recv_sem=self.recv.at[kind],
-            device_id={"wide": self.index(ahead)},
+            device_id={"wide": wrap(self.z + ahead) * 2 + self.core},
             device_id_type=MESH,
         )
 
@@ -489,14 +770,14 @@
             self.take(kind - 1, shift)
             self.copy(kind).wait_recv()
             rows = pl.ds((kind - 2) * self.half_rows, self.half_rows)
-            self.w[self.index(shift), rows, :] += self.half_in[kind - 2]
+            self.w[self.keep, wrap(self.z + shift), rows, :] += self.half_in[kind - 2]
             self.copy(kind - 2).start()
         self.take(3, 0)
 
     def finish(self):
         for kind in (0, 1):
             self.copy(kind).wait_recv()
-        return self.w[self.index(0)] + self.whole_in[0] + self.whole_in[1]
+        return self.w[self.keep, self.z] + self.whole_in[0] + self.whole_in[1]
 
     def drain(self):
         for kind in range(4):
@@ -550,12 +831,16 @@
     go_ref,
     gk_ref,
     gv_ref,
+    dq_two,
+    att_two,
     gpart,
     dpart,
     ghalf,
     gquarter,
+    gacross,
     dhalf,
     dquarter,
+    w_tile,
     tile,
     near_tile,
     dk_tile,
@@ -576,6 +861,8 @@
     kv_near,
     kv_whole,
     kv_half,
+    gq_done,
+    go_done,
     g_send,
     g_recv,
     d_send,
@@ -586,6 +873,8 @@
     in_recv,
     kv_send,
     kv_recv,
+    pair_send,
+    pair_recv,
     swap_send,
     swap_recv,
     load_sem,
@@ -604,12 +893,23 @@
     ]
     for copy in weights:
         copy.start()
-    greet(place)
-    wide_sum = Reduce(place, gpart, ghalf, gquarter, g_send, g_recv)
+    right = pl.ds(width, width)
+    halves = [
+        partner_copy(place, dq_ref, dq_two.at[:, right], pair_send.at[0], pair_recv.at[0]),
+        partner_copy(place, att_ref, att_two.at[:, right], pair_send.at[1], pair_recv.at[1]),
+    ]
+    greet(place, True)
+    for copy in halves:
+        copy.start()
+    dq_two[:, :width] = dq_ref[...]
+    att_two[:, :width] = att_ref[...]
+    core = lax.rem(lax.axis_index("wide"), 2)
+    keep = lax.rem(core + place.set, 2)
+    wide_sum = SetReduce(place, gpart, ghalf, gquarter, gacross, g_send, g_recv)
     near_sum = Reduce(place, dpart, dhalf, dquarter, d_send, d_recv)
-    out_ring = Ring(out_w, out_near, out_whole, out_half, out_send, out_recv)
-    in_ring = Ring(in_w, in_near, in_whole, in_half, in_send, in_recv)
-    kv_ring = Ring(kv_w, kv_near, kv_whole, kv_half, kv_send, kv_recv)
+    out_ring = Ring(out_w, out_near, out_whole, out_half, out_send, out_recv, keep)
+    in_ring = Ring(in_w, in_near, in_whole, in_half, in_send, in_recv, keep)
+    kv_ring = Ring(kv_w, kv_near, kv_whole, kv_half, kv_send, kv_recv, core)
 
     def dot(a, b, ca, cb):
         return lax.dot_general(
@@ -617,53 +917,60 @@
         )
 
     def g_load(i, slot):
-        bx = wrap(x + shift_of(i // 2))
-        start = pl.multiple_of((bx * SIDE + 2 * lax.rem(i, 2)) * width, width)
-        return [pltpu.make_async_copy(wq_hbm.at[pl.ds(start, 2 * width)], tile.at[slot], tile_sem.at[slot])]
+        block = wq_hbm.at[wrap(x + shift_of(i // 2)), lax.rem(i, 2)]
+        return [pltpu.make_async_copy(block, w_tile.at[slot], tile_sem.at[slot])]
 
     def g_work(i, slot):
-        bx, by = wrap(x + shift_of(i // 2)), 2 * lax.rem(i, 2)
-        both = dot(dq_ref[...], tile[slot], 1, 1)
-        gpart[bx, by] = both[:, :width]
-        gpart[bx, by + 1] = both[:, width:]
+        shift = shift_of(i // 2)
+        gpart[wrap(x + shift), lax.rem(i, 2)] = dot(dq_two[...], w_tile[slot], 1, 1)
+
+        @pl.when(i == 1)
+        def _():
+            wide_sum.begin(1)
+            wide_sum.begin(2)
 
         @pl.when(lax.rem(i, 2) == 1)
         def _():
-            wide_sum.begin(0, shift_of(i // 2) + 1)
-
-        @pl.when(i == 1)
+            wide_sum.across(shift).start()
+
+    def weight_grad(source, two_ref, ring):
+        def load(i, slot):
+            block = source.at[wrap(ring.z + shift_of(i // 2)), lax.rem(i, 2)]
+            return [pltpu.make_async_copy(block, tile.at[slot], tile_sem.at[slot])]
+
+        def work(i, slot):
+            shift, u = shift_of(i // 2), lax.rem(i, 2)
+            part = pl.ds(pl.multiple_of(u * width, width), width)
+            both = dot(tile[slot], two_ref[...], 0, 0)
+            ring.w[0, wrap(ring.z + shift), part, :] = both[:, :width]
+            ring.w[1, wrap(ring.z + shift), part, :] = both[:, width:]
+
+            @pl.when(u == 1)
+            def _():
+                ring.swap(i // 2, shift).start()
+
+        stream(2 * SIDE, load, work)
+
+    def handed(which, done, out_ref):
+        return partner_copy(
+            place, done, out_ref, pair_send.at[2 + which], pair_recv.at[2 + which], True
+        )
+
+    def deliver(which, ring, done, out_ref):
+        done[...] = ring.finish()
+
+        @pl.when(keep == 0)
         def _():
-            for turn in TURNS:
-                wide_sum.begin(1, turn)
-
-    stream(2 * SIDE, g_load, g_work)
-
-    def weight_grad(source, right_ref, ring, other):
-        core = 1 - ring.core if other else ring.core
-
-        def at(i):
-            return wrap(ring.z + shift_of(i // 2)) * 2 + core, lax.rem(i, 2)
-
-        def load(i, slot):
-            g, u = at(i)
-            m = 2 * g + u
-            return [
-                pltpu.make_async_copy(
-                    source.at[m // SIDE, lax.rem(m, SIDE)], tile.at[slot], tile_sem.at[slot]
-                )
-            ]
-
-        def work(i, slot):
-            g, u = at(i)
-            part = pl.ds(pl.multiple_of(u * width, width), width)
-            ring.w[g, part, :] = dot(tile[slot], right_ref[...], 0, 0)
-            if other:
-
-                @pl.when(u == 1)
-                def _():
-                    ring.swap(i // 2, shift_of(i // 2)).start()
-
-        stream(2 * SIDE, load, work)
+            out_ref[...] = done[...]
+
+        @pl.when(keep == 1)
+        def _():
+            handed(which, done, out_ref).start()
+
+    def delivered(which, done, out_ref):
+        @pl.when(keep == 1)
+        def _():
+            handed(which, done, out_ref).wait()
 
     def near_load(sources):
         def load(i, slot):
@@ -696,7 +1003,9 @@
         dv = dv_tile[slot].reshape(2 * rows, width)
         near = near_tile[slot].reshape(2 * rows, enc)
         pair = dot(near, jnp.concatenate([dk, dv], axis=1), 0, 0)
-        kv_w[...] += pair.reshape(kv_w.shape)
+        for group in range(groups):
+            share = pair[group * kv_w.shape[2] : (group + 1) * kv_w.shape[2]]
+            kv_w[group % 2, group // 2] += share
 
     def kv_grad():
         kv_w[...] = jnp.zeros_like(kv_w)
@@ -706,60 +1015,66 @@
         for turn, shift in enumerate((2, 1, 3, 0)):
             kv_ring.swap(turn, shift).start()
 
-    def middle(target, turn):
+    def near_middle(turn):
         for half in (0, 1):
-            target.middle(half, turn)
-
-    def finish(target, turn):
+            near_sum.middle(half, turn)
+
+    def near_finish(turn):
         for half in (0, 1):
-            target.finish(half, turn)
+            near_sum.finish(half, turn)
         if turn == 3:
             for half in (0, 1):
-                target.begin(half, 0)
-
-    middle(wide_sum, 3)
-    weight_grad(hid_hbm, dq_ref, in_ring, True)
-    middle(wide_sum, 2)
+                near_sum.begin(half, 0)
+
     neighbour_grad()
-    weight_grad(hid_hbm, dq_ref, in_ring, False)
-    middle(wide_sum, 4)
+    halves[0].wait()
+    stream(2 * SIDE, g_load, g_work)
+    weight_grad(hid_hbm, dq_two, in_ring)
+    wide_sum.middle(1)
+    wide_sum.take(2)
+    wide_sum.begin(0)
     in_ring.begin()
-    weight_grad(cot_hbm, att_ref, out_ring, True)
-    middle(near_sum, 2)
-    weight_grad(cot_hbm, att_ref, out_ring, False)
-    middle(near_sum, 1)
-    middle(wide_sum, 1)
+    halves[1].wait()
+    weight_grad(cot_hbm, att_two, out_ring)
+    near_middle(3)
+    near_middle(4)
+    near_middle(2)
+    out_ring.begin()
     in_ring.middle()
-    out_ring.begin()
-    middle(near_sum, 3)
     kv_grad()
-    middle(near_sum, 4)
-    finish(wide_sum, 4)
+    near_finish(3)
     kv_ring.begin()
-    finish(near_sum, 2)
+    wide_sum.middle(2)
+    near_middle(1)
     out_ring.middle()
-    finish(near_sum, 3)
-    gq_ref[...] = in_ring.finish()
-    finish(wide_sum, 3)
-    finish(near_sum, 4)
-    finish(wide_sum, 2)
-    middle(near_sum, 0)
+    near_finish(4)
+    deliver(0, in_ring, gq_done, gq_ref)
+    near_finish(2)
+    near_middle(0)
+    wide_sum.take(1)
+    wide_sum.take(3)
     kv_ring.middle()
-    finish(wide_sum, 1)
-    middle(wide_sum, 0)
-    finish(near_sum, 1)
-    go_ref[...] = out_ring.finish()
-    finish(near_sum, 0)
+    wide_sum.finish(2)
+    wide_sum.across(4).start()
+    wide_sum.finish(1)
+    near_finish(1)
+    deliver(1, out_ring, go_done, go_ref)
+    wide_sum.middle(0)
+    near_finish(0)
     for i in range(groups * cap):
         mine[i] = dpart[x, y, pl.ds(i * piece_rows, piece_rows), :]
     for slot in range(groups * cap):
         going[slot // cap, slot % cap] = mine[inst_ref[slot]]
     swaps = exchange(going, came_ref, swap_send, swap_recv, load_sem.at[3])
-    finish(wide_sum, 0)
-    gh_ref[...] = gpart[x, y]
+    wide_sum.take(0)
     pair = kv_ring.finish()
     gk_ref[...] = pair[:, :width]
     gv_ref[...] = pair[:, width:]
+    wide_sum.take(4)
+    wide_sum.finish(0)
+    gh_ref[...] = gpart[x, place.member]
+    delivered(0, gq_done, gq_ref)
+    delivered(1, go_done, go_ref)
     for copy in swaps:
         copy.wait()
     for target in (wide_sum, near_sum, out_ring, in_ring, kv_ring):
@@ -799,35 +1114,41 @@
     going = (groups, slots.shape[0] // groups, piece_rows, enc)
     rows = slots.shape[0] * piece_rows
     dma = pltpu.SemaphoreType.DMA
+    blocks = (SIDE, 2, tokens, width)
+    pairs = (SIDE, 2, width, 2 * width)
     out_shape = [
-        f32(SIDE, SIDE, tokens, width),
-        f32(SIDE, SIDE, tokens, width),
+        f32(*blocks),
+        f32(*blocks),
         f32(SIDE, SIDE, rows, enc),
+        f32(*pairs),
         f32(tokens, width),
         f32(tokens, width),
         f32(SIDE, SIDE, rows, width),
         f32(SIDE, SIDE, rows, width),
     ]
     scratch = [
+        pltpu.VMEM((tokens, 2 * width), jnp.float32),
+        pltpu.VMEM((tokens, 2 * width), jnp.float32),
         pltpu.VMEM((tokens, width), jnp.float32),
         pltpu.VMEM((tokens, width), jnp.float32),
         pltpu.VMEM((SIDE, SIDE, rows, width), jnp.float32),
         pltpu.VMEM((SIDE, SIDE, rows, width), jnp.float32),
-        pltpu.VMEM((SIDE, SIDE, tokens, width), jnp.float32),
-        pltpu.VMEM((SIDE, SIDE, tokens, width), jnp.float32),
+        pltpu.VMEM(blocks, jnp.float32),
+        pltpu.VMEM(blocks, jnp.float32),
         pltpu.VMEM((SIDE, SIDE, rows, enc), jnp.float32),
-        pltpu.VMEM(wq.shape, jnp.float32),
-        pltpu.VMEM(wo.shape, jnp.float32),
+        pltpu.VMEM(pairs, jnp.float32),
+        pltpu.VMEM(pairs, jnp.float32),
         pltpu.VMEM((enc, 2 * width), jnp.float32),
         pltpu.VMEM(going, jnp.float32),
         pltpu.VMEM(going, jnp.float32),
     ]
-    scratch += [dma((40,))] * 6 + [dma((groups,))] * 2 + [dma((8,)), dma((30,))]
+    scratch += [dma((17,))] * 4 + [dma((40,))] * 2 + [dma((8,))] * 4 + [dma((2,))] * 2
+    scratch += [dma((groups,))] * 2 + [dma((8,)), dma((12,))]
     return pl.pallas_call(
         gather_kernel,
         out_shape=out_shape,
         in_specs=hbm(2) + vmem(1) + smem(2) + hbm(4),
-        out_specs=hbm(3) + vmem(4),
+        out_specs=hbm(4) + vmem(4),
         scratch_shapes=scratch,
         compiler_params=pltpu.CompilerParams(
             collective_id=0, has_side_effects=True, vmem_limit_bytes=VMEM_LIMIT
@@ -845,22 +1166,26 @@
     piece_rows = rows // slots
     dma = pltpu.SemaphoreType.DMA
     going = (groups, cap, piece_rows, enc)
-    out_rows, enc_rows = wq.shape[0] // groups, enc // groups
+    out_rows, enc_rows = 2 * width, enc // groups
 
     def ring(rows, cols):
         return [
-            pltpu.VMEM((n, r, cols), jnp.float32)
-            for n, r in ((groups, rows), (groups // 2, rows), (2, rows), (2, rows // 2))
+            pltpu.VMEM((*n, r, cols), jnp.float32)
+            for n, r in (((2, SIDE), rows), ((SIDE,), rows), ((2,), rows), ((2,), rows // 2))
         ]
 
     scratch = [
-        pltpu.VMEM((SIDE, SIDE, tokens, width), jnp.float32),
+        pltpu.VMEM((tokens, 2 * width), jnp.float32),
+        pltpu.VMEM((tokens, 2 * width), jnp.float32),
+        pltpu.VMEM((SIDE, 2, tokens, width), jnp.float32),
         pltpu.VMEM((SIDE, SIDE, rows, enc), jnp.float32),
-        pltpu.VMEM((20, tokens // 2, width), jnp.float32),
-        pltpu.VMEM((20, tokens // 4, width), jnp.float32),
+        pltpu.VMEM((6, tokens // 2, width), jnp.float32),
+        pltpu.VMEM((6, tokens // 4, width), jnp.float32),
+        pltpu.VMEM((5, tokens // 2, width), jnp.float32),
         pltpu.VMEM((20, rows // 2, enc), jnp.float32),
         pltpu.VMEM((20, rows // 4, enc), jnp.float32),
-        pltpu.VMEM((2, 2 * width, width), jnp.float32),
+        pltpu.VMEM((2, width, 2 * width), jnp.float32),
+        pltpu.VMEM((2, tokens, width), jnp.float32),
         pltpu.VMEM((2, 2, rows, enc), jnp.float32),
         pltpu.VMEM((2, 2, rows, width), jnp.float32),
         pltpu.VMEM((2, 2, rows, width), jnp.float32),
@@ -870,8 +1195,9 @@
         pltpu.VMEM((slots, piece_rows, enc), jnp.float32),
     ]
     scratch += ring(out_rows, width) + ring(out_rows, width) + ring(enc_rows, 2 * width)
-    scratch += [dma((40,))] * 4 + [dma((8,))] * 6 + [dma((groups,))] * 2
-    scratch += [dma((4,)), dma((2,)), dma((6,))]
+    scratch += [pltpu.VMEM((out_rows, width), jnp.float32)] * 2
+    scratch += [dma((17,))] * 2 + [dma((40,))] * 2 + [dma((8,))] * 6 + [dma((4,))] * 2
+    scratch += [dma((groups,))] * 2 + [dma((4,)), dma((2,)), dma((6,))]
     return pl.pallas_call(
         reduce_kernel,
         out_shape=[
@@ -917,11 +1243,15 @@
     numbers = jnp.arange(inst, dtype=jnp.int32)
     inst_of = jnp.sum(jnp.where(mine[None, :] == numbers[:, None], numbers[None, :], 0), axis=1)
 
-    hid, cot, nei, attended, d_query, d_keys, d_values = gather_call(
-        hidden_states, out_cotangent, enc_table, picks, mine, w_query, w_out, w_key, w_value, groups
+    query_blocks = w_query.reshape(SIDE, SIDE, width, width)
+    out_blocks = w_out.reshape(SIDE, SIDE, width, width)
+    hid, cot, nei, query_pair, attended, d_query, d_keys, d_values = gather_call(
+        hidden_states, out_cotangent, enc_table, picks, mine, query_blocks, out_blocks, w_key,
+        w_value, groups,
     )
     grad_hidden, arrived, grad_query, grad_out, grad_key, grad_value = reduce_call(
-        d_query, attended, inst_of, d_keys, d_values, hid, cot, nei, w_query, w_key, w_value, groups
+        d_query, attended, inst_of, d_keys, d_values, hid, cot, nei, query_pair, w_key, w_value,
+        groups,
     )
     sums = (grad_hidden, grad_query, grad_key, grad_value, grad_out)
     grad_table, *sums = pl.pallas_call(

time: 262 us -> 251 us (0.958)
  Pallas kernels: 257 us -> 247 us
    pallas_call x1, Pallas kernels: 97.2 us -> 90.5 us  [reduce_call(): pl.pallas_call(reduce_kernel, out_shape=[f32(tokens, width), f32(*going),...]
    pallas_call x1, Pallas kernels: 157 us -> 153 us  [gather_call(): pl.pallas_call(gather_kernel, out_shape=out_shape, in_specs=hbm(2) + vmem...]
where the time goes in v4:
time: 251 us; the launch traced here: 250 us
  Pallas kernels  247 us (98%)
    pallas_call x1, Pallas kernels, gather_call(): pl.pallas_call(gather_kernel, out_shape=out_shape, in_specs=hbm(2) + vmem...  153 us
    pallas_call x1, Pallas kernels, reduce_call(): pl.pallas_call(reduce_kernel, out_shape=[f32(tokens, width), f32(*going),...  90.5 us

profile of v4, /device:TPU:1, one launch (start us, length us, event | category | flops | bytes accessed | tf_op | source)
XLA Modules:
  0.0 250.1 jit_solution(2473907721970619125)
XLA Ops:
  0.6 0.9 select_reduce_fusion
  1.5 0.1 copy.17
  1.6 0.1 reshape.120
  1.7 0.3 convert_reduce_fusion
  2.0 0.1 select_reduce_fusion.2
  2.2 0.0 copy-start
  2.2 0.6 select_reduce_fusion.1.inst_ref
  2.8 0.1 copy.18
  2.9 0.6 reshape.121.pick_ref.slot_ref
  3.5 0.0 copy-done
  3.5 153.1 %shard_map.136 = (f32[4,2,512,256]{3,2,1,0:T(8,128)}, f32[4,2,512,256]{3,2,1,0:T(8,128)}, f32[4,4,128,896]{3,2,1,0:T(8,128)}, f32[4,2,256,512]{3,2,1,0:T(8,128)}...) custom-call(f32[512,256]{1,0:T(8,128)} %hid_ref.1, ...), custom_call_target="tpu_custom_call" | custom-call | flops 24000000000 | bytes 60000000 | tf_op jit(solution)/shard_map/pallas_call | solution.py:1147
  156.6 90.5 %shard_map.137 = (f32[512,256]{1,0:T(8,128)}, f32[8,2,8,896]{3,2,1,0:T(8,128)}, f32[512,256]{1,0:T(8,128)}, f32[512,256]{1,0:T(8,128)}, f32[112,256]{1,0:T(8,128)}, /*index=5*/f32[112,256]{1,0:T(8,128)}) custom-call(f32[512,256]{1,0:T(8,128)} %get-tuple-element.26.dq_ref, f32[512,256]{1,0:T(8,128)} %get-tuple-element.27.att_ref, ...), custom_call_target="tpu_custom_call" | custom-call | flops 49999998976 | bytes 60000000 | tf_op jit(solution)/shard_map/pallas_call | solution.py:1201
  247.1 3.0 %shard_map.138 = (f32[16,8,896]{2,1,0:T(8,128)}, f32[512,256]{1,0:T(8,128)}, f32[512,256]{1,0:T(8,128)}, f32[112,256]{1,0:T(8,128)}, f32[112,256]{1,0:T(8,128)}, /*index=5*/f32[512,256]{1,0:T(8,128)}) custom-call(s32[16]{0:T(128)} %reshape.121.pick_ref.slot_ref, f32[8,2,8,896]{3,2,1,0:T(8,128)} %get-tuple-element.34.came_ref, ...), custom_call_target="tpu_custom_call" | custom-call | tf_op jit(solution)/shard_map/pallas_call | solution.py:1257
  (5 shorter events, 0.1 us)
Async XLA Ops:
  2.2 1.3 copy-start

commit v5 on v4

--- a/solution.py
+++ b/solution.py
@@ -315,7 +315,7 @@
                     self.describe(half, turn, kind).wait_send()
 
 
-def attend(q_ref, da_ref, keys_ref, values_ref, att_ref, dq_ref, dk_ref, dv_ref):
+def attend(half, q_ref, da_ref, keys_ref, values_ref, att_ref, dq_ref, dk_ref, dv_ref):
     scale = HEAD_DIM ** (-0.5)
     heads = q_ref.shape[1] // HEAD_DIM
     spans = q_ref.shape[0] // SPAN
@@ -350,7 +350,7 @@
             dv_ref[:, :, pieces, cols] = dot(probs, da, 0, 0).reshape(shape)
         return carry
 
-    lax.fori_loop(0, spans, span, 0)
+    lax.fori_loop(half * spans // 2, (half + 1) * spans // 2, span, 0)
 
 
 class Spread:
@@ -493,108 +493,93 @@
         Spread(place, wq_ref, wq, wq_send, wq_recv),
         Spread(place, wo_ref, wo, wo_send, wo_recv),
     ]
-    for gather in pair:
-        gather.begin(0)
-        gather.across(4).start()
-    for spread in spreads:
-        spread.first().start()
-    for gather in pair:
-        gather.across(0).start()
-        gather.begin(1)
-    for i in range(groups * cap):
-        going[i // cap, i % cap] = table_ref[pick_ref[i]]
-    swaps = exchange(going, came, swap_send, swap_recv, load_sem.at[6])
-    for copy in weights:
-        copy.start()
-    for gather in pair:
+    hid_set, cot_set = pair
+
+    def offer():
+        for i in range(groups * cap):
+            going[i // cap, i % cap] = table_ref[pick_ref[i]]
+        return exchange(going, came, swap_send, swap_recv, load_sem.at[6])
+
+    def accept(swaps):
+        for copy in swaps:
+            copy.wait()
+        for i in range(inst):
+            slot = slot_ref[i]
+            nei[x, y, pl.ds(i * piece_rows, piece_rows), :] = came[
+                slot // cap, lax.rem(slot, cap)
+            ]
+
+    def set_forward(gather):
         gather.forward(0)
         gather.across(1).start()
         gather.across(3).start()
+
+    def set_other(gather):
         gather.across(4, True).wait_recv()
         gather.begin(2)
-    for spread in spreads:
-        spread.spread()
-    for copy in swaps:
-        copy.wait()
-    for i in range(inst):
-        slot = slot_ref[i]
-        nei[x, y, pl.ds(i * piece_rows, piece_rows), :] = came[slot // cap, lax.rem(slot, cap)]
-    for half in (0, 1):
-        near.begin(half, 0)
-    for gather in pair:
+
+    def set_finish(gather):
         gather.finish(0)
         gather.across(2).start()
-    for gather in pair:
-        gather.forward(1)
-    for half in (0, 1):
-        near.begin(half, 1)
-    for gather in pair:
-        gather.forward(2)
-    for spread in spreads:
-        spread.pass_on()
-    for half in (0, 1):
-        near.forward(half, 0)
-        near.begin(half, 2)
-        near.begin(half, 4)
-    for copy in weights:
-        copy.wait()
-    for spread in spreads:
-        spread.finish()
-    keep_weights = pltpu.make_async_copy(wq, wq_out, load_sem.at[7])
-    keep_weights.start()
-    q_two[...] = jnp.zeros_like(q_two)
-    da_two[...] = jnp.zeros_like(da_two)
-
-    def project(half, bx):
+
+    def add_products(gather, half, bx):
         rows = pl.ds(half * (tokens // 2), tokens // 2)
+        total, weight, precision = (
+            (q_two, wq, HIGH) if gather is hid_set else (da_two, wo, MID)
+        )
 
         def column(member, carry):
-            q_two[rows, :] += jnp.dot(
-                hid[bx, member, rows, :], wq[bx, member], precision=HIGH,
-                preferred_element_type=jnp.float32,
-            )
-            da_two[rows, :] += jnp.dot(
-                cot[bx, member, rows, :], wo[bx, member], precision=MID,
+            total[rows, :] += jnp.dot(
+                gather.buf[bx, member, rows, :], weight[bx, member], precision=precision,
                 preferred_element_type=jnp.float32,
             )
             return carry
 
         lax.fori_loop(0, 2, column, 0)
 
-    for turn in (0, 1, 3, 2):
-        for gather in pair:
-            gather.across(turn, True).wait_recv()
-        project(0, wrap(x + turn))
-    for half in (0, 1):
-        near.finish(half, 0)
-        near.begin(half, 3)
-    for gather in pair:
+    def project(gather, half):
+        if half == 0:
+            for turn in (0, 1, 3, 2):
+                gather.across(turn, True).wait_recv()
+                add_products(gather, 0, wrap(x + turn))
+            return
         gather.finish(1)
         gather.finish(2)
 
-    def second_half(bx, carry):
-        project(1, bx)
-        return carry
-
-    lax.fori_loop(0, SIDE, second_half, 0)
-    right = pl.ds(width, width)
-    halves = [
-        partner_copy(place, q_two.at[:, right], q_came, pair_send.at[0], pair_recv.at[0]),
-        partner_copy(place, da_two.at[:, right], da_came, pair_send.at[1], pair_recv.at[1]),
-    ]
-    for copy in halves:
-        copy.start()
-    keeps = [
-        pltpu.make_async_copy(hid, hid_out, store_sem.at[0]),
-        pltpu.make_async_copy(cot, cot_out, store_sem.at[1]),
-    ]
-    for copy in keeps:
-        copy.start()
-
-    def turn_of(step):
-        return step + (step // 2) * (1 - 2 * lax.rem(step, 2)) + 1
-
-    def near_project(half, first):
+        def block(bx, carry):
+            add_products(gather, 1, bx)
+            return carry
+
+        lax.fori_loop(0, SIDE, block, 0)
+
+    def half_copy(gather, half):
+        rows = pl.ds(half * (tokens // 2), tokens // 2)
+        total, came_ref = (q_two, q_came) if gather is hid_set else (da_two, da_came)
+        sem = half + 2 * int(gather is cot_set)
+        return partner_copy(
+            place,
+            total.at[rows, pl.ds(width, width)],
+            came_ref.at[rows],
+            pair_send.at[sem],
+            pair_recv.at[sem],
+        )
+
+    def add_half(gather, half):
+        half_copy(gather, half).wait_recv()
+        rows = pl.ds(half * (tokens // 2), tokens // 2)
+        total, came_ref = (q_two, q_came) if gather is hid_set else (da_two, da_came)
+        came_ref[rows, :] += total[rows, :width]
+
+    def near_keep(half, turn):
+        first = wrap(place.own(half)[0] + turn - 1)
+        rows = pl.ds(half * (nei.shape[2] // 2), nei.shape[2] // 2)
+        at = (first, slice(None), rows) if half == 0 else (slice(None), first, rows)
+        return pltpu.make_async_copy(nei.at[at], nei_out.at[at], store_sem.at[2 + half * 5 + turn])
+
+    def near_project(half, turn):
+        near.finish(half, turn)
+        near_keep(half, turn).start()
+        first = wrap(place.own(half)[0] + turn - 1)
         few = nei.shape[2] // 2
         rows = pl.ds(half * few, few)
         if half == 0:
@@ -612,48 +597,101 @@
             keys_ref[:, first, rows, :] = both[:, :, :width]
             values_ref[:, first, rows, :] = both[:, :, width:]
 
-    def keep(half, turn, first):
-        rows = pl.ds(half * (nei.shape[2] // 2), nei.shape[2] // 2)
-        at = (first, slice(None), rows) if half == 0 else (slice(None), first, rows)
-        return pltpu.make_async_copy(nei.at[at], nei_out.at[at], store_sem.at[2 + half * 5 + turn])
-
-    def pass_on(turn):
+    def near_begin(turn):
         for half in (0, 1):
-            near.forward(half, turn)
-
-    pass_on(turn_of(0))
-
-    def main(step, carry):
-        @pl.when(step < SIDE - 1)
-        def _():
-            pass_on(turn_of(step + 1))
-
-        turn = turn_of(step)
-        for half in (0, 1):
-            near.finish(half, turn)
-            first = wrap(place.own(half)[0] + turn - 1)
-            keep(half, turn, first).start()
-            near_project(half, first)
-        return carry
-
-    lax.fori_loop(0, SIDE, main, 0)
-    for copy in halves:
+            near.begin(half, turn)
+
+    attended = (q_came, da_came, keys_ref, values_ref, att_ref, dq_ref, dk_ref, dv_ref)
+
+    hid_set.begin(1)
+    hid_set.across(4).start()
+    cot_set.begin(1)
+    for spread in spreads:
+        spread.first().start()
+    cot_set.begin(0)
+    swaps = offer()
+    cot_set.across(0).start()
+    cot_set.across(4).start()
+    for copy in weights:
+        copy.start()
+    q_two[...] = jnp.zeros_like(q_two)
+    da_two[...] = jnp.zeros_like(da_two)
+    for spread in spreads:
+        spread.spread()
+    set_other(hid_set)
+    accept(swaps)
+    near_begin(1)
+    set_forward(cot_set)
+    near_begin(0)
+    for spread in spreads:
+        spread.pass_on()
+    set_other(cot_set)
+    near.forward(0, 1)
+    hid_set.begin(0)
+    set_finish(cot_set)
+    cot_set.forward(1)
+    cot_set.forward(2)
+    for half in (0, 1):
+        near.forward(half, 0)
+    near_begin(2)
+    near_begin(4)
+    for copy in weights:
         copy.wait()
-    q_came[...] += q_two[:, :width]
-    da_came[...] += da_two[:, :width]
-    attend(q_came, da_came, keys_ref, values_ref, att_ref, dq_ref, dk_ref, dv_ref)
+    for spread in spreads:
+        spread.finish()
+    keep_weights = pltpu.make_async_copy(wq, wq_out, load_sem.at[7])
+    keep_weights.start()
+    near.forward(0, 2)
+    hid_set.across(0).start()
+    project(cot_set, 1)
+    half_copy(cot_set, 1).start()
+    set_forward(hid_set)
+    near_project(0, 2)
+    hid_set.forward(2)
+    project(cot_set, 0)
+    near_project(0, 1)
+    set_finish(hid_set)
+    hid_set.forward(1)
+    near.forward(1, 2)
+    for half in (0, 1):
+        near.finish(half, 0)
+    near_begin(3)
+    half_copy(cot_set, 0).start()
+    keep_cot = pltpu.make_async_copy(cot, cot_out, store_sem.at[1])
+    keep_cot.start()
+    project(hid_set, 1)
+    near.forward(1, 1)
+    add_half(cot_set, 1)
+    half_copy(hid_set, 1).start()
+    near_project(1, 2)
+    near.forward(1, 4)
+    near.forward(0, 4)
+    near.forward(1, 3)
+    project(hid_set, 0)
+    half_copy(hid_set, 0).start()
+    keep_hid = pltpu.make_async_copy(hid, hid_out, store_sem.at[0])
+    keep_hid.start()
+    near_project(1, 1)
+    near_project(1, 4)
+    near_project(1, 3)
+    near.forward(0, 3)
+    add_half(hid_set, 1)
+    attend(1, *attended)
+    add_half(cot_set, 0)
+    near_project(0, 4)
+    near_project(0, 3)
+    add_half(hid_set, 0)
+    attend(0, *attended)
     for target in (*pair, near, *spreads):
         target.drain()
-    keep_weights.wait()
-    for copy in keeps:
+    for gather in pair:
+        for half in (0, 1):
+            half_copy(gather, half).wait_send()
+    for copy in (keep_weights, keep_hid, keep_cot):
         copy.wait()
-
-    def stored(turn, carry):
-        for half in (0, 1):
-            keep(half, turn, wrap(place.own(half)[0] + turn - 1)).wait()
-        return carry
-
-    lax.fori_loop(1, SIDE + 1, stored, 0)
+    for half in (0, 1):
+        for turn in range(1, SIDE + 1):
+            near_keep(half, turn).wait()
 
 
 class Reduce:
@@ -1142,7 +1180,7 @@
         pltpu.VMEM(going, jnp.float32),
         pltpu.VMEM(going, jnp.float32),
     ]
-    scratch += [dma((17,))] * 4 + [dma((40,))] * 2 + [dma((8,))] * 4 + [dma((2,))] * 2
+    scratch += [dma((17,))] * 4 + [dma((40,))] * 2 + [dma((8,))] * 4 + [dma((4,))] * 2
     scratch += [dma((groups,))] * 2 + [dma((8,)), dma((12,))]
     return pl.pallas_call(
         gather_kernel,

time: 251 us -> 218 us (0.87)
  Pallas kernels: 247 us -> 213 us
    pallas_call x1, Pallas kernels: 153 us -> 121 us  [gather_call(): pl.pallas_call(gather_kernel, out_shape=out_shape, in_specs=hbm(2) + vmem...]
where the time goes in v5:
time: 218 us; the launch traced here: 217 us
  Pallas kernels  213 us (98%)
    pallas_call x1, Pallas kernels, gather_call(): pl.pallas_call(gather_kernel, out_shape=out_shape, in_specs=hbm(2) + vmem...  121 us
    pallas_call x1, Pallas kernels, reduce_call(): pl.pallas_call(reduce_kernel, out_shape=[f32(tokens, width), f32(*going),...  89.3 us

profile of v5, /device:TPU:1, one launch (start us, length us, event | category | flops | bytes accessed | tf_op | source)
XLA Modules:
  0.0 216.9 jit_solution(15490922514960516236)
XLA Ops:
  0.6 0.9 select_reduce_fusion
  1.5 0.1 copy.17
  1.6 0.1 reshape.120
  1.7 0.3 convert_reduce_fusion
  2.0 0.1 select_reduce_fusion.2
  2.2 0.0 copy-start
  2.2 0.6 select_reduce_fusion.1.inst_ref
  2.8 0.1 copy.18
  2.9 0.6 reshape.121.pick_ref.slot_ref
  3.5 0.0 copy-done
  3.5 121.1 %shard_map.136 = (f32[4,2,512,256]{3,2,1,0:T(8,128)}, f32[4,2,512,256]{3,2,1,0:T(8,128)}, f32[4,4,128,896]{3,2,1,0:T(8,128)}, f32[4,2,256,512]{3,2,1,0:T(8,128)}...) custom-call(f32[512,256]{1,0:T(8,128)} %hid_ref.1, ...), custom_call_target="tpu_custom_call" | custom-call | flops 24000000000 | bytes 60000000 | tf_op jit(solution)/shard_map/pallas_call | solution.py:1185
  124.7 89.3 %shard_map.137 = (f32[512,256]{1,0:T(8,128)}, f32[8,2,8,896]{3,2,1,0:T(8,128)}, f32[512,256]{1,0:T(8,128)}, f32[512,256]{1,0:T(8,128)}, f32[112,256]{1,0:T(8,128)}, /*index=5*/f32[112,256]{1,0:T(8,128)}) custom-call(f32[512,256]{1,0:T(8,128)} %get-tuple-element.26.dq_ref, f32[512,256]{1,0:T(8,128)} %get-tuple-element.27.att_ref, ...), custom_call_target="tpu_custom_call" | custom-call | flops 49999998976 | bytes 60000000 | tf_op jit(solution)/shard_map/pallas_call | solution.py:1239
  213.9 3.0 %shard_map.138 = (f32[16,8,896]{2,1,0:T(8,128)}, f32[512,256]{1,0:T(8,128)}, f32[512,256]{1,0:T(8,128)}, f32[112,256]{1,0:T(8,128)}, f32[112,256]{1,0:T(8,128)}, /*index=5*/f32[512,256]{1,0:T(8,128)}) custom-call(s32[16]{0:T(128)} %reshape.121.pick_ref.slot_ref, f32[8,2,8,896]{3,2,1,0:T(8,128)} %get-tuple-element.34.came_ref, ...), custom_call_target="tpu_custom_call" | custom-call | tf_op jit(solution)/shard_map/pallas_call | solution.py:1295
  (5 shorter events, 0.1 us)
Async XLA Ops:
  2.2 1.3 copy-start

commit v6 on v5

--- a/solution.py
+++ b/solution.py
@@ -417,8 +417,8 @@
     hid_ref,
     cot_ref,
     table_ref,
-    pick_ref,
-    slot_ref,
+    nbr_ref,
+    map_ref,
     wq_ref,
     wo_ref,
     wk_ref,
@@ -427,6 +427,9 @@
     cot_out,
     nei_out,
     wq_out,
+    pick_ref,
+    slot_ref,
+    inst_ref,
     att_ref,
     dq_ref,
     dk_ref,
@@ -495,10 +498,45 @@
     ]
     hid_set, cot_set = pair
 
+    group = lax.axis_index("wide")
+    stored = table_ref.shape[0]
+
+    def stored_at(g, i):
+        return map_ref[nbr_ref[g * (inst // NEIGH) + i // NEIGH, i % NEIGH]]
+
     def offer():
-        for i in range(groups * cap):
-            going[i // cap, i % cap] = table_ref[pick_ref[i]]
+        def one(g, carry):
+            count = jnp.int32(0)
+            chosen = [jnp.int32(0)] * cap
+            for i in range(inst):
+                at = stored_at(g, i) - group * stored
+                hit = (at >= 0) & (at < stored)
+                chosen = [
+                    jnp.where(hit & (count == r), at, old) for r, old in enumerate(chosen)
+                ]
+                count = count + hit.astype(jnp.int32)
+            for r in range(cap):
+                pick_ref[g * cap + r] = chosen[r]
+                going[g, r] = table_ref[chosen[r]]
+            return carry
+
+        lax.fori_loop(0, groups, one, 0)
         return exchange(going, came, swap_send, swap_recv, load_sem.at[6])
+
+    def places():
+        owners = [lax.div(stored_at(group, i), stored) for i in range(inst)]
+        slots = [
+            owner * cap + sum((owners[j] == owner).astype(jnp.int32) for j in range(i))
+            for i, owner in enumerate(owners)
+        ]
+        for i in range(inst):
+            slot_ref[i] = slots[i]
+
+        def one(slot, carry):
+            inst_ref[slot] = sum(jnp.where(slot_ref[i] == slot, i, 0) for i in range(inst))
+            return carry
+
+        lax.fori_loop(0, inst, one, 0)
 
     def accept(swaps):
         for copy in swaps:
@@ -610,6 +648,7 @@
         spread.first().start()
     cot_set.begin(0)
     swaps = offer()
+    places()
     cot_set.across(0).start()
     cot_set.across(4).start()
     for copy in weights:
@@ -1012,7 +1051,7 @@
 
     def near_load(sources):
         def load(i, slot):
-            at = (i // 2, pl.ds(2 * lax.rem(i, 2), 2))
+            at = (wrap(x + shift_of(i // 2)), pl.ds(2 * lax.rem(i, 2), 2))
             return [
                 pltpu.make_async_copy(source.at[at], buf.at[slot], near_sem.at[2 * which + slot])
                 for which, (source, buf) in enumerate(sources)
@@ -1021,20 +1060,27 @@
         return load
 
     def d_work(i, slot):
-        bx, by = i // 2, 2 * lax.rem(i, 2)
+        shift = shift_of(i // 2)
+        bx, by = wrap(x + shift), 2 * lax.rem(i, 2)
         dk = dk_tile[slot].reshape(2 * rows, width)
         dv = dv_tile[slot].reshape(2 * rows, width)
         dpart[bx, pl.ds(by, 2)] = (dot(dk, wk[...], 1, 1) + dot(dv, wv[...], 1, 1)).reshape(
             2, rows, enc
         )
 
+        @pl.when(i == 1)
+        def _():
+            for turn in TURNS:
+                near_sum.begin(1, turn)
+
+        @pl.when(lax.rem(i, 2) == 1)
+        def _():
+            near_sum.begin(0, shift + 1)
+
     def neighbour_grad():
         for copy in weights:
             copy.wait()
         stream(2 * SIDE, near_load(((dk_hbm, dk_tile), (dv_hbm, dv_tile))), d_work)
-        for turn in TURNS:
-            for half in (0, 1):
-                near_sum.begin(half, turn)
 
     def kv_work(i, slot):
         dk = dk_tile[slot].reshape(2 * rows, width)
@@ -1146,11 +1192,13 @@
     return jax.ShapeDtypeStruct(shape, jnp.float32)
 
 
-def gather_call(hidden, cotangent, table, picks, slots, wq, wo, wk, wv, groups):
+def gather_call(hidden, cotangent, table, nbr_ids, owner_map, wq, wo, wk, wv, groups):
     tokens, width = hidden.shape
     _, piece_rows, enc = table.shape
-    going = (groups, slots.shape[0] // groups, piece_rows, enc)
-    rows = slots.shape[0] * piece_rows
+    inst = nbr_ids.size // groups
+    going = (groups, inst // groups, piece_rows, enc)
+    rows = inst * piece_rows
+    places = jax.ShapeDtypeStruct((inst,), jnp.int32)
     dma = pltpu.SemaphoreType.DMA
     blocks = (SIDE, 2, tokens, width)
     pairs = (SIDE, 2, width, 2 * width)
@@ -1159,6 +1207,9 @@
         f32(*blocks),
         f32(SIDE, SIDE, rows, enc),
         f32(*pairs),
+        places,
+        places,
+        places,
         f32(tokens, width),
         f32(tokens, width),
         f32(SIDE, SIDE, rows, width),
@@ -1186,13 +1237,13 @@
         gather_kernel,
         out_shape=out_shape,
         in_specs=hbm(2) + vmem(1) + smem(2) + hbm(4),
-        out_specs=hbm(4) + vmem(4),
+        out_specs=hbm(4) + smem(3) + vmem(4),
         scratch_shapes=scratch,
         compiler_params=pltpu.CompilerParams(
             collective_id=0, has_side_effects=True, vmem_limit_bytes=VMEM_LIMIT
         ),
         cost_estimate=pl.CostEstimate(flops=24_000_000_000, bytes_accessed=60_000_000, transcendentals=0),
-    )(hidden, cotangent, table, picks, slots, wq, wo, wk, wv)
+    )(hidden, cotangent, table, nbr_ids, owner_map, wq, wo, wk, wv)
 
 
 def reduce_call(dq, att, inst_of, dk, dv, hid, cot, nei, wq, wk, wv, groups):
@@ -1260,32 +1311,12 @@
     hidden_states, out_cotangent, enc_table, nbr_ids, owner_map, w_query, w_key, w_value, w_out
 ):
     groups = lax.axis_size("wide")
-    group = lax.axis_index("wide")
-    stored = enc_table.shape[0]
-    table_size = owner_map.shape[0]
-    tokens, width = hidden_states.shape
-    inst = NEIGH * (tokens // SPAN)
-    capacity = inst // groups
-    match = nbr_ids[:, :, None] == jnp.arange(table_size, dtype=jnp.int32)[None, None, :]
-    slots = jnp.sum(jnp.where(match, owner_map[None, None, :], 0), axis=-1)
-    slots = slots.reshape(groups, inst)
-    owners = slots // stored
-    local_slot = slots - owners * stored
-    earlier = jnp.arange(inst)[None, :] < jnp.arange(inst)[:, None]
-    same = owners[:, :, None] == owners[:, None, :]
-    rank = jnp.sum((same & earlier[None, :, :]).astype(jnp.int32), axis=-1)
-    slot_range = jnp.arange(capacity, dtype=jnp.int32)
-    pick = (owners[:, None, :] == group) & (rank[:, None, :] == slot_range[None, :, None])
-    picks = jnp.sum(jnp.where(pick, local_slot[:, None, :], 0), axis=-1).reshape(-1)
-    mine = lax.dynamic_index_in_dim(owners * capacity + rank, group, 0, keepdims=False)
-    numbers = jnp.arange(inst, dtype=jnp.int32)
-    inst_of = jnp.sum(jnp.where(mine[None, :] == numbers[:, None], numbers[None, :], 0), axis=1)
-
+    width = hidden_states.shape[1]
     query_blocks = w_query.reshape(SIDE, SIDE, width, width)
     out_blocks = w_out.reshape(SIDE, SIDE, width, width)
-    hid, cot, nei, query_pair, attended, d_query, d_keys, d_values = gather_call(
-        hidden_states, out_cotangent, enc_table, picks, mine, query_blocks, out_blocks, w_key,
-        w_value, groups,
+    hid, cot, nei, query_pair, picks, _, inst_of, attended, d_query, d_keys, d_values = gather_call(
+        hidden_states, out_cotangent, enc_table, nbr_ids, owner_map, query_blocks, out_blocks,
+        w_key, w_value, groups,
     )
     grad_hidden, arrived, grad_query, grad_out, grad_key, grad_value = reduce_call(
         d_query, attended, inst_of, d_keys, d_values, hid, cot, nei, query_pair, w_key, w_value,

time: 218 us -> 217 us (level)
  no operation moved by 1% of the time
where the time goes in v6:
time: 217 us; the launch traced here: 216 us
  Pallas kernels  214 us (99%)
    pallas_call x1, Pallas kernels, gather_call(): pl.pallas_call(gather_kernel, out_shape=out_shape, in_specs=hbm(2) + vmem...  121 us
    pallas_call x1, Pallas kernels, reduce_call(): pl.pallas_call(reduce_kernel, out_shape=[f32(tokens, width), f32(*going),...  89.3 us

profile of v6, /device:TPU:1, one launch (start us, length us, event | category | flops | bytes accessed | tf_op | source)
XLA Modules:
  0.0 215.7 jit_solution(15301601325276097624)
XLA Ops:
  0.6 1.4 copy.15.nbr_ref
  2.0 121.3 %shard_map.136 = (f32[4,2,512,256]{3,2,1,0:T(8,128)}, f32[4,2,512,256]{3,2,1,0:T(8,128)}, f32[4,4,128,896]{3,2,1,0:T(8,128)}, f32[4,2,256,512]{3,2,1,0:T(8,128)}...) custom-call(f32[512,256]{1,0:T(8,128)} %hid_ref.1, ...), custom_call_target="tpu_custom_call" | custom-call | flops 24000000000 | bytes 60000000 | tf_op jit(solution)/shard_map/pallas_call | solution.py:1236
  123.3 89.3 %shard_map.137 = (f32[512,256]{1,0:T(8,128)}, f32[8,2,8,896]{3,2,1,0:T(8,128)}, f32[512,256]{1,0:T(8,128)}, f32[512,256]{1,0:T(8,128)}, f32[112,256]{1,0:T(8,128)}, /*index=5*/f32[112,256]{1,0:T(8,128)}) custom-call(f32[512,256]{1,0:T(8,128)} %get-tuple-element.29.dq_ref, f32[512,256]{1,0:T(8,128)} %get-tuple-element.30.att_ref, ...), custom_call_target="tpu_custom_call" | custom-call | flops 49999998976 | bytes 60000000 | tf_op jit(solution)/shard_map/pallas_call | solution.py:1290
  212.7 3.0 %shard_map.138 = (f32[16,8,896]{2,1,0:T(8,128)}, f32[512,256]{1,0:T(8,128)}, f32[512,256]{1,0:T(8,128)}, f32[112,256]{1,0:T(8,128)}, f32[112,256]{1,0:T(8,128)}, /*index=5*/f32[512,256]{1,0:T(8,128)}) custom-call(s32[16]{0:T(128)} %get-tuple-element.28.slot_ref, f32[8,2,8,896]{3,2,1,0:T(8,128)} %get-tuple-element.38.came_ref, ...), custom_call_target="tpu_custom_call" | custom-call | tf_op jit(solution)/shard_map/pallas_call | solution.py:1326

commit v7 on v6

--- a/solution.py
+++ b/solution.py
@@ -281,9 +281,15 @@
             return wrap(first + shift), second
         return wrap(first + turn - 1), wrap(second + shift)
 
+    def along_y(self, half, turn):
+        return half == 1 if isinstance(turn, int) and turn == 0 else half == 0
+
     def describe(self, half, turn, kind):
         shift = (0, 0, -1, 1)[kind]
         ahead = (1, -1, 1, -1)[kind]
+        if kind >= 2 and self.along_y(half, turn):
+            ahead = 2 * self.place.member - 1
+            shift = -ahead
         return self.copy(
             half, turn, kind, self.at(half, turn, shift), self.place.line(half, turn, ahead)
         )
@@ -300,6 +306,12 @@
         self.describe(half, turn, 1).start()
 
     def forward(self, half, turn):
+        if self.along_y(half, turn):
+            for kind in (0, 1):
+                self.arrival(half, turn, kind).wait_recv()
+            for kind in (2, 3):
+                self.describe(half, turn, kind).start()
+            return
         for kind in (0, 1):
             self.arrival(half, turn, kind).wait_recv()
             self.describe(half, turn, kind + 2).start()
@@ -502,7 +514,7 @@
     stored = table_ref.shape[0]
 
     def stored_at(g, i):
-        return map_ref[nbr_ref[g * (inst // NEIGH) + i // NEIGH, i % NEIGH]]
+        return map_ref[nbr_ref[i % NEIGH, g * (inst // NEIGH) + i // NEIGH]]
 
     def offer():
         def one(g, carry):
@@ -641,83 +653,83 @@
 
     attended = (q_came, da_came, keys_ref, values_ref, att_ref, dq_ref, dk_ref, dv_ref)
 
-    hid_set.begin(1)
-    hid_set.across(4).start()
-    cot_set.begin(1)
+    cot_set.begin(0)
     for spread in spreads:
         spread.first().start()
-    cot_set.begin(0)
+    cot_set.across(0).start()
+    cot_set.begin(1)
+    cot_set.across(4).start()
     swaps = offer()
     places()
-    cot_set.across(0).start()
-    cot_set.across(4).start()
     for copy in weights:
         copy.start()
     q_two[...] = jnp.zeros_like(q_two)
     da_two[...] = jnp.zeros_like(da_two)
+    accept(swaps)
+    set_forward(cot_set)
+    set_other(cot_set)
+    near_begin(0)
+    hid_set.across(4).start()
     for spread in spreads:
         spread.spread()
-    set_other(hid_set)
-    accept(swaps)
     near_begin(1)
-    set_forward(cot_set)
-    near_begin(0)
-    for spread in spreads:
-        spread.pass_on()
-    set_other(cot_set)
-    near.forward(0, 1)
     hid_set.begin(0)
-    set_finish(cot_set)
-    cot_set.forward(1)
-    cot_set.forward(2)
     for half in (0, 1):
         near.forward(half, 0)
     near_begin(2)
     near_begin(4)
+    hid_set.begin(1)
+    set_other(hid_set)
+    set_forward(hid_set)
+    for spread in spreads:
+        spread.pass_on()
+    cot_set.forward(2)
+    cot_set.forward(1)
+    near.forward(0, 1)
+    near.forward(0, 4)
+    near.forward(1, 1)
     for copy in weights:
         copy.wait()
+    near_project(0, 4)
+    set_finish(cot_set)
+    near.forward(0, 2)
+    near_project(0, 1)
+    hid_set.forward(1)
     for spread in spreads:
         spread.finish()
     keep_weights = pltpu.make_async_copy(wq, wq_out, load_sem.at[7])
     keep_weights.start()
-    near.forward(0, 2)
-    hid_set.across(0).start()
-    project(cot_set, 1)
-    half_copy(cot_set, 1).start()
-    set_forward(hid_set)
-    near_project(0, 2)
     hid_set.forward(2)
-    project(cot_set, 0)
-    near_project(0, 1)
-    set_finish(hid_set)
-    hid_set.forward(1)
-    near.forward(1, 2)
     for half in (0, 1):
         near.finish(half, 0)
     near_begin(3)
+    near.forward(1, 4)
+    project(cot_set, 0)
+    hid_set.across(0).start()
     half_copy(cot_set, 0).start()
+    project(cot_set, 1)
+    half_copy(cot_set, 1).start()
     keep_cot = pltpu.make_async_copy(cot, cot_out, store_sem.at[1])
     keep_cot.start()
+    near_project(1, 1)
+    set_finish(hid_set)
+    near_project(0, 2)
     project(hid_set, 1)
-    near.forward(1, 1)
-    add_half(cot_set, 1)
     half_copy(hid_set, 1).start()
-    near_project(1, 2)
-    near.forward(1, 4)
-    near.forward(0, 4)
+    near.forward(1, 2)
+    project(hid_set, 0)
+    near.forward(0, 3)
     near.forward(1, 3)
-    project(hid_set, 0)
     half_copy(hid_set, 0).start()
     keep_hid = pltpu.make_async_copy(hid, hid_out, store_sem.at[0])
     keep_hid.start()
-    near_project(1, 1)
     near_project(1, 4)
+    near_project(1, 2)
+    add_half(cot_set, 1)
     near_project(1, 3)
-    near.forward(0, 3)
+    add_half(cot_set, 0)
     add_half(hid_set, 1)
     attend(1, *attended)
-    add_half(cot_set, 0)
-    near_project(0, 4)
     near_project(0, 3)
     add_half(hid_set, 0)
     attend(0, *attended)
@@ -1166,14 +1178,20 @@
 
 
 def result_kernel(slot_ref, came_ref, *refs):
-    sources, table_ref, results = refs[:5], refs[5], refs[6:]
-    for source, result in zip(sources, results):
-        result[...] = source[...]
+    sources, table_ref, results, sems = refs[:5], refs[5], refs[6:11], refs[11]
+    copies = [
+        pltpu.make_async_copy(source, result, sems.at[i])
+        for i, (source, result) in enumerate(zip(sources, results))
+    ]
+    for copy in copies:
+        copy.start()
     table_ref[...] = jnp.zeros_like(table_ref)
     cap = came_ref.shape[1]
     for i in range(came_ref.shape[0] * cap):
         slot = slot_ref[i]
         table_ref[slot] += came_ref[i // cap, i % cap]
+    for copy in copies:
+        copy.wait()
 
 
 def vmem(n):
@@ -1315,7 +1333,7 @@
     query_blocks = w_query.reshape(SIDE, SIDE, width, width)
     out_blocks = w_out.reshape(SIDE, SIDE, width, width)
     hid, cot, nei, query_pair, picks, _, inst_of, attended, d_query, d_keys, d_values = gather_call(
-        hidden_states, out_cotangent, enc_table, nbr_ids, owner_map, query_blocks, out_blocks,
+        hidden_states, out_cotangent, enc_table, nbr_ids.T, owner_map, query_blocks, out_blocks,
         w_key, w_value, groups,
     )
     grad_hidden, arrived, grad_query, grad_out, grad_key, grad_value = reduce_call(
@@ -1326,8 +1344,9 @@
     grad_table, *sums = pl.pallas_call(
         result_kernel,
         out_shape=[f32(*enc_table.shape)] + [f32(*t.shape) for t in sums],
-        in_specs=smem(1) + vmem(6),
-        out_specs=vmem(6),
+        in_specs=smem(1) + vmem(1) + hbm(5),
+        out_specs=vmem(1) + hbm(5),
+        scratch_shapes=[pltpu.SemaphoreType.DMA((5,))],
     )(picks, arrived, *sums)
     return (*sums, grad_table)
 

time: 217 us -> 269 us (1.24)
  Pallas kernels: 214 us -> 267 us
    pallas_call x1, Pallas kernels: 3.01 us -> 57.5 us  [body(): pl.pallas_call(result_kernel, out_shape=[f32(*enc_table.shape)] + [f32(*t...]
where the time goes in v7:
time: 269 us; the launch traced here: 268 us
  Pallas kernels  267 us (99%)
    pallas_call x1, Pallas kernels, gather_call(): pl.pallas_call(gather_kernel, out_shape=out_shape, in_specs=hbm(2) + vmem...  120 us
    pallas_call x1, Pallas kernels, reduce_call(): pl.pallas_call(reduce_kernel, out_shape=[f32(tokens, width), f32(*going),...  89.7 us
    pallas_call x1, Pallas kernels, body(): pl.pallas_call(result_kernel, out_shape=[f32(*enc_table.shape)] + [f32(*t...  57.5 us

profile of v7, /device:TPU:1, one launch (start us, length us, event | category | flops | bytes accessed | tf_op | source)
XLA Modules:
  0.0 268.0 jit_solution(6118507616927252105)
XLA Ops:
  0.6 119.9 %shard_map.136 = (f32[4,2,512,256]{3,2,1,0:T(8,128)}, f32[4,2,512,256]{3,2,1,0:T(8,128)}, f32[4,4,128,896]{3,2,1,0:T(8,128)}, f32[4,2,256,512]{3,2,1,0:T(8,128)}...) custom-call(f32[512,256]{1,0:T(8,128)} %hid_ref.1, ...), custom_call_target="tpu_custom_call" | custom-call | flops 24000000000 | bytes 60000000 | tf_op jit(solution)/shard_map/pallas_call | solution.py:1254
  120.5 89.7 %shard_map.137 = (f32[512,256]{1,0:T(8,128)}, f32[8,2,8,896]{3,2,1,0:T(8,128)}, f32[512,256]{1,0:T(8,128)}, f32[512,256]{1,0:T(8,128)}, f32[112,256]{1,0:T(8,128)}, /*index=5*/f32[112,256]{1,0:T(8,128)}) custom-call(f32[512,256]{1,0:T(8,128)} %get-tuple-element.29.dq_ref, f32[512,256]{1,0:T(8,128)} %get-tuple-element.30.att_ref, ...), custom_call_target="tpu_custom_call" | custom-call | flops 49999998976 | bytes 60000000 | tf_op jit(solution)/shard_map/pallas_call | solution.py:1308
  210.2 57.5 %shard_map.138 = (f32[16,8,896]{2,1,0:T(8,128)}, f32[512,256]{1,0:T(8,128)}, f32[512,256]{1,0:T(8,128)}, f32[112,256]{1,0:T(8,128)}, f32[112,256]{1,0:T(8,128)}, /*index=5*/f32[512,256]{1,0:T(8,128)}) custom-call(s32[16]{0:T(128)} %get-tuple-element.28.slot_ref, f32[8,2,8,896]{3,2,1,0:T(8,128)} %get-tuple-element.38.came_ref, ...), custom_call_target="tpu_custom_call" | custom-call | tf_op jit(solution)/shard_map/pallas_call | solution.py:1344

commit v8 on v7

--- a/solution.py
+++ b/solution.py
@@ -1178,20 +1178,14 @@
 
 
 def result_kernel(slot_ref, came_ref, *refs):
-    sources, table_ref, results, sems = refs[:5], refs[5], refs[6:11], refs[11]
-    copies = [
-        pltpu.make_async_copy(source, result, sems.at[i])
-        for i, (source, result) in enumerate(zip(sources, results))
-    ]
-    for copy in copies:
-        copy.start()
+    sources, table_ref, results = refs[:5], refs[5], refs[6:]
+    for source, result in zip(sources, results):
+        result[...] = source[...]
     table_ref[...] = jnp.zeros_like(table_ref)
     cap = came_ref.shape[1]
     for i in range(came_ref.shape[0] * cap):
         slot = slot_ref[i]
         table_ref[slot] += came_ref[i // cap, i % cap]
-    for copy in copies:
-        copy.wait()
 
 
 def vmem(n):
@@ -1344,9 +1338,8 @@
     grad_table, *sums = pl.pallas_call(
         result_kernel,
         out_shape=[f32(*enc_table.shape)] + [f32(*t.shape) for t in sums],
-        in_specs=smem(1) + vmem(1) + hbm(5),
-        out_specs=vmem(1) + hbm(5),
-        scratch_shapes=[pltpu.SemaphoreType.DMA((5,))],
+        in_specs=smem(1) + vmem(6),
+        out_specs=vmem(6),
     )(picks, arrived, *sums)
     return (*sums, grad_table)
 

time: 269 us -> 214 us (0.80)
  Pallas kernels: 267 us -> 213 us
    pallas_call x1, Pallas kernels: 57.5 us -> 3.01 us  [body(): pl.pallas_call(result_kernel, out_shape=[f32(*enc_table.shape)] + [f32(*t...]
where the time goes in v8:
time: 214 us; the launch traced here: 213 us
  Pallas kernels  213 us (100%)
    pallas_call x1, Pallas kernels, gather_call(): pl.pallas_call(gather_kernel, out_shape=out_shape, in_specs=hbm(2) + vmem...  120 us
    pallas_call x1, Pallas kernels, reduce_call(): pl.pallas_call(reduce_kernel, out_shape=[f32(tokens, width), f32(*going),...  89.7 us

profile of v8, /device:TPU:1, one launch (start us, length us, event | category | flops | bytes accessed | tf_op | source)
XLA Modules:
  0.0 213.2 jit_solution(1589722265730426293)
XLA Ops:
  0.6 119.9 %shard_map.136 = (f32[4,2,512,256]{3,2,1,0:T(8,128)}, f32[4,2,512,256]{3,2,1,0:T(8,128)}, f32[4,4,128,896]{3,2,1,0:T(8,128)}, f32[4,2,256,512]{3,2,1,0:T(8,128)}...) custom-call(f32[512,256]{1,0:T(8,128)} %hid_ref.1, ...), custom_call_target="tpu_custom_call" | custom-call | flops 24000000000 | bytes 60000000 | tf_op jit(solution)/shard_map/pallas_call | solution.py:1248
  120.5 89.7 %shard_map.137 = (f32[512,256]{1,0:T(8,128)}, f32[8,2,8,896]{3,2,1,0:T(8,128)}, f32[512,256]{1,0:T(8,128)}, f32[512,256]{1,0:T(8,128)}, f32[112,256]{1,0:T(8,128)}, /*index=5*/f32[112,256]{1,0:T(8,128)}) custom-call(f32[512,256]{1,0:T(8,128)} %get-tuple-element.29.dq_ref, f32[512,256]{1,0:T(8,128)} %get-tuple-element.30.att_ref, ...), custom_call_target="tpu_custom_call" | custom-call | flops 49999998976 | bytes 60000000 | tf_op jit(solution)/shard_map/pallas_call | solution.py:1302
  210.2 3.0 %shard_map.138 = (f32[16,8,896]{2,1,0:T(8,128)}, f32[512,256]{1,0:T(8,128)}, f32[512,256]{1,0:T(8,128)}, f32[112,256]{1,0:T(8,128)}, f32[112,256]{1,0:T(8,128)}, /*index=5*/f32[512,256]{1,0:T(8,128)}) custom-call(s32[16]{0:T(128)} %get-tuple-element.28.slot_ref, f32[8,2,8,896]{3,2,1,0:T(8,128)} %get-tuple-element.38.came_ref, ...), custom_call_target="tpu_custom_call" | custom-call | tf_op jit(solution)/shard_map/pallas_call | solution.py:1338

commit v9 on v8

--- a/solution.py
+++ b/solution.py
@@ -636,16 +636,19 @@
             blocks = nei[first, :, rows, :]
         else:
             blocks = nei[:, first, rows, :]
-        both = jnp.dot(
-            blocks.reshape(SIDE * few, nei.shape[3]), wkv[...], precision=HIGH,
-            preferred_element_type=jnp.float32,
-        ).reshape(SIDE, few, 2 * width)
+        flat = blocks.reshape(SIDE * few, nei.shape[3])
+        keys = jnp.dot(
+            flat, wkv[:, :width], precision=HIGH, preferred_element_type=jnp.float32
+        ).reshape(SIDE, few, width)
+        values = jnp.dot(
+            flat, wkv[:, width:], precision=MID, preferred_element_type=jnp.float32
+        ).reshape(SIDE, few, width)
         if half == 0:
-            keys_ref[first, :, rows, :] = both[:, :, :width]
-            values_ref[first, :, rows, :] = both[:, :, width:]
+            keys_ref[first, :, rows, :] = keys
+            values_ref[first, :, rows, :] = values
         else:
-            keys_ref[:, first, rows, :] = both[:, :, :width]
-            values_ref[:, first, rows, :] = both[:, :, width:]
+            keys_ref[:, first, rows, :] = keys
+            values_ref[:, first, rows, :] = values
 
     def near_begin(turn):
         for half in (0, 1):

time: 214 us -> 213 us (level)
  no operation moved by 1% of the time
where the time goes in v9:
time: 213 us
  Pallas kernels  212 us (100%)
    pallas_call x1, Pallas kernels, gather_call(): pl.pallas_call(gather_kernel, out_shape=out_shape, in_specs=hbm(2) + vmem...  120 us
    pallas_call x1, Pallas kernels, reduce_call(): pl.pallas_call(reduce_kernel, out_shape=[f32(tokens, width), f32(*going),...  89.1 us

profile of v9, /device:TPU:1, one launch (start us, length us, event | category | flops | bytes accessed | tf_op | source)
XLA Modules:
  0.0 212.7 jit_solution(8203240790829072116)
XLA Ops:
  0.6 119.9 %shard_map.136 = (f32[4,2,512,256]{3,2,1,0:T(8,128)}, f32[4,2,512,256]{3,2,1,0:T(8,128)}, f32[4,4,128,896]{3,2,1,0:T(8,128)}, f32[4,2,256,512]{3,2,1,0:T(8,128)}...) custom-call(f32[512,256]{1,0:T(8,128)} %hid_ref.1, ...), custom_call_target="tpu_custom_call" | custom-call | flops 24000000000 | bytes 60000000 | tf_op jit(solution)/shard_map/pallas_call | solution.py:1251
  120.5 89.1 %shard_map.137 = (f32[512,256]{1,0:T(8,128)}, f32[8,2,8,896]{3,2,1,0:T(8,128)}, f32[512,256]{1,0:T(8,128)}, f32[512,256]{1,0:T(8,128)}, f32[112,256]{1,0:T(8,128)}, /*index=5*/f32[112,256]{1,0:T(8,128)}) custom-call(f32[512,256]{1,0:T(8,128)} %get-tuple-element.29.dq_ref, f32[512,256]{1,0:T(8,128)} %get-tuple-element.30.att_ref, ...), custom_call_target="tpu_custom_call" | custom-call | flops 49999998976 | bytes 60000000 | tf_op jit(solution)/shard_map/pallas_call | solution.py:1305
  209.7 3.0 %shard_map.138 = (f32[16,8,896]{2,1,0:T(8,128)}, f32[512,256]{1,0:T(8,128)}, f32[512,256]{1,0:T(8,128)}, f32[112,256]{1,0:T(8,128)}, f32[112,256]{1,0:T(8,128)}, /*index=5*/f32[512,256]{1,0:T(8,128)}) custom-call(s32[16]{0:T(128)} %get-tuple-element.28.slot_ref, f32[8,2,8,896]{3,2,1,0:T(8,128)} %get-tuple-element.38.came_ref, ...), custom_call_target="tpu_custom_call" | custom-call | tf_op jit(solution)/shard_map/pallas_call | solution.py:1341
